TPU v7x, 32 devices: a whole 2x2x4 slice. The times are simulated.
32 devices in a mesh: groups: 2 (over y), ctx: 4 (over z), heads: 4 (over x, core).
Axes of the slice: x: 2, y: 2, z: 4, core: 2. Of those that a mesh axis runs over, the one named last changes fastest.
Arguments:
- queries: bfloat16 [4096, 28, 128], P(('groups', 'ctx'), 'heads'), parts along dimension 0, may hold values from -9 to 9
- key_states: bfloat16 [4096, 4, 128], P(('groups', 'ctx'), 'heads'), parts along dimension 0, may hold values from -9 to 9
- value_states: bfloat16 [4096, 4, 128], P(('groups', 'ctx'), 'heads'), parts along dimension 0, may hold values from -6 to 6
- out_weight: bfloat16 [3584, 3584], P('heads'), may hold values from -1.5 to 1.5
- slash_offsets: int32 [8, 8], P(('groups', 'heads')), parts along dimension 0, may hold values from 0 to 23, as said below
- vertical_blocks: int32 [8, 4], P(('groups', 'heads')), parts along dimension 0, may hold values from 0 to 7
Outputs:
- output: bfloat16 [4096, 3584], P(('groups', 'ctx'), 'heads'), parts along dimension 0
There are 2 independent parts, one for each index of `groups`. A program takes and returns all parts, laid end to end along the dimension named above; an argument that names none is the same for every part. Nothing has to cross between parts.
Inputs may be any that keep to these rules, and one draw needn't show every extreme that they name: `slash_offsets`: each key-value head's 8 offsets are distinct and include 0 and 3 * 512 // 64 - 1.
All inputs are finite; a program needn't handle non-finite values.
Results may differ from a plain program's by a relative error of at most 0.011.
Values may be sent and summed in bfloat16 or wider, within the bound.
No kernel may reach another device: no remote copies, remote signals or barrier semaphores. Data moves between devices by JAX's collectives and lax.ppermute only.
A program may use at most 192 MiB of HBM per device.

v0:
```python
import jax
import jax.numpy as jnp
from jax import lax
from jax.sharding import PartitionSpec as P

BLOCK = 64
BAND = 3


def shifted(value, axis, steps):
    count = lax.axis_size(axis)
    first, last = (max(0, -steps), min(count, count - steps))
    return lax.ppermute(value, axis, [(source, source + steps) for source in range(first, last)])


def on_device(queries, key_states, value_states, out_weight, slash_offsets, vertical_blocks):
    rows_here, per_group, head_size = queries.shape
    blocks = rows_here // BLOCK
    score_scale = head_size ** (-0.5)
    shard_index = lax.axis_index("ctx")
    ctx_count = lax.axis_size("ctx")
    offsets = slash_offsets[0]
    key_rows = key_states[:, 0, :]
    value_rows = value_states[:, 0, :]
    within = jnp.arange(rows_here, dtype=jnp.int32)
    query_block = shard_index * blocks + within // BLOCK

    def in_band(distance):
        return jnp.any(distance[..., None] == offsets, axis=-1)

    def attend(carry_state, key_part, value_part, allowed):
        running_max, running_sum, weighted = carry_state
        scores = (
            jnp.einsum("qgd,kd->qgk", queries, key_part, preferred_element_type=jnp.float32)
            * score_scale
        )
        scores = jnp.where(allowed[:, None, :], scores, -1e30)
        new_max = jnp.maximum(running_max, jnp.max(scores, axis=-1))
        rescale = jnp.exp(running_max - new_max)
        weights = jnp.where(allowed[:, None, :], jnp.exp(scores - new_max[..., None]), 0.0)
        running_sum = running_sum * rescale + jnp.sum(weights, axis=-1)
        weighted = weighted * rescale[..., None] + jnp.einsum(
            "qgk,kd->qgd",
            weights.astype(jnp.bfloat16),
            value_part,
            preferred_element_type=jnp.float32,
        )
        return (new_max, running_sum, weighted)

    def band_allowed(stride):
        block_row = shard_index * blocks + jnp.arange(blocks, dtype=jnp.int32)
        block_col = (shard_index - stride) * blocks + jnp.arange(blocks, dtype=jnp.int32)
        coarse = in_band(block_row[:, None] - block_col[None, :]) & (block_col >= 0)[None, :]
        token_mask = jnp.repeat(jnp.repeat(coarse, BLOCK, axis=0), BLOCK, axis=1)
        if stride == 0:
            token_mask = token_mask & (within[None, :] <= within[:, None])
        return token_mask

    initial = (
        jnp.full((rows_here, per_group), -1e30, jnp.float32),
        jnp.zeros((rows_here, per_group), jnp.float32),
        jnp.zeros((rows_here, per_group, head_size), jnp.float32),
    )
    carry_state = attend(initial, key_rows, value_rows, band_allowed(0))
    moving = (key_rows, value_rows)
    for stride in range(1, BAND + 1):
        moving = shifted((moving[0], moving[1]), "ctx", 1)
        carry_state = attend(carry_state, moving[0], moving[1], band_allowed(stride))
    own_block = lax.dynamic_index_in_dim(vertical_blocks[0], shard_index, 0, keepdims=False)
    tile_keys = lax.dynamic_slice_in_dim(key_rows, own_block * BLOCK, BLOCK, 0)
    tile_values = lax.dynamic_slice_in_dim(value_rows, own_block * BLOCK, BLOCK, 0)
    global_blocks = jnp.arange(ctx_count, dtype=jnp.int32) * blocks + vertical_blocks[0]
    tile_key_part = lax.all_gather(tile_keys, "ctx", axis=0, tiled=True)
    tile_value_part = lax.all_gather(tile_values, "ctx", axis=0, tiled=True)
    tile_rows = tile_key_part.shape[0]
    owners = jnp.arange(tile_rows, dtype=jnp.int32) // BLOCK
    matches = owners[:, None] == jnp.arange(ctx_count, dtype=jnp.int32)[None, :]
    column_block = jnp.sum(jnp.where(matches, global_blocks[None, :], 0), axis=1)
    distance = query_block[:, None] - column_block[None, :]
    allowed = (distance > 0) & jnp.logical_not(in_band(distance))
    carry_state = attend(carry_state, tile_key_part, tile_value_part, allowed)
    running_max, running_sum, weighted = carry_state
    attended = (
        (weighted / running_sum[..., None])
        .astype(jnp.bfloat16)
        .reshape(rows_here, per_group * head_size)
    )
    partial_value = jnp.dot(attended, out_weight, preferred_element_type=jnp.float32)
    return lax.psum_scatter(
        partial_value.astype(jnp.bfloat16), "heads", scatter_dimension=1, tiled=True
    )


def solution(mesh):
    placed = (
        P(("groups", "ctx"), "heads", None),
        P(("groups", "ctx"), "heads", None),
        P(("groups", "ctx"), "heads", None),
        P("heads", None),
        P(("groups", "heads"), None),
        P(("groups", "heads"), None),
    )
    return jax.shard_map(
        on_device,
        mesh=mesh,
        in_specs=placed,
        out_specs=P(("groups", "ctx"), "heads"),
        check_vma=False,
    )
```

profile of v0, /device:TPU:28, one launch (start us, length us, event | category | flops | bytes accessed | tf_op | source)
XLA Modules:
  0.0 153.8 jit_solution(10760463946559047945)
XLA Ops:
  6.5 1.4 collective-permute-start
  9.0 1.3 collective-permute-start.1
  10.4 1.3 compare_reduce_fusion.1
  17.5 15.5 %all-gather = bf16[256,1,128]{2,0,1:T(8,128)(2,1)S(1)} all-gather(bf16[64,1,128]{2,0,1:T(8,128)(2,1)S(1)} %constant_dynamic-slice_fusion), channel_id=2, replica_groups=mesh['groups'=2,'ctx'=4,'heads'=4] {'ctx'}, dimensions={0}, use_global_device_ids=true | all-gather | bytes 81920 | tf_op jit(solution)/shard_map/all_gather | solution.py:73
  33.3 2.2 %compare_reduce_fusion = pred[512,256]{1,0:T(8,128)(4,1)S(1)} fusion(s32[512,256]{1,0:T(8,128)S(1)} %broadcast_subtract_fusion, s32[8]{0:T(128)} %bitcast.100), kind=kLoop, calls=%fused_computation.21 | loop fusion | flops 1966080 | bytes 655392 | tf_op jit(solution)/shard_map/reduce_or | solution.py:29
  35.9 2.2 %fusion = (f32[512,7]{0,1:T(8,128)S(1)}, f32[512,7,512]{0,2,1:T(8,128)S(1)}) fusion(pred[512,512]{0,1:T(8,128)(4,1)S(1)} %fusion.36, bf16[512,7,128]{2,0,1:T(8,128)(2,1)S(1)} %copy-done, bf16[512,1,128]{2,0,1:T(8,128)(2,1)} %param.7), kind=kOutput, calls=%fused_computation.8 | convolution fusion | flops 475263488 | bytes 8665088 | tf_op jit(solution)/shard_map/qgd,kd->qgk/dot_general | solution.py:34
  38.9 13.1 %all-gather.1 = bf16[256,1,128]{2,0,1:T(8,128)(2,1)S(1)} all-gather(bf16[64,1,128]{2,0,1:T(8,128)(2,1)S(1)} %constant_dynamic-slice_fusion.2), channel_id=3, replica_groups=mesh['groups'=2,'ctx'=4,'heads'=4] {'ctx'}, dimensions={0}, use_global_device_ids=true | all-gather | bytes 81920 | tf_op jit(solution)/shard_map/all_gather | solution.py:74
  53.5 1.4 fusion.1
  56.1 2.8 %collective-permute-done.2 = bf16[512,128]{1,0:T(8,128)(2,1)S(1)} collective-permute-done((bf16[512,128]{1,0:T(8,128)(2,1)S(1)}, bf16[512,128]{1,0:T(8,128)(2,1)S(1)}, u32[]{:S(2)}, u32[]{:S(2)}) %collective-permute-start.2) | collective-permute-done | bytes 131104 | tf_op jit(solution)/shard_map/ppermute | solution.py:13
  60.3 4.3 %fusion.2 = (f32[512,7]{0,1:T(8,128)S(1)}, f32[512,7,512]{0,2,1:T(8,128)}) fusion(pred[512,512]{0,1:T(8,128)(4,1)S(1)} %bitcast.93, bf16[512,7,128]{2,0,1:T(8,128)(2,1)S(1)} %copy-done, bf16[512,128]{1,0:T(8,128)(2,1)S(1)} %collective-permute-done.2), kind=kOutput, calls=%fused_computation.10 | convolution fusion | flops 475263488 | bytes 8665088 | tf_op jit(solution)/shard_map/qgd,kd->qgk/dot_general | solution.py:34
  64.6 1.5 collective-permute-start.5
  66.2 1.4 fusion.3
  67.6 1.8 %fusion.4 = f32[512,7]{0,1:T(8,128)S(1)} fusion(f32[512,7,512]{0,2,1:T(8,128)S(1)} %get-tuple-element.33, f32[512,7]{0,1:T(8,128)S(1)} %get-tuple-element.19, pred[512,512]{0,1:T(8,128)(4,1)S(1)} %fusion.36), kind=kLoop, calls=%fused_computation.13 | loop fusion | flops 9171456 | bytes 7630848 | tf_op jit(solution)/shard_map/reduce_sum | solution.py:41
  69.4 3.7 %fusion.18 = f32[512,7,128]{0,2,1:T(8,128)} fusion(f32[512,7,512]{0,2,1:T(8,128)S(1)} %get-tuple-element.33, f32[512,7]{0,1:T(8,128)S(1)} %get-tuple-element.19, pred[512,512]{0,1:T(8,128)(4,1)S(1)} %fusion.36, bf16[512,1,128]{2,0,1:T(8,128)(2,1)S(1)} %copy-done.1), kind=kOutput, calls=%fused_computation.27 | convolution fusion | flops 478937088 | bytes 9582592 | tf_op jit(solution)/shard_map/qgk,kd->qgd/dot_general | solution.py:42
  75.2 1.8 %fusion.6 = f32[512,7]{0,1:T(8,128)S(1)} fusion(f32[512,7,512]{0,2,1:T(8,128)S(1)} %get-tuple-element.31, f32[512,7]{0,1:T(8,128)S(1)} %get-tuple-element.17, pred[512,512]{0,1:T(8,128)(4,1)S(1)} %bitcast.88), kind=kLoop, calls=%fused_computation.15 | loop fusion | flops 9171456 | bytes 7630848 | tf_op jit(solution)/shard_map/reduce_sum | solution.py:41
  77.4 1.8 %fusion.8 = f32[512,7]{0,1:T(8,128)S(1)} fusion(f32[512,7,512]{0,2,1:T(8,128)S(1)} %bitcast.85, f32[512,7]{0,1:T(8,128)S(1)} %get-tuple-element.16, pred[512,512]{0,1:T(8,128)(4,1)S(1)} %bitcast.94), kind=kLoop, calls=%fused_computation.17 | loop fusion | flops 9171456 | bytes 7630848 | tf_op jit(solution)/shard_map/reduce_sum | solution.py:41
  79.1 2.0 %fusion.10 = f32[512,7]{0,1:T(8,128)S(1)} fusion(f32[512,7,512]{0,2,1:T(8,128)S(1)} %get-tuple-element.27, f32[512,7]{0,1:T(8,128)S(1)} %get-tuple-element.15, pred[512,512]{0,1:T(8,128)(4,1)S(1)} %bitcast.91), kind=kLoop, calls=%fused_computation.19 | loop fusion | flops 9171456 | bytes 7630848 | tf_op jit(solution)/shard_map/reduce_sum | solution.py:41
  81.1 2.3 %fusion.16 = f32[512,7,128]{0,2,1:T(8,128)S(1)} fusion(f32[512,7,512]{0,2,1:T(8,128)S(1)} %get-tuple-element.31, f32[512,7]{0,1:T(8,128)S(1)} %get-tuple-element.17, pred[512,512]{0,1:T(8,128)(4,1)S(1)} %bitcast.89, bf16[512,128]{0,1:T(8,128)(2,1)S(1)} %collective-permute-done.1), kind=kOutput, calls=%fused_computation.26 | convolution fusion | flops 478937088 | bytes 9582592 | tf_op jit(solution)/shard_map/qgk,kd->qgd/dot_general | solution.py:42
  83.4 2.3 %fusion.14 = f32[512,7,128]{0,2,1:T(8,128)S(1)} fusion(f32[512,7,512]{0,2,1:T(8,128)S(1)} %bitcast.85, f32[512,7]{0,1:T(8,128)S(1)} %get-tuple-element.16, pred[512,512]{0,1:T(8,128)(4,1)S(1)} %bitcast.95, bf16[512,128]{0,1:T(8,128)(2,1)S(1)} %collective-permute-done.3), kind=kOutput, calls=%fused_computation.25 | convolution fusion | flops 478937088 | bytes 9582592 | tf_op jit(solution)/shard_map/qgk,kd->qgd/dot_general | solution.py:42
  85.8 2.7 %divide_convert_fusion = bf16[512,7,128]{0,2,1:T(8,128)(2,1)S(1)} fusion(f32[512,7,128]{0,2,1:T(8,128)S(1)} %fusion.27, f32[512,7,128]{0,2,1:T(8,128)S(1)} %fusion.14, f32[512,7,128]{0,2,1:T(8,128)S(1)} %fusion.16, f32[512,7,128]{0,2,1:T(8,128)S(1)} %copy-done.2, f32[512,7,512]{0,2,1:T(8,128)S(1)} %get-tuple-element.27, ...), kind=kOutput, calls=%fused_computation.36 | convolution fusion | flops 483983360 | bytes 16091136 | tf_op jit(solution)/shard_map/qgk,kd->qgd/dot_general | solution.py:42
  88.5 5.6 %convolution_convert_fusion = bf16[512,3584]{1,0:T(8,128)(2,1)} fusion(bf16[512,896]{0,1:T(8,128)(2,1)S(1)} %bitcast.103, bf16[896,3584]{1,0:T(8,128)(2,1)S(1)} %bitcast.102), kind=kOutput, calls=%fused_computation.12 | convolution fusion | flops 3290169344 | bytes 11010048 | tf_op jit(solution)/shard_map/dot_general | solution.py:88
  94.1 5.9 %copy.40 = bf16[512,3584]{0,1:T(8,128)(2,1)} copy(bf16[512,3584]{1,0:T(8,128)(2,1)} %convolution_convert_fusion) | data formatting | bytes 7340032
  100.0 44.7 %reduce-scatter.4.cloned.1.call-done = bf16[896,512]{1,0:T(8,128)(2,1)} async-done(((bf16[3584,512]{1,0:T(8,128)(2,1)}), bf16[896,512]{1,0:T(8,128)(2,1)}) %reduce-scatter.4.cloned.1.call-update) | async-done | bytes 917520
  144.7 2.2 %copy.41 = bf16[512,896]{1,0:T(8,128)(2,1)} copy(bf16[512,896]{0,1:T(8,128)(2,1)} %bitcast.96) | data formatting | bytes 1835008
  (67 shorter events, 13.0 us)
Async XLA Ops:
  6.5 29.3 %copy-start = (bf16[512,7,128]{2,0,1:T(8,128)(2,1)S(1)}, bf16[512,7,128]{2,0,1:T(8,128)(2,1)}, u32[]{:S(2)}) copy-start(bf16[512,7,128]{2,0,1:T(8,128)(2,1)} %param.6) | copy-start | bytes 2752516
  6.5 138.2 %reduce-scatter.4.cloned.1.call-start = ((), (), s32[]{:S(2)}) async-start(), calls=%async_computation.1 | async-start | bytes 4587520
  6.5 45.6 %collective-permute-start = (bf16[512,128]{1,0:T(8,128)(2,1)}, bf16[512,128]{1,0:T(8,128)(2,1)S(1)}, u32[]{:S(2)}, u32[]{:S(2)}) collective-permute-start(bf16[512,128]{1,0:T(8,128)(2,1)} %bitcast.97), channel_id=1, source_target_pairs={{0,4},{4,8},{8,12},{1,5},{5,9},{9,13},{2,6},{6,10},{10,14},{3,7},{... | collective-permute-start | bytes 393224 | tf_op jit(solution)/shard_map/ppermute | solution.py:13
  9.0 45.8 %collective-permute-start.1 = (bf16[512,128]{0,1:T(8,128)(2,1)S(1)}, bf16[512,128]{0,1:T(8,128)(2,1)S(1)}, u32[]{:S(2)}, u32[]{:S(2)}) collective-permute-start(bf16[512,128]{0,1:T(8,128)(2,1)S(1)} %bitcast.98), channel_id=1, source_target_pairs={{0,4},{4,8},{8,12},{1,5},{5,9},{9,13},{2,6},{6,10},{10,14},{3,7},{... | collective-permute-start | bytes 393224 | tf_op jit(solution)/shard_map/ppermute | solution.py:13
  33.3 5.7 %copy-start.1 = (bf16[512,1,128]{2,0,1:T(8,128)(2,1)S(1)}, bf16[512,1,128]{2,0,1:T(8,128)(2,1)}, u32[]{:S(2)}) copy-start(bf16[512,1,128]{2,0,1:T(8,128)(2,1)} %param.8) | copy-start | bytes 393220
  52.1 6.9 %collective-permute-start.2 = (bf16[512,128]{1,0:T(8,128)(2,1)S(1)}, bf16[512,128]{1,0:T(8,128)(2,1)S(1)}, u32[]{:S(2)}, u32[]{:S(2)}) collective-permute-start(bf16[512,128]{1,0:T(8,128)(2,1)S(1)} %collective-permute-done), channel_id=1, source_target_pairs={{0,4},{4,8},{8,12},{1,5},{5,9},{9,13},{2,6},{6,10},{10,14},{3,7},{... | collective-permute-start | bytes 393224 | tf_op jit(solution)/shard_map/ppermute | solution.py:13
  54.8 9.8 %collective-permute-start.3 = (bf16[512,128]{0,1:T(8,128)(2,1)S(1)}, bf16[512,128]{0,1:T(8,128)(2,1)S(1)}, u32[]{:S(2)}, u32[]{:S(2)}) collective-permute-start(bf16[512,128]{0,1:T(8,128)(2,1)S(1)} %collective-permute-done.1), channel_id=1, source_target_pairs={{0,4},{4,8},{8,12},{1,5},{5,9},{9,13},{2,6},{6,10},{10,14},{3,7},{... | collective-permute-start | bytes 393224 | tf_op jit(solution)/shard_map/ppermute | solution.py:13
  59.0 7.2 %collective-permute-start.4 = (bf16[512,128]{1,0:T(8,128)(2,1)S(1)}, bf16[512,128]{1,0:T(8,128)(2,1)S(1)}, u32[]{:S(2)}, u32[]{:S(2)}) collective-permute-start(bf16[512,128]{1,0:T(8,128)(2,1)S(1)} %collective-permute-done.2), channel_id=1, source_target_pairs={{0,4},{4,8},{8,12},{1,5},{5,9},{9,13},{2,6},{6,10},{10,14},{3,7},{... | collective-permute-start | bytes 393224 | tf_op jit(solution)/shard_map/ppermute | solution.py:13
  64.6 21.1 %collective-permute-start.5 = (bf16[512,128]{0,1:T(8,128)(2,1)S(1)}, bf16[512,128]{0,1:T(8,128)(2,1)S(1)}, u32[]{:S(2)}, u32[]{:S(2)}) collective-permute-start(bf16[512,128]{0,1:T(8,128)(2,1)S(1)} %collective-permute-done.3), channel_id=1, source_target_pairs={{0,4},{4,8},{8,12},{1,5},{5,9},{9,13},{2,6},{6,10},{10,14},{3,7},{... | collective-permute-start | bytes 393224 | tf_op jit(solution)/shard_map/ppermute | solution.py:13
  74.0 3.0 %slice-start = ((s8[7340032]{0:T(1024)(128)(4,1)}), s8[4194304]{0:T(1024)(128)(4,1)S(1)}, s32[]{:S(2)}) async-start(s8[7340032]{0:T(1024)(128)(4,1)} %bitcast.84), calls=%async_computation.2 | async-start | bytes 8388608
  75.2 2.1 %slice-start.1 = ((s8[7340032]{0:T(1024)(128)(4,1)}), s8[3145728]{0:T(1024)(128)(4,1)S(1)}, s32[]{:S(2)}) async-start(s8[7340032]{0:T(1024)(128)(4,1)} %bitcast.84), calls=%async_computation.3 | async-start | bytes 6291456
  83.4 2.4 %copy-start.2 = (f32[512,7,128]{0,2,1:T(8,128)S(1)}, f32[512,7,128]{0,2,1:T(8,128)}, u32[]{:S(2)}) copy-start(f32[512,7,128]{0,2,1:T(8,128)} %fusion.18) | copy-start | bytes 5505028
  83.4 5.1 %slice-start.2 = ((s8[6422528]{0:T(1024)(128)(4,1)}), s8[4194304]{0:T(1024)(128)(4,1)S(1)}, s32[]{:S(2)}) async-start(s8[6422528]{0:T(1024)(128)(4,1)} %bitcast.101), calls=%async_computation.4 | async-start | bytes 8388608
  85.8 2.7 %slice-start.3 = ((s8[6422528]{0:T(1024)(128)(4,1)}), s8[2228224]{0:T(1024)(128)(4,1)S(1)}, s32[]{:S(2)}) async-start(s8[6422528]{0:T(1024)(128)(4,1)} %bitcast.101), calls=%async_computation.5 | async-start | bytes 4456448
Sparse Core Ops, SparseCore 0:
  100.1 44.5 reduce-scatter.3
where the time goes:
time: 156 us; the launch traced here: 154 us
  waiting for transfers between devices  47.6 us (31%)
  blocking collectives  28.6 us (18%)
  matrix products  27.8 us (18%)
  between operations  15.8 us (10%)
  other arithmetic  14.2 us (9%)
  local copies, waits for them, and re-layouts  11.7 us (8%)
  starting transfers between devices  8.02 us (5%)
    unnamed x2, waiting for transfers between devices  44.7 us
    all_gather x1, blocking collectives, on_device(): tile_key_part = lax.all_gather(tile_keys, 'ctx', axis=0, tiled=True)  15.5 us
    all_gather x1, blocking collectives, on_device(): tile_value_part = lax.all_gather(tile_values, 'ctx', axis=0, tiled=True)  13.1 us
    dot_general x5, matrix products, attend(): jnp.einsum('qgk,kd->qgd', weights.astype(jnp.bfloat16), value_part, prefe...  12.2 us
    dot_general x5, matrix products, attend(): jnp.einsum('qgd,kd->qgk', queries, key_part, preferred_element_type=jnp.f...  10 us
    unnamed x17, local copies, waits for them, and re-layouts  9.52 us
    reduce_sum x5, other arithmetic, attend(): running_sum = running_sum * rescale + jnp.sum(weights, axis=-1)  8.15 us
    ppermute x6, starting transfers between devices, shifted(): lax.ppermute(value, axis, [(source, source + steps) for source in range(f...  8.02 us
  transfers between devices with their start and end apart: 7, of which 2 were waited for; matrix products, arithmetic and copies ran while one was open for 24% of the time, Pallas kernels for 0%

commit v1 on v0

v1 whole, which is shorter than its diff:
```python
import functools
import math

import jax
import jax.numpy as jnp
from jax import lax
from jax.experimental import pallas as pl
from jax.experimental.pallas import tpu as pltpu
from jax.sharding import PartitionSpec as P

BLOCK = 64
BAND = 3
NEG = -1e30


def shifted(value, axis, steps):
    count = lax.axis_size(axis)
    return lax.ppermute(value, axis, [(source, source + steps) for source in range(count - steps)])


def swapped(value, flip):
    count = lax.axis_size("heads")
    return lax.ppermute(value, "heads", [(source, source ^ flip) for source in range(count)])


def attend_rows(cfg, info, q_ref, win, tiles, gathered, row, first_block, store):
    slash, n_vert, blocks, heads_here, head = cfg
    shard = info[slash + n_vert]
    local = first_block + row
    own = shard * blocks + local
    base = (shard - BAND) * blocks
    count = slash + n_vert
    allowed = []
    for slot in range(slash):
        if slot == 0:
            source = BAND * blocks + local
            allowed.append(None)
        else:
            offset = info[slot]
            offset = jnp.where(offset == 0, info[0], offset)
            source = BAND * blocks + local - offset
            allowed.append(own - offset >= 0)
        gathered[slot * BLOCK : (slot + 1) * BLOCK, :] = win[pl.ds(pl.multiple_of(source * BLOCK, BLOCK), BLOCK), :]
    for shard_from in range(n_vert):
        slot = slash + shard_from
        column = shard_from * blocks + info[slot]
        gap = own - column
        fine = gap > 0
        for other in range(slash):
            fine = jnp.logical_and(fine, gap != info[other])
        allowed.append(fine)
        if tiles is None:
            source = jnp.where(shard - shard_from == BAND, (BAND + 1) * blocks, column - base)
            source = jnp.where(fine, source, BAND * blocks + local)
            piece = win[pl.ds(pl.multiple_of(source * BLOCK, BLOCK), BLOCK), :]
        else:
            piece = tiles[shard_from * BLOCK : (shard_from + 1) * BLOCK, :]
        gathered[slot * BLOCK : (slot + 1) * BLOCK, :] = piece
    lane = lax.broadcasted_iota(jnp.int32, (1, count * BLOCK), 1) // BLOCK
    bias = jnp.zeros((1, count * BLOCK), jnp.float32)
    for slot in range(1, count):
        bias = jnp.where(lane == slot, jnp.where(allowed[slot], 0.0, NEG), bias)
    rows = heads_here * BLOCK
    keys = gathered[:, :head]
    values = gathered[:, head:]
    q = q_ref[row]
    scores = lax.dot_general(q, keys, (((1,), (1,)), ((), ())), preferred_element_type=jnp.float32)
    scores = scores + bias
    col = lax.broadcasted_iota(jnp.int32, (BLOCK, 2 * BLOCK), 1)
    line = lax.broadcasted_iota(jnp.int32, (BLOCK, 2 * BLOCK), 0)
    causal = jnp.where(jnp.logical_or(col <= line, col >= BLOCK), 0.0, NEG)
    causal = jnp.concatenate([causal] * heads_here, axis=0)
    scores = jnp.concatenate([scores[:, : 2 * BLOCK] + causal, scores[:, 2 * BLOCK :]], axis=1)
    factor = math.log2(math.e) * head ** (-0.5)
    row_max = jnp.max(scores, axis=1, keepdims=True)
    weights = jnp.exp2((scores - row_max) * factor).astype(jnp.bfloat16)
    extended = jnp.concatenate([values, jnp.ones_like(values)], axis=1)
    mixed = lax.dot_general(weights, extended, (((1,), (0,)), ((), ())), preferred_element_type=jnp.float32)
    result = (mixed[:, :head] / mixed[:, head:]).astype(jnp.bfloat16)
    for h in range(heads_here):
        store(row, h, result[h * BLOCK : (h + 1) * BLOCK])


def attention_body(cfg, first_block, loads, n_kv, with_tiles, *refs):
    slash, n_vert, blocks, heads_here, head = cfg
    info = refs[0]
    q_ref = refs[1]
    weight = refs[2]
    pieces = refs[3 : 3 + n_kv]
    tiles = refs[3 + n_kv]
    attended, keep, send = refs[4 + n_kv : 7 + n_kv]
    win, gathered, w_keep, w_send, sems, w_sems = refs[7 + n_kv :]
    width = keep.shape[1]
    keep_col = info[slash + n_vert + 1]
    send_col = info[slash + n_vert + 2]
    w_copies = [
        pltpu.make_async_copy(weight.at[:, pl.ds(pl.multiple_of(keep_col * width, 128), width)], w_keep, w_sems.at[0]),
        pltpu.make_async_copy(weight.at[:, pl.ds(pl.multiple_of(send_col * width, 128), width)], w_send, w_sems.at[1]),
    ]
    copies = []
    for index, (piece, at) in enumerate(zip(pieces, loads)):
        copies.append(pltpu.make_async_copy(piece, win.at[at : at + piece.shape[0]], sems.at[index]))
    if not with_tiles:
        at = (BAND + 1) * blocks * BLOCK
        copies.append(pltpu.make_async_copy(tiles, win.at[at : at + BLOCK], sems.at[n_kv]))
    for copy in copies:
        copy.start()
    for copy in w_copies:
        copy.start()
    for copy in copies:
        copy.wait()

    def store(row, h, value):
        attended[row * BLOCK : (row + 1) * BLOCK, h * head : (h + 1) * head] = value

    for row in range(q_ref.shape[0]):
        attend_rows(cfg, info, q_ref, win, tiles if with_tiles else None, gathered, row, first_block, store)
    for copy in w_copies:
        copy.wait()
    send[...] = jnp.dot(attended[...], w_send[...], preferred_element_type=jnp.float32).astype(send.dtype)
    keep[...] = jnp.dot(attended[...], w_keep[...], preferred_element_type=jnp.float32).astype(keep.dtype)


def attention(cfg, info, q, weight, pieces, loads, tiles, first_block, with_tiles):
    slash, n_vert, blocks, heads_here, head = cfg
    rows = q.shape[0] * BLOCK
    width = weight.shape[1] // 4
    count = slash + n_vert
    n_kv = len(pieces)
    vmem = pl.BlockSpec(memory_space=pltpu.VMEM)
    anywhere = pl.BlockSpec(memory_space=pl.ANY)
    out = jax.ShapeDtypeStruct((rows, width), jnp.bfloat16)
    return pl.pallas_call(
        functools.partial(attention_body, cfg, first_block, loads, n_kv, with_tiles),
        out_shape=[jax.ShapeDtypeStruct((rows, heads_here * head), jnp.bfloat16), out, out],
        in_specs=[pl.BlockSpec(memory_space=pltpu.SMEM), vmem, anywhere]
        + [anywhere] * n_kv
        + [vmem if with_tiles else anywhere],
        out_specs=[vmem] * 3,
        scratch_shapes=[
            pltpu.VMEM((((BAND + 1) * blocks + 1) * BLOCK, 2 * head), jnp.bfloat16),
            pltpu.VMEM((count * BLOCK, 2 * head), jnp.bfloat16),
            pltpu.VMEM((weight.shape[0], width), jnp.bfloat16),
            pltpu.VMEM((weight.shape[0], width), jnp.bfloat16),
            pltpu.SemaphoreType.DMA((n_kv + 1,)),
            pltpu.SemaphoreType.DMA((2,)),
        ],
        compiler_params=pltpu.CompilerParams(vmem_limit_bytes=40 * 1024 * 1024),
        cost_estimate=pl.CostEstimate(flops=2 * rows * heads_here * head * (2 * width + 4 * count * BLOCK), bytes_accessed=6_000_000, transcendentals=rows * heads_here * count * BLOCK),
        name="attend",
    )(info, q, weight, *pieces, tiles)


def project_body(info, at_low, at_high, weight, keep, send, w_keep, w_send, w_sems):
    width = keep.shape[1]
    rows = at_low.shape[0]
    last = info.shape[0] - 1
    copies = [
        pltpu.make_async_copy(weight.at[:, pl.ds(pl.multiple_of(info[last - 1] * width, 128), width)], w_keep, w_sems.at[0]),
        pltpu.make_async_copy(weight.at[:, pl.ds(pl.multiple_of(info[last] * width, 128), width)], w_send, w_sems.at[1]),
    ]
    for copy in copies:
        copy.start()
    for copy in copies:
        copy.wait()
    for part, source in ((0, at_low), (1, at_high)):
        where = slice(part * rows, (part + 1) * rows)
        send[where, :] = jnp.dot(source[...], w_send[...], preferred_element_type=jnp.float32).astype(send.dtype)
        keep[where, :] = jnp.dot(source[...], w_keep[...], preferred_element_type=jnp.float32).astype(keep.dtype)


def project(info, at_low, at_high, weight):
    rows = at_low.shape[0] * 2
    width = weight.shape[1] // 4
    vmem = pl.BlockSpec(memory_space=pltpu.VMEM)
    out = jax.ShapeDtypeStruct((rows, width), jnp.bfloat16)
    return pl.pallas_call(
        project_body,
        out_shape=[out, out],
        in_specs=[pl.BlockSpec(memory_space=pltpu.SMEM), vmem, vmem, pl.BlockSpec(memory_space=pl.ANY)],
        out_specs=[vmem] * 2,
        scratch_shapes=[
            pltpu.VMEM((weight.shape[0], width), jnp.bfloat16),
            pltpu.VMEM((weight.shape[0], width), jnp.bfloat16),
            pltpu.SemaphoreType.DMA((2,)),
        ],
        compiler_params=pltpu.CompilerParams(vmem_limit_bytes=40 * 1024 * 1024),
        cost_estimate=pl.CostEstimate(flops=4 * rows * weight.shape[0] * width, bytes_accessed=6_000_000, transcendentals=0),
        name="project",
    )(info, at_low, at_high, weight)


def on_device(queries, key_states, value_states, out_weight, slash_offsets, vertical_blocks):
    rows_here, per_group, head = queries.shape
    blocks = rows_here // BLOCK
    half = rows_here // 2
    slash = slash_offsets.shape[1]
    shard = lax.axis_index("ctx")
    ctx_count = lax.axis_size("ctx")
    place = lax.axis_index("heads")
    cfg = (slash, ctx_count, blocks, per_group, head)

    kv = jnp.concatenate([key_states[:, 0, :], value_states[:, 0, :]], axis=1)
    low, high = [kv[:half]], [kv[half:]]
    for _ in range(BAND):
        high.append(shifted(high[-1], "ctx", 1))
        low.append(shifted(low[-1], "ctx", 1))
    own_vertical = lax.dynamic_index_in_dim(vertical_blocks[0], shard, 0, keepdims=False)
    tile = lax.dynamic_slice_in_dim(kv, own_vertical * BLOCK, BLOCK, 0)
    with_tiles = ctx_count > BAND + 1
    if with_tiles:
        tiles = lax.all_gather(tile, "ctx", axis=0, tiled=True)
    else:
        tiles = shifted(tile, "ctx", BAND)

    q = queries.reshape(blocks, BLOCK, per_group, head).transpose(0, 2, 1, 3)
    q = q.reshape(blocks, per_group * BLOCK, head)

    far_keep = place ^ 2
    far_send = place ^ 3
    position = jnp.concatenate([slash_offsets[0], vertical_blocks[0]])
    info_far = jnp.concatenate([position, jnp.stack([shard, far_keep, far_send]).astype(jnp.int32)])
    info_near = jnp.stack([place, place ^ 1]).astype(jnp.int32)

    def window(parts):
        pieces, loads = [], []
        for stride, part in parts:
            pieces.append((low, high)[part][stride])
            loads.append((BAND - stride) * rows_here + part * half)
        return pieces, loads

    upper = window([(3, 1), (2, 0), (2, 1), (1, 0), (1, 1), (0, 0), (0, 1)])
    lower = window([(3, 0), (3, 1), (2, 0), (2, 1), (1, 0), (1, 1), (0, 0)])
    mid = blocks // 2
    att_high, keep_high, send_high = attention(cfg, info_far, q[mid:], out_weight, *upper, tiles, mid, with_tiles)
    from_core_high = swapped(send_high, 1)
    across_high = swapped(keep_high + from_core_high, 2)
    att_low, keep_low, send_low = attention(cfg, info_far, q[:mid], out_weight, *lower, tiles, 0, with_tiles)
    from_core_low = swapped(send_low, 1)
    across_low = swapped(keep_low + from_core_low, 2)
    keep, send = project(info_near, att_low, att_high, out_weight)
    from_core = swapped(send, 1)
    across = jnp.concatenate([across_low, across_high], axis=0).astype(jnp.float32)
    total = keep.astype(jnp.float32) + from_core.astype(jnp.float32) + across
    return total.astype(jnp.bfloat16)


def solution(mesh):
    placed = (
        P(("groups", "ctx"), "heads", None),
        P(("groups", "ctx"), "heads", None),
        P(("groups", "ctx"), "heads", None),
        P("heads", None),
        P(("groups", "heads"), None),
        P(("groups", "heads"), None),
    )
    return jax.shard_map(
        on_device,
        mesh=mesh,
        in_specs=placed,
        out_specs=P(("groups", "ctx"), "heads"),
        check_vma=False,
    )
```

time: 156 us -> 76.7 us (0.49)
  the two profiles are of different devices: /device:TPU:28 before, /device:TPU:0 now
where the time goes in v1:
time: 76.7 us; the launch traced here: 76.2 us
  starting transfers between devices  26.7 us (35%)
  waiting for transfers between devices  22.8 us (30%)
  Pallas kernels  14.2 us (19%)
  other arithmetic  5.32 us (7%)
  local copies, waits for them, and re-layouts  5.15 us (7%)
  between operations  2.04 us (3%)
    ppermute x7, starting transfers between devices, shifted(): lax.ppermute(value, axis, [(source, source + steps) for source in range(c...  23.8 us
    ppermute x5, waiting for transfers between devices, swapped(): lax.ppermute(value, 'heads', [(source, source ^ flip) for source in range...  20.5 us
    pallas_call x2, Pallas kernels, attention(): pl.pallas_call(functools.partial(attention_body, cfg, first_block, loads,...  11.1 us
    unnamed x14, local copies, waits for them, and re-layouts  3.74 us
    pallas_call x1, Pallas kernels, project(): pl.pallas_call(project_body, out_shape=[out, out], in_specs=[pl.BlockSpec...  3.14 us
    ppermute x5, starting transfers between devices, swapped(): lax.ppermute(value, 'heads', [(source, source ^ flip) for source in range...  2.87 us
    concatenate x2, other arithmetic, on_device(): kv = jnp.concatenate([key_states[:, 0, :], value_states[:, 0, :]], axis=1)  2.48 us
    ppermute x7, waiting for transfers between devices, shifted(): lax.ppermute(value, axis, [(source, source + steps) for source in range(c...  2.34 us
  transfers between devices with their start and end apart: 12, of which 4 were waited for; matrix products, arithmetic and copies ran while one was open for 6% of the time, Pallas kernels for 11%

profile of v1, /device:TPU:0, one launch (start us, length us, event | category | flops | bytes accessed | tf_op | source)
XLA Modules:
  0.0 76.2 jit_solution(3232245436719655502)
XLA Ops:
  0.0 1.1 %fusion.1 = (bf16[256,256]{1,0:T(8,128)(2,1)S(1)}, bf16[256,256]{1,0:T(8,128)(2,1)S(1)}) fusion(bf16[512,128]{1,0:T(8,128)(2,1)} %bitcast.22, bf16[512,128]{1,0:T(8,128)(2,1)} %bitcast.24), kind=kLoop, calls=%fused_computation.9 | loop fusion | flops 524288 | bytes 524288 | tf_op jit(solution)/shard_map/concatenate | solution.py:203
  1.1 4.9 %collective-permute-start = (bf16[256,256]{1,0:T(8,128)(2,1)S(1)}, bf16[256,256]{1,0:T(8,128)(2,1)S(1)}, u32[]{:S(2)}, u32[]{:S(2)}) collective-permute-start(bf16[256,256]{1,0:T(8,128)(2,1)S(1)} %get-tuple-element.24.refs_9_.refs_8_), channel_id=1, source_target_pairs={{0,4},{4,8},{8,12},{1,5},{5,9},{9,13},{2,6},{6,10},{10,14},{3,7},{... | collective-permute-start | bytes 393224 | tf_op jit(solution)/shard_map/ppermute | solution.py:18
  6.1 3.5 %collective-permute-start.3 = (bf16[256,256]{1,0:T(8,128)(2,1)S(1)}, bf16[256,256]{1,0:T(8,128)(2,1)S(1)}, u32[]{:S(2)}, u32[]{:S(2)}) collective-permute-start(bf16[256,256]{1,0:T(8,128)(2,1)S(1)} %get-tuple-element.23.refs_9_), channel_id=1, source_target_pairs={{0,4},{4,8},{8,12},{1,5},{5,9},{9,13},{2,6},{6,10},{10,14},{3,7},{... | collective-permute-start | bytes 393224 | tf_op jit(solution)/shard_map/ppermute | solution.py:18
  9.6 4.2 %collective-permute-start.1 = (bf16[256,256]{1,0:T(8,128)(2,1)S(1)}, bf16[256,256]{1,0:T(8,128)(2,1)}, u32[]{:S(2)}, u32[]{:S(2)}) collective-permute-start(bf16[256,256]{1,0:T(8,128)(2,1)S(1)} %collective-permute-done.refs_7_.refs_6_), channel_id=1, source_target_pairs={{0,4},{4,8},{8,12},{1,5},{5,9},{9,13},{2,6},{6,10},{10,14},{3,7},{... | collective-permute-start | bytes 393224 | tf_op jit(solution)/shard_map/ppermute | solution.py:18
  13.8 3.5 %collective-permute-start.4 = (bf16[256,256]{1,0:T(8,128)(2,1)S(1)}, bf16[256,256]{1,0:T(8,128)(2,1)}, u32[]{:S(2)}, u32[]{:S(2)}) collective-permute-start(bf16[256,256]{1,0:T(8,128)(2,1)S(1)} %collective-permute-done.3.refs_8_.refs_7_), channel_id=1, source_target_pairs={{0,4},{4,8},{8,12},{1,5},{5,9},{9,13},{2,6},{6,10},{10,14},{3,7},{... | collective-permute-start | bytes 393224 | tf_op jit(solution)/shard_map/ppermute | solution.py:18
  17.3 1.3 %fusion.4 = s32[1,1]{1,0:T(1,128)} fusion(s32[1,4]{1,0:T(1,128)} %param.11, s32[]{:T(128)S(6)} %select_n.7), kind=kLoop, calls=%fused_computation.14 | loop fusion | flops 1 | bytes 12 | tf_op jit(solution)/shard_map/mul | solution.py:209
  20.5 1.4 %fusion.2 = bf16[64,256]{1,0:T(8,128)(2,1)} fusion(s32[]{:T(128)S(6)} %select_n.8, bf16[512,128]{1,0:T(8,128)(2,1)} %bitcast.23, bf16[512,128]{1,0:T(8,128)(2,1)} %bitcast.25), kind=kLoop, calls=%fused_computation.10 | loop fusion | flops 65536 | bytes 294916 | tf_op jit(solution)/shard_map/concatenate | solution.py:203
  21.9 2.6 %collective-permute-start.6 = (bf16[64,256]{1,0:T(8,128)(2,1)}, bf16[64,256]{1,0:T(8,128)(2,1)}, u32[]{:S(2)}, u32[]{:S(2)}) collective-permute-start(bf16[64,256]{1,0:T(8,128)(2,1)} %fusion.2), channel_id=1, source_target_pairs={{0,12},{1,13},{2,14},{3,15},{16,28},{17,29},{18,30},{19,31}} | collective-permute-start | bytes 98312 | tf_op jit(solution)/shard_map/ppermute | solution.py:18
  24.4 1.3 %copy.9 = bf16[8,64,7,128]{3,1,2,0:T(8,128)(2,1)S(1)} copy(bf16[8,64,7,128]{3,1,0,2:T(8,128)(2,1)} %bitcast.21) | data formatting | bytes 1835008 | tf_op jit(solution)/shard_map/reshape | solution.py:216
  25.7 3.1 %collective-permute-start.2 = (bf16[256,256]{1,0:T(8,128)(2,1)}, bf16[256,256]{1,0:T(8,128)(2,1)}, u32[]{:S(2)}, u32[]{:S(2)}) collective-permute-start(bf16[256,256]{1,0:T(8,128)(2,1)} %collective-permute-done.1.refs_5_.refs_4_), channel_id=1, source_target_pairs={{0,4},{4,8},{8,12},{1,5},{5,9},{9,13},{2,6},{6,10},{10,14},{3,7},{... | collective-permute-start | bytes 393224 | tf_op jit(solution)/shard_map/ppermute | solution.py:18
  28.8 1.9 %collective-permute-start.5 = (bf16[256,256]{1,0:T(8,128)(2,1)}, bf16[256,256]{1,0:T(8,128)(2,1)}, u32[]{:S(2)}, u32[]{:S(2)}) collective-permute-start(bf16[256,256]{1,0:T(8,128)(2,1)} %collective-permute-done.4.refs_6_.refs_5_), channel_id=1, source_target_pairs={{0,4},{4,8},{8,12},{1,5},{5,9},{9,13},{2,6},{6,10},{10,14},{3,7},{... | collective-permute-start | bytes 393224 | tf_op jit(solution)/shard_map/ppermute | solution.py:18
  31.0 0.9 %collective-permute-done.2.refs_3_ = bf16[256,256]{1,0:T(8,128)(2,1)} collective-permute-done((bf16[256,256]{1,0:T(8,128)(2,1)}, bf16[256,256]{1,0:T(8,128)(2,1)}, u32[]{:S(2)}, u32[]{:S(2)}) %collective-permute-start.2) | collective-permute-done | bytes 131104 | tf_op jit(solution)/shard_map/ppermute | solution.py:18
  31.9 1.4 %collective-permute-done.5.refs_4_.refs_3_ = bf16[256,256]{1,0:T(8,128)(2,1)} collective-permute-done((bf16[256,256]{1,0:T(8,128)(2,1)}, bf16[256,256]{1,0:T(8,128)(2,1)}, u32[]{:S(2)}, u32[]{:S(2)}) %collective-permute-start.5) | collective-permute-done | bytes 131104 | tf_op jit(solution)/shard_map/ppermute | solution.py:18
  33.3 2.8 %copy-done = bf16[896,3584]{1,0:T(8,128)(2,1)S(1)} copy-done((bf16[896,3584]{1,0:T(8,128)(2,1)S(1)}, bf16[896,3584]{1,0:T(8,128)(2,1)}, u32[]{:S(2)}) %copy-start) | copy-done | bytes 6422552
  36.2 0.9 %copy-done.2 = bf16[256,256]{1,0:T(8,128)(2,1)S(1)} copy-done((bf16[256,256]{1,0:T(8,128)(2,1)S(1)}, bf16[256,256]{1,0:T(8,128)(2,1)}, u32[]{:S(2)}) %copy-start.2) | copy-done | bytes 131096
  37.1 5.5 %attend.2 = (bf16[256,896]{1,0:T(8,128)(2,1)S(1)}, bf16[256,896]{1,0:T(8,128)(2,1)S(1)}, bf16[256,896]{1,0:T(8,128)(2,1)S(1)}) custom-call(s32[15]{0:T(128)S(1)} %concatenate.9.refs_0_, bf16[4,448,128]{2,1,0:T(8,128)(2,1)S(1)} %bitcast.19, bf16[896,3584]{1,0:T(8,128)(2,1)S(1)} %copy-done, bf16[256,256]{1,0:T(8,128)(2,1)} %collective-permute-done.2.refs_3_, ...), custom_call_target="tpu_custom_call" | custom-call | flops 2231369728 | bytes 6000000 | tf_op jit(solution)/shard_map/attend/pallas_call | solution.py:133
  42.7 5.6 %attend.3 = (bf16[256,896]{1,0:T(8,128)(2,1)S(1)}, bf16[256,896]{1,0:T(8,128)(2,1)S(1)}, bf16[256,896]{1,0:T(8,128)(2,1)S(1)}) custom-call(s32[15]{0:T(128)S(1)} %concatenate.9.refs_0_, bf16[4,448,128]{2,1,0:T(8,128)(2,1)S(1)} %bitcast.18, bf16[896,3584]{1,0:T(8,128)(2,1)S(1)} %bitcast.17, bf16[256,256]{1,0:T(8,128)(2,1)} %collective-permute-done.5.refs_4_.refs_3_, ...), custom_call_target="tpu_custom_call" | custom-call | flops 2231369728 | bytes 6000000 | tf_op jit(solution)/shard_map/attend/pallas_call | solution.py:133
  48.3 0.5 collective-permute-start.10
  48.8 3.1 %project.1 = (bf16[512,896]{1,0:T(8,128)(2,1)S(1)}, bf16[512,896]{1,0:T(8,128)(2,1)S(1)}) custom-call(s32[2]{0:T(128)S(1)} %pad_add_fusion.info, bf16[256,896]{1,0:T(8,128)(2,1)S(1)} %get-tuple-element.13.at_low, bf16[256,896]{1,0:T(8,128)(2,1)S(1)} %get-tuple-element.14.at_high, bf16[896,3584]{1,0:T(8,128)(2,1)S(1)} %bitcast.17), custom_call_target="tpu_custom_call" | custom-call | flops 1644167168 | bytes 6000000 | tf_op jit(solution)/shard_map/project/pallas_call | solution.py:177
  52.2 1.6 %collective-permute-start.9 = (bf16[256,896]{1,0:T(8,128)(2,1)S(1)}, bf16[256,896]{1,0:T(8,128)(2,1)S(1)}, u32[]{:S(2)}, u32[]{:S(2)}) collective-permute-start(bf16[256,896]{1,0:T(8,128)(2,1)S(1)} %add.22), channel_id=1, source_target_pairs={{0,2},{1,3},{2,0},{3,1},{4,6},{5,7},{6,4},{7,5},{8,10},{9,11},{10,... | collective-permute-start | bytes 1376264 | tf_op jit(solution)/shard_map/ppermute | solution.py:23
  53.9 0.6 collective-permute-start.11
  54.5 11.1 %collective-permute-done.9 = bf16[256,896]{1,0:T(8,128)(2,1)S(1)} collective-permute-done((bf16[256,896]{1,0:T(8,128)(2,1)S(1)}, bf16[256,896]{1,0:T(8,128)(2,1)S(1)}, u32[]{:S(2)}, u32[]{:S(2)}) %collective-permute-start.9) | collective-permute-done | bytes 458784 | tf_op jit(solution)/shard_map/ppermute | solution.py:23
  65.6 9.4 %collective-permute-done.11 = bf16[256,896]{1,0:T(8,128)(2,1)S(1)} collective-permute-done((bf16[256,896]{1,0:T(8,128)(2,1)S(1)}, bf16[256,896]{1,0:T(8,128)(2,1)S(1)}, u32[]{:S(2)}, u32[]{:S(2)}) %collective-permute-start.11) | collective-permute-done | bytes 458784 | tf_op jit(solution)/shard_map/ppermute | solution.py:23
  75.0 1.3 %add_convert_fusion = bf16[512,896]{1,0:T(8,128)(2,1)} fusion(bf16[512,896]{1,0:T(8,128)(2,1)S(1)} %collective-permute-done.7, bf16[512,896]{1,0:T(8,128)(2,1)S(1)} %get-tuple-element.15, bf16[256,896]{1,0:T(8,128)(2,1)S(1)} %collective-permute-done.11, bf16[256,896]{1,0:T(8,128)(2,1)S(1)} %collective-permute-done.9), kind=kLoop, calls=%fused_computation | loop fusion | flops 4128768 | bytes 3670016 | tf_op jit(solution)/shard_map/convert_element_type | solution.py:245
  (28 shorter events, 0.7 us)
Async XLA Ops:
  0.0 42.6 %slice-start = ((s8[6422528]{0:T(1024)(128)(4,1)}), s8[2228224]{0:T(1024)(128)(4,1)S(1)}, s32[]{:S(2)}) async-start(s8[6422528]{0:T(1024)(128)(4,1)} %bitcast.16), calls=%async_computation | async-start | bytes 4456448
  1.1 8.4 %collective-permute-start = (bf16[256,256]{1,0:T(8,128)(2,1)S(1)}, bf16[256,256]{1,0:T(8,128)(2,1)S(1)}, u32[]{:S(2)}, u32[]{:S(2)}) collective-permute-start(bf16[256,256]{1,0:T(8,128)(2,1)S(1)} %get-tuple-element.24.refs_9_.refs_8_), channel_id=1, source_target_pairs={{0,4},{4,8},{8,12},{1,5},{5,9},{9,13},{2,6},{6,10},{10,14},{3,7},{... | collective-permute-start | bytes 393224 | tf_op jit(solution)/shard_map/ppermute | solution.py:18
  6.1 7.8 %collective-permute-start.3 = (bf16[256,256]{1,0:T(8,128)(2,1)S(1)}, bf16[256,256]{1,0:T(8,128)(2,1)S(1)}, u32[]{:S(2)}, u32[]{:S(2)}) collective-permute-start(bf16[256,256]{1,0:T(8,128)(2,1)S(1)} %get-tuple-element.23.refs_9_), channel_id=1, source_target_pairs={{0,4},{4,8},{8,12},{1,5},{5,9},{9,13},{2,6},{6,10},{10,14},{3,7},{... | collective-permute-start | bytes 393224 | tf_op jit(solution)/shard_map/ppermute | solution.py:18
  9.6 16.1 %collective-permute-start.1 = (bf16[256,256]{1,0:T(8,128)(2,1)S(1)}, bf16[256,256]{1,0:T(8,128)(2,1)}, u32[]{:S(2)}, u32[]{:S(2)}) collective-permute-start(bf16[256,256]{1,0:T(8,128)(2,1)S(1)} %collective-permute-done.refs_7_.refs_6_), channel_id=1, source_target_pairs={{0,4},{4,8},{8,12},{1,5},{5,9},{9,13},{2,6},{6,10},{10,14},{3,7},{... | collective-permute-start | bytes 393224 | tf_op jit(solution)/shard_map/ppermute | solution.py:18
  13.8 16.9 %copy-start.1 = (bf16[256,256]{1,0:T(8,128)(2,1)}, bf16[256,256]{1,0:T(8,128)(2,1)S(1)}, u32[]{:S(2)}) copy-start(bf16[256,256]{1,0:T(8,128)(2,1)S(1)} %collective-permute-done.3.refs_8_.refs_7_) | copy-start | bytes 393220
  13.8 15.0 %collective-permute-start.4 = (bf16[256,256]{1,0:T(8,128)(2,1)S(1)}, bf16[256,256]{1,0:T(8,128)(2,1)}, u32[]{:S(2)}, u32[]{:S(2)}) collective-permute-start(bf16[256,256]{1,0:T(8,128)(2,1)S(1)} %collective-permute-done.3.refs_8_.refs_7_), channel_id=1, source_target_pairs={{0,4},{4,8},{8,12},{1,5},{5,9},{9,13},{2,6},{6,10},{10,14},{3,7},{... | collective-permute-start | bytes 393224 | tf_op jit(solution)/shard_map/ppermute | solution.py:18
  21.9 9.1 %collective-permute-start.6 = (bf16[64,256]{1,0:T(8,128)(2,1)}, bf16[64,256]{1,0:T(8,128)(2,1)}, u32[]{:S(2)}, u32[]{:S(2)}) collective-permute-start(bf16[64,256]{1,0:T(8,128)(2,1)} %fusion.2), channel_id=1, source_target_pairs={{0,12},{1,13},{2,14},{3,15},{16,28},{17,29},{18,30},{19,31}} | collective-permute-start | bytes 98312 | tf_op jit(solution)/shard_map/ppermute | solution.py:18
  24.4 6.5 %copy-start.3 = (s32[1,8]{1,0:T(1,128)S(1)}, s32[1,8]{1,0:T(1,128)}, u32[]{:S(2)}) copy-start(s32[1,8]{1,0:T(1,128)} %param.10) | copy-start | bytes 100
  24.4 6.5 %copy-start.4 = (s32[1,4]{1,0:T(1,128)S(1)}, s32[1,4]{1,0:T(1,128)}, u32[]{:S(2)}) copy-start(s32[1,4]{1,0:T(1,128)} %param.11) | copy-start | bytes 52
  25.7 6.2 %collective-permute-start.2 = (bf16[256,256]{1,0:T(8,128)(2,1)}, bf16[256,256]{1,0:T(8,128)(2,1)}, u32[]{:S(2)}, u32[]{:S(2)}) collective-permute-start(bf16[256,256]{1,0:T(8,128)(2,1)} %collective-permute-done.1.refs_5_.refs_4_), channel_id=1, source_target_pairs={{0,4},{4,8},{8,12},{1,5},{5,9},{9,13},{2,6},{6,10},{10,14},{3,7},{... | collective-permute-start | bytes 393224 | tf_op jit(solution)/shard_map/ppermute | solution.py:18
  28.8 4.5 %collective-permute-start.5 = (bf16[256,256]{1,0:T(8,128)(2,1)}, bf16[256,256]{1,0:T(8,128)(2,1)}, u32[]{:S(2)}, u32[]{:S(2)}) collective-permute-start(bf16[256,256]{1,0:T(8,128)(2,1)} %collective-permute-done.4.refs_6_.refs_5_), channel_id=1, source_target_pairs={{0,4},{4,8},{8,12},{1,5},{5,9},{9,13},{2,6},{6,10},{10,14},{3,7},{... | collective-permute-start | bytes 393224 | tf_op jit(solution)/shard_map/ppermute | solution.py:18
  33.3 2.8 %copy-start = (bf16[896,3584]{1,0:T(8,128)(2,1)S(1)}, bf16[896,3584]{1,0:T(8,128)(2,1)}, u32[]{:S(2)}) copy-start(bf16[896,3584]{1,0:T(8,128)(2,1)} %weight.1) | copy-start | bytes 19267588
  36.2 0.9 %copy-start.2 = (bf16[256,256]{1,0:T(8,128)(2,1)S(1)}, bf16[256,256]{1,0:T(8,128)(2,1)}, u32[]{:S(2)}) copy-start(bf16[256,256]{1,0:T(8,128)(2,1)} %copy-done.1) | copy-start | bytes 393220
  37.1 5.6 %slice-start.1 = ((s8[6422528]{0:T(1024)(128)(4,1)}), s8[4194304]{0:T(1024)(128)(4,1)S(1)}, s32[]{:S(2)}) async-start(s8[6422528]{0:T(1024)(128)(4,1)} %bitcast.16), calls=%async_computation.1 | async-start | bytes 8388608
  42.6 9.5 %collective-permute-start.8 = (bf16[256,896]{1,0:T(8,128)(2,1)S(1)}, bf16[256,896]{1,0:T(8,128)(2,1)S(1)}, u32[]{:S(2)}, u32[]{:S(2)}) collective-permute-start(bf16[256,896]{1,0:T(8,128)(2,1)S(1)} %get-tuple-element.18), channel_id=1, source_target_pairs={{0,1},{1,0},{2,3},{3,2},{4,5},{5,4},{6,7},{7,6},{8,9},{9,8},{10,11... | collective-permute-start | bytes 1376264 | tf_op jit(solution)/shard_map/ppermute | solution.py:23
  48.3 5.5 %collective-permute-start.10 = (bf16[256,896]{1,0:T(8,128)(2,1)S(1)}, bf16[256,896]{1,0:T(8,128)(2,1)S(1)}, u32[]{:S(2)}, u32[]{:S(2)}) collective-permute-start(bf16[256,896]{1,0:T(8,128)(2,1)S(1)} %get-tuple-element.20), channel_id=1, source_target_pairs={{0,1},{1,0},{2,3},{3,2},{4,5},{5,4},{6,7},{7,6},{8,9},{9,8},{10,11... | collective-permute-start | bytes 1376264 | tf_op jit(solution)/shard_map/ppermute | solution.py:23
  52.0 23.0 %collective-permute-start.7 = (bf16[512,896]{1,0:T(8,128)(2,1)S(1)}, bf16[512,896]{1,0:T(8,128)(2,1)S(1)}, u32[]{:S(2)}, u32[]{:S(2)}) collective-permute-start(bf16[512,896]{1,0:T(8,128)(2,1)S(1)} %get-tuple-element.16), channel_id=1, source_target_pairs={{0,1},{1,0},{2,3},{3,2},{4,5},{5,4},{6,7},{7,6},{8,9},{9,8},{10,11... | collective-permute-start | bytes 2752520 | tf_op jit(solution)/shard_map/ppermute | solution.py:23
  52.2 13.4 %collective-permute-start.9 = (bf16[256,896]{1,0:T(8,128)(2,1)S(1)}, bf16[256,896]{1,0:T(8,128)(2,1)S(1)}, u32[]{:S(2)}, u32[]{:S(2)}) collective-permute-start(bf16[256,896]{1,0:T(8,128)(2,1)S(1)} %add.22), channel_id=1, source_target_pairs={{0,2},{1,3},{2,0},{3,1},{4,6},{5,7},{6,4},{7,5},{8,10},{9,11},{10,... | collective-permute-start | bytes 1376264 | tf_op jit(solution)/shard_map/ppermute | solution.py:23
  53.9 21.1 %collective-permute-start.11 = (bf16[256,896]{1,0:T(8,128)(2,1)S(1)}, bf16[256,896]{1,0:T(8,128)(2,1)S(1)}, u32[]{:S(2)}, u32[]{:S(2)}) collective-permute-start(bf16[256,896]{1,0:T(8,128)(2,1)S(1)} %add.23), channel_id=1, source_target_pairs={{0,2},{1,3},{2,0},{3,1},{4,6},{5,7},{6,4},{7,5},{8,10},{9,11},{10,... | collective-permute-start | bytes 1376264 | tf_op jit(solution)/shard_map/ppermute | solution.py:23

commit v2 on v0

v2 whole, which is shorter than its diff:
```python
import functools
import math

import jax
import jax.numpy as jnp
from jax import lax
from jax.experimental import pallas as pl
from jax.experimental.pallas import tpu as pltpu
from jax.sharding import PartitionSpec as P

BLOCK = 64
BAND = 3
NEG = -1e30
VMEM_LIMIT = 12 * 1024 * 1024
COST = pl.CostEstimate(flops=1, bytes_accessed=1, transcendentals=0)
HBM = pl.BlockSpec(memory_space=pltpu.HBM)
VMEM = pl.BlockSpec(memory_space=pltpu.VMEM)
SMEM = pl.BlockSpec(memory_space=pltpu.SMEM)


def shifted(value, axis, steps):
    count = lax.axis_size(axis)
    return lax.ppermute(value, axis, [(source, source + steps) for source in range(count - steps)])


def swapped(value, flip):
    count = lax.axis_size("heads")
    return lax.ppermute(value, "heads", [(source, source ^ flip) for source in range(count)])


def pack_body(keys, values, whole):
    head = keys.shape[1]
    whole[:, :head] = keys[...]
    whole[:, head:] = values[...]


def pack(keys, values):
    rows, head = keys.shape
    return pl.pallas_call(
        pack_body,
        out_shape=jax.ShapeDtypeStruct((rows, 2 * head), keys.dtype),
        in_specs=[VMEM, VMEM],
        out_specs=VMEM,
        compiler_params=pltpu.CompilerParams(vmem_limit_bytes=VMEM_LIMIT),
        cost_estimate=COST,
        name="pack",
    )(keys, values)


def attend_block(cfg, info, q_ref, win, tiles, gathered, local, store):
    slash, n_vert, blocks, heads_here, head = cfg
    shard = lax.axis_index("ctx")
    own = shard * blocks + local
    base = (shard - BAND) * blocks
    count = slash + n_vert
    rows = heads_here * BLOCK
    allowed = []
    for slot in range(slash):
        if slot == 0:
            source = BAND * blocks + local
            allowed.append(None)
        else:
            offset = info[slot]
            offset = jnp.where(offset == 0, info[0], offset)
            source = BAND * blocks + local - offset
            allowed.append(own - offset >= 0)
        piece = win[pl.ds(pl.multiple_of(source * BLOCK, BLOCK), BLOCK), :]
        gathered[slot * BLOCK : (slot + 1) * BLOCK, : 2 * head] = piece
    for shard_from in range(n_vert):
        slot = slash + shard_from
        column = shard_from * blocks + info[slot]
        gap = own - column
        fine = gap > 0
        for other in range(slash):
            fine = jnp.logical_and(fine, gap != info[other])
        allowed.append(fine)
        if tiles is None:
            source = jnp.where(fine, column - base, BAND * blocks + local)
            piece = win[pl.ds(pl.multiple_of(source * BLOCK, BLOCK), BLOCK), :]
        else:
            piece = tiles[shard_from * BLOCK : (shard_from + 1) * BLOCK, :]
        gathered[slot * BLOCK : (slot + 1) * BLOCK, : 2 * head] = piece
    lane = lax.broadcasted_iota(jnp.int32, (1, count * BLOCK), 1) // BLOCK
    bias = jnp.zeros((1, count * BLOCK), jnp.float32)
    for slot in range(1, count):
        bias = jnp.where(lane == slot, jnp.where(allowed[slot], 0.0, NEG), bias)
    col = lax.broadcasted_iota(jnp.int32, (BLOCK, 2 * BLOCK), 1)
    line = lax.broadcasted_iota(jnp.int32, (BLOCK, 2 * BLOCK), 0)
    near = jnp.where(jnp.logical_or(col <= line, col >= BLOCK), bias[:, : 2 * BLOCK], NEG)
    near = jnp.concatenate([near] * heads_here, axis=0)
    q = q_ref[:, local * BLOCK : (local + 1) * BLOCK, :].reshape(rows, head)
    scores = lax.dot_general(q, gathered[:, :head], (((1,), (1,)), ((), ())), preferred_element_type=jnp.float32)
    scores = jnp.concatenate([scores[:, : 2 * BLOCK] + near, scores[:, 2 * BLOCK :] + bias[:, 2 * BLOCK :]], axis=1)
    factor = math.log2(math.e) * head ** (-0.5)
    row_max = jnp.max(scores, axis=1, keepdims=True)
    weights = jnp.exp2((scores - row_max) * factor).astype(jnp.bfloat16)
    mixed = lax.dot_general(weights, gathered[:, head:], (((1,), (0,)), ((), ())), preferred_element_type=jnp.float32)
    result = (mixed[:, :head] / mixed[:, head:]).astype(jnp.bfloat16)
    for h in range(heads_here):
        store(h, result[h * BLOCK : (h + 1) * BLOCK])


def weight_columns(weight, block, width):
    return weight.at[:, pl.ds(pl.multiple_of(block * width, 128), width)]


def matmul(left, right, out):
    out[...] = jnp.dot(left[...], right[...], preferred_element_type=jnp.float32).astype(out.dtype)


def attend_rows(cfg, info, q_ref, win, tiles, gathered, first, attended):
    slash, n_vert, blocks, heads_here, head = cfg
    for index in range(attended.shape[0] // BLOCK):

        def store(h, value):
            attended[index * BLOCK : (index + 1) * BLOCK, h * head : (h + 1) * head] = value

        part = gathered.at[index % gathered.shape[0]]
        attend_block(cfg, info, q_ref, win, tiles, part, first + index, store)


def fill_ones(gathered, head):
    for slot in range(gathered.shape[0]):
        gathered[slot, :, 2 * head :] = jnp.ones((gathered.shape[1], head), jnp.bfloat16)


def early_body(cfg, first, n_pieces, info, q_ref, w_send, *refs):
    head = cfg[-1]
    pieces = refs[:n_pieces]
    tiles = refs[n_pieces] if len(refs) > n_pieces + 5 else None
    attended, send, win, gathered, sems = refs[-5:]
    rows = pieces[0].shape[0]
    copies = []
    for index, piece in enumerate(pieces):
        copies.append(pltpu.make_async_copy(piece, win.at[index * rows : (index + 1) * rows, :], sems.at[index]))
    for copy in copies:
        copy.start()
    fill_ones(gathered, head)
    for copy in copies:
        copy.wait()
    attend_rows(cfg, info, q_ref, win, tiles, gathered, first, attended)
    matmul(attended, w_send, send)


def late_body(cfg, info, q_ref, w_send, w_keep, win, early, *refs):
    head = cfg[-1]
    tiles = refs[0] if len(refs) > 5 else None
    attended, send, keep, keep_early, gathered = refs[-5:]
    fill_ones(gathered, head)
    attend_rows(cfg, info, q_ref, win, tiles, gathered, 0, attended)
    matmul(attended, w_send, send)
    matmul(early, w_keep, keep_early)
    matmul(attended, w_keep, keep)


def rows_of(count, like):
    return jax.ShapeDtypeStruct((count, like), jnp.bfloat16)


def kernel_params(tiles):
    return dict(
        compiler_params=pltpu.CompilerParams(vmem_limit_bytes=4 * VMEM_LIMIT if tiles else VMEM_LIMIT),
        cost_estimate=COST,
    )


def gather_scratch(cfg):
    return pltpu.VMEM((2, (cfg[0] + cfg[1]) * BLOCK, 3 * cfg[-1]), jnp.bfloat16)


def attend_early(cfg, first, info, q, w_send, pieces, tiles):
    slash, n_vert, blocks, heads_here, head = cfg
    rows = (blocks - first) * BLOCK
    return pl.pallas_call(
        functools.partial(early_body, cfg, first, len(pieces)),
        out_shape=[rows_of(rows, heads_here * head), rows_of(rows, w_send.shape[1]), rows_of((BAND + 1) * blocks * BLOCK, 2 * head)],
        in_specs=[SMEM, VMEM, VMEM] + [HBM] * len(pieces) + [VMEM] * len(tiles),
        out_specs=[VMEM] * 3,
        scratch_shapes=[gather_scratch(cfg), pltpu.SemaphoreType.DMA((len(pieces),))],
        name="attend_early",
        **kernel_params(tiles),
    )(info, q, w_send, *pieces, *tiles)


def attend_late(cfg, count, info, q, w_send, w_keep, win, early, tiles):
    slash, n_vert, blocks, heads_here, head = cfg
    rows = count * BLOCK
    width = w_send.shape[1]
    return pl.pallas_call(
        functools.partial(late_body, cfg),
        out_shape=[rows_of(rows, heads_here * head), rows_of(rows, width), rows_of(rows, width), rows_of(early.shape[0], width)],
        in_specs=[SMEM] + [VMEM] * (5 + len(tiles)),
        out_specs=[VMEM] * 4,
        scratch_shapes=[gather_scratch(cfg)],
        name="attend_late",
        **kernel_params(tiles),
    )(info, q, w_send, w_keep, win, early, *tiles)


def stage_body(queries, weight, first, q, *refs):
    slots, sems = refs[:4], refs[4]
    width = slots[0].shape[1]
    place = lax.axis_index("heads")
    copies = [pltpu.make_async_copy(queries, q, sems.at[0])]
    for index, flip in enumerate((3, 2, 1, 0)):
        copies.append(pltpu.make_async_copy(weight_columns(weight, place ^ flip, width), slots[index], sems.at[1 + index]))
    for copy in copies:
        copy.start()
    for copy in copies:
        copy.wait()


def stage(q, weight, first):
    part = jax.ShapeDtypeStruct((weight.shape[0], weight.shape[1] // 4), weight.dtype)
    return pl.pallas_call(
        stage_body,
        out_shape=[jax.ShapeDtypeStruct(q.shape, q.dtype)] + [part] * 4,
        in_specs=[HBM] * 3,
        out_specs=[VMEM] * 5,
        scratch_shapes=[pltpu.SemaphoreType.DMA((5,))],
        compiler_params=pltpu.CompilerParams(vmem_limit_bytes=VMEM_LIMIT),
        cost_estimate=COST,
        name="stage",
    )(q, weight, first)


def project_body(late, early, w_send, w_keep, after, send, keep):
    rows = late.shape[0]
    for at, source in ((slice(0, rows), late), (slice(rows, send.shape[0]), early)):
        matmul(source, w_send, send.at[at, :])
        matmul(source, w_keep, keep.at[at, :])


def project(late, early, w_send, w_keep, after):
    rows = late.shape[0] + early.shape[0]
    return pl.pallas_call(
        project_body,
        out_shape=[rows_of(rows, w_send.shape[1])] * 2,
        in_specs=[VMEM] * 4 + [HBM],
        out_specs=[VMEM] * 2,
        compiler_params=pltpu.CompilerParams(vmem_limit_bytes=VMEM_LIMIT),
        cost_estimate=COST,
        name="project",
    )(late, early, w_send, w_keep, after)


def finish_body(at, near, other, across, *refs):
    out, total, sem = refs[-3:]
    rows = total.shape[0]
    where = slice(at, at + rows)
    value = near[where, :].astype(jnp.float32) + other[where, :].astype(jnp.float32) + across[...].astype(jnp.float32)
    total[...] = value.astype(total.dtype)
    copy = pltpu.make_async_copy(total, out.at[where, :], sem)
    copy.start()
    copy.wait()


def finish(near, other, across, at, before=None):
    held = [] if before is None else [before]
    return pl.pallas_call(
        functools.partial(finish_body, at),
        out_shape=rows_of(*near.shape),
        in_specs=[VMEM] * 3 + [HBM] * len(held),
        out_specs=HBM,
        scratch_shapes=[pltpu.VMEM(across.shape, across.dtype), pltpu.SemaphoreType.DMA],
        input_output_aliases={3: 0} if held else {},
        compiler_params=pltpu.CompilerParams(vmem_limit_bytes=VMEM_LIMIT),
        cost_estimate=COST,
        name="finish",
    )(near, other, across, *held)


def on_device(queries, key_states, value_states, out_weight, slash_offsets, vertical_blocks):
    rows_here, per_group, head = queries.shape
    blocks = rows_here // BLOCK
    late_blocks = blocks // 2
    ctx_count = lax.axis_size("ctx")
    cfg = (slash_offsets.shape[1], ctx_count, blocks, per_group, head)

    whole = pack(key_states[:, 0, :], value_states[:, 0, :])
    pieces = [shifted(whole, "ctx", stride) for stride in range(BAND, 0, -1)] + [whole]
    q, w_far_send, w_far_keep, w_near_send, w_near_keep = stage(queries.transpose(1, 0, 2), out_weight, whole)
    tiles = []
    if ctx_count > BAND + 1:
        start = lax.dynamic_index_in_dim(vertical_blocks[0], lax.axis_index("ctx"), 0, keepdims=False) * BLOCK
        tile = lax.dynamic_slice_in_dim(whole, start, BLOCK, 0)
        tiles.append(lax.all_gather(tile, "ctx", axis=0, tiled=True))
    info = jnp.concatenate([slash_offsets[0], vertical_blocks[0]])

    early, send, win = attend_early(cfg, late_blocks, info, q, w_far_send, pieces, tiles)
    core_early = swapped(send, 1)
    late, send, keep_late, keep_early = attend_late(cfg, late_blocks, info, q, w_far_send, w_far_keep, win, early, tiles)
    core_late = swapped(send, 1)
    across_early = swapped(keep_early + core_early, 2)
    mine_late = keep_late + core_late
    across_late = swapped(mine_late, 2)
    near_send, near_keep = project(late, early, w_near_send, w_near_keep, mine_late)
    core_near = swapped(near_send, 1)
    out = finish(near_keep, core_near, across_early, late_blocks * BLOCK)
    return finish(near_keep, core_near, across_late, 0, out)


def solution(mesh):
    placed = (
        P(("groups", "ctx"), "heads", None),
        P(("groups", "ctx"), "heads", None),
        P(("groups", "ctx"), "heads", None),
        P("heads", None),
        P(("groups", "heads"), None),
        P(("groups", "heads"), None),
    )
    return jax.shard_map(
        on_device,
        mesh=mesh,
        in_specs=placed,
        out_specs=P(("groups", "ctx"), "heads"),
        check_vma=False,
    )
```

time: 156 us -> 65 us (0.42); the launches traced: 154 us -> 64.7 us
  blocking collectives: 28.6 us -> 0 us
  matrix products: 27.8 us -> 0 us
  between operations: 15.8 us -> 0.12 us
  other arithmetic: 14.2 us -> 0.32 us
  Pallas kernels: 0 us -> 12.9 us
  waiting for transfers between devices: 47.6 us -> 38.8 us
  local copies, waits for them, and re-layouts: 11.7 us -> 5.81 us
    unnamed x2 -> x0, waiting for transfers between devices: 44.7 us -> none
    ppermute x6 -> x8, waiting for transfers between devices: 2.85 us -> 38.8 us  [the longest x5 20.9 us: swapped(): lax.ppermute(value, 'heads', [(source, source ^ flip) for source in range...]
    all_gather x2 -> x0, blocking collectives: 28.6 us -> none  [the longest x1 15.5 us: on_device(): tile_key_part = lax.all_gather(tile_keys, 'ctx', axis=0, tiled=True)]
    dot_general x11 -> x0, matrix products: 27.8 us -> none  [the longest x5 12.2 us: attend(): jnp.einsum('qgk,kd->qgd', weights.astype(jnp.bfloat16), value_part, prefe...]
    pallas_call x0 -> x7, Pallas kernels: none -> 12.9 us  [the longest x1 4.42 us: attend_late(): pl.pallas_call(functools.partial(late_body, cfg), out_shape=[rows_of(rows...]
    reduce_sum x6 -> x0, other arithmetic: 8.24 us -> none  [the longest x5 8.15 us: attend(): running_sum = running_sum * rescale + jnp.sum(weights, axis=-1)]
    unnamed x17 -> x12, local copies, waits for them, and re-layouts: 9.52 us -> 5.81 us
    reduce_or x2 -> x0, other arithmetic: 3.51 us -> none  [in_band(): return jnp.any(distance[..., None] == offsets, axis=-1)]
  transfers between devices with their start and end apart: 7 -> 8, of which waited for: 2 -> 5; matrix products, arithmetic and copies ran while one was open for 24% -> 0% of each run, Pallas kernels for 0% -> 6%
where the time goes in v2:
time: 65 us; the launch traced here: 64.7 us
  waiting for transfers between devices  38.8 us (60%)
  Pallas kernels  12.9 us (20%)
  starting transfers between devices  6.75 us (10%)
  local copies, waits for them, and re-layouts  5.81 us (9%)
    ppermute x5, waiting for transfers between devices, swapped(): lax.ppermute(value, 'heads', [(source, source ^ flip) for source in range...  20.9 us
    ppermute x3, waiting for transfers between devices, shifted(): lax.ppermute(value, axis, [(source, source + steps) for source in range(c...  17.9 us
    unnamed x12, local copies, waits for them, and re-layouts  5.81 us
    pallas_call x1, Pallas kernels, attend_late(): pl.pallas_call(functools.partial(late_body, cfg), out_shape=[rows_of(rows...  4.42 us
    ppermute x3, starting transfers between devices, shifted(): lax.ppermute(value, axis, [(source, source + steps) for source in range(c...  3.88 us
    pallas_call x1, Pallas kernels, attend_early(): pl.pallas_call(functools.partial(early_body, cfg, first, len(pieces)), ou...  3.49 us
    ppermute x5, starting transfers between devices, swapped(): lax.ppermute(value, 'heads', [(source, source ^ flip) for source in range...  2.88 us
    pallas_call x1, Pallas kernels, project(): pl.pallas_call(project_body, out_shape=[rows_of(rows, w_send.shape[1])] *...  2.27 us
  transfers between devices with their start and end apart: 8, of which 5 were waited for; matrix products, arithmetic and copies ran while one was open for 0% of the time, Pallas kernels for 6%

profile of v2, /device:TPU:28, one launch (start us, length us, event | category | flops | bytes accessed | tf_op | source)
XLA Modules:
  0.0 64.7 jit_solution(4046856844327716221)
XLA Ops:
  0.0 0.9 %copy-done.2 = bf16[512,1,128]{2,0,1:T(8,128)(2,1)S(1)} copy-done((bf16[512,1,128]{2,0,1:T(8,128)(2,1)S(1)}, bf16[512,1,128]{2,0,1:T(8,128)(2,1)}, u32[]{:S(2)}) %copy-start.2) | copy-done | bytes 131096
  0.9 0.9 %copy-done.3 = bf16[512,1,128]{2,0,1:T(8,128)(2,1)S(1)} copy-done((bf16[512,1,128]{2,0,1:T(8,128)(2,1)S(1)}, bf16[512,1,128]{2,0,1:T(8,128)(2,1)}, u32[]{:S(2)}) %copy-start.3) | copy-done | bytes 131096
  1.9 1.3 %collective-permute-start.2 = (bf16[512,256]{1,0:T(8,128)(2,1)S(1)}, bf16[512,256]{1,0:T(8,128)(2,1)S(1)}, u32[]{:S(2)}, u32[]{:S(2)}) collective-permute-start(bf16[512,256]{1,0:T(8,128)(2,1)S(1)} %pack.1.first.refs_3_), channel_id=1, source_target_pairs={{0,4},{4,8},{8,12},{1,5},{5,9},{9,13},{2,6},{6,10},{10,14},{3,7},{... | collective-permute-start | bytes 786440 | tf_op jit(solution)/shard_map/ppermute | solution.py:23
  3.2 1.3 %collective-permute-start.1 = (bf16[512,256]{1,0:T(8,128)(2,1)S(1)}, bf16[512,256]{1,0:T(8,128)(2,1)S(1)}, u32[]{:S(2)}, u32[]{:S(2)}) collective-permute-start(bf16[512,256]{1,0:T(8,128)(2,1)S(1)} %pack.1.first.refs_3_), channel_id=1, source_target_pairs={{0,8},{4,12},{1,9},{5,13},{2,10},{6,14},{3,11},{7,15},{16,24},{20,... | collective-permute-start | bytes 786440 | tf_op jit(solution)/shard_map/ppermute | solution.py:23
  4.5 1.3 %collective-permute-start = (bf16[512,256]{1,0:T(8,128)(2,1)S(1)}, bf16[512,256]{1,0:T(8,128)(2,1)S(1)}, u32[]{:S(2)}, u32[]{:S(2)}) collective-permute-start(bf16[512,256]{1,0:T(8,128)(2,1)S(1)} %pack.1.first.refs_3_), channel_id=1, source_target_pairs={{0,12},{1,13},{2,14},{3,15},{16,28},{17,29},{18,30},{19,31}} | collective-permute-start | bytes 786440 | tf_op jit(solution)/shard_map/ppermute | solution.py:23
  5.8 2.8 %copy-done = bf16[896,3584]{1,0:T(8,128)(2,1)S(1)} copy-done((bf16[896,3584]{1,0:T(8,128)(2,1)S(1)}, bf16[896,3584]{1,0:T(8,128)(2,1)}, u32[]{:S(2)}) %copy-start) | copy-done | bytes 6422552
  8.6 1.2 %copy-done.1 = bf16[512,7,128]{2,0,1:T(8,128)(2,1)S(1)} copy-done((bf16[512,7,128]{2,0,1:T(8,128)(2,1)S(1)}, bf16[512,7,128]{2,0,1:T(8,128)(2,1)}, u32[]{:S(2)}) %copy-start.1) | copy-done | bytes 917528
  9.8 0.8 %stage.1 = (bf16[7,512,128]{2,1,0:T(8,128)(2,1)S(1)}, bf16[896,896]{1,0:T(8,128)(2,1)S(1)}, bf16[896,896]{1,0:T(8,128)(2,1)S(1)}, bf16[896,896]{1,0:T(8,128)(2,1)S(1)}, bf16[896,896]{1,0:T(8,128)(2,1)S(1)}) custom-call(bf16[7,512,128]{2,1,0:T(8,128)(2,1)S(1)} %bitcast.5, bf16[896,3584]{1,0:T(8,128)(2,1)S(1)} %copy-done, bf16[512,256]{1,0:T(8,128)(2,1)S(1)} %pack.1.first.refs_3_), custom_call_target="tpu_custom_call" | custom-call | flops 1 | bytes 1 | tf_op jit(solution)/shard_map/stage/pallas_call | solution.py:215
  10.7 1.5 %collective-permute-done.2.refs_2_ = bf16[512,256]{1,0:T(8,128)(2,1)S(1)} collective-permute-done((bf16[512,256]{1,0:T(8,128)(2,1)S(1)}, bf16[512,256]{1,0:T(8,128)(2,1)S(1)}, u32[]{:S(2)}, u32[]{:S(2)}) %collective-permute-start.2) | collective-permute-done | bytes 262176 | tf_op jit(solution)/shard_map/ppermute | solution.py:23
  12.2 16.4 %collective-permute-done.1.refs_1_ = bf16[512,256]{1,0:T(8,128)(2,1)S(1)} collective-permute-done((bf16[512,256]{1,0:T(8,128)(2,1)S(1)}, bf16[512,256]{1,0:T(8,128)(2,1)S(1)}, u32[]{:S(2)}, u32[]{:S(2)}) %collective-permute-start.1) | collective-permute-done | bytes 262176 | tf_op jit(solution)/shard_map/ppermute | solution.py:23
  28.5 3.5 %attend_early.1 = (bf16[256,896]{1,0:T(8,128)(2,1)S(1)}, bf16[256,896]{1,0:T(8,128)(2,1)S(1)}, bf16[2048,256]{1,0:T(8,128)(2,1)S(1)}) custom-call(s32[12]{0:T(128)S(1)} %pad_add_fusion.info, bf16[7,512,128]{2,1,0:T(8,128)(2,1)S(1)} %get-tuple-element.19.q_ref, bf16[896,896]{1,0:T(8,128)(2,1)S(1)} %get-tuple-element.20.w_send, ...), custom_call_target="tpu_custom_call" | custom-call | flops 1 | bytes 1 | tf_op jit(solution)/shard_map/attend_early/pallas_call | solution.py:174
  32.0 4.4 %attend_late.1 = (bf16[256,896]{1,0:T(8,128)(2,1)S(1)}, bf16[256,896]{1,0:T(8,128)(2,1)S(1)}, bf16[256,896]{1,0:T(8,128)(2,1)S(1)}, bf16[256,896]{1,0:T(8,128)(2,1)S(1)}) custom-call(s32[12]{0:T(128)S(1)} %pad_add_fusion.info, bf16[7,512,128]{2,1,0:T(8,128)(2,1)S(1)} %get-tuple-element.19.q_ref, bf16[896,896]{1,0:T(8,128)(2,1)S(1)} %get-tuple-element.20.w_send, ...), custom_call_target="tpu_custom_call" | custom-call | flops 1 | bytes 1 | tf_op jit(solution)/shard_map/attend_late/pallas_call | solution.py:189
  36.5 0.5 collective-permute-start.6
  37.0 1.3 %collective-permute-done.3 = bf16[256,896]{1,0:T(8,128)(2,1)S(1)} collective-permute-done((bf16[256,896]{1,0:T(8,128)(2,1)S(1)}, bf16[256,896]{1,0:T(8,128)(2,1)S(1)}, u32[]{:S(2)}, u32[]{:S(2)}) %collective-permute-start.3) | collective-permute-done | bytes 458784 | tf_op jit(solution)/shard_map/ppermute | solution.py:28
  38.3 0.1 add.6.after
  38.5 2.3 %project.1 = (bf16[512,896]{1,0:T(8,128)(2,1)S(1)}, bf16[512,896]{1,0:T(8,128)(2,1)S(1)}) custom-call(bf16[256,896]{1,0:T(8,128)(2,1)S(1)} %get-tuple-element.24.late, bf16[256,896]{1,0:T(8,128)(2,1)S(1)} %get-tuple-element.23.early, bf16[896,896]{1,0:T(8,128)(2,1)S(1)} %get-tuple-element.25.w_send, bf16[896,896]{1,0:T(8,128)(2,1)S(1)} %get-tuple-element.26.w_keep, ...), custom_call_target="tpu_custom_call" | custom-call | flops 1 | bytes 1 | tf_op jit(solution)/shard_map/project/pallas_call | solution.py:236
  40.7 0.2 collective-permute-start.4
  41.0 0.1 add.7
  41.1 1.6 %collective-permute-start.7 = (bf16[256,896]{1,0:T(8,128)(2,1)S(1)}, bf16[256,896]{1,0:T(8,128)(2,1)S(1)}, u32[]{:S(2)}, u32[]{:S(2)}) collective-permute-start(bf16[256,896]{1,0:T(8,128)(2,1)S(1)} %add.7), channel_id=1, source_target_pairs={{0,2},{1,3},{2,0},{3,1},{4,6},{5,7},{6,4},{7,5},{8,10},{9,11},{10,... | collective-permute-start | bytes 1376264 | tf_op jit(solution)/shard_map/ppermute | solution.py:28
  42.7 0.5 collective-permute-start.5
  43.2 11.3 %collective-permute-done.7.across = bf16[256,896]{1,0:T(8,128)(2,1)S(1)} collective-permute-done((bf16[256,896]{1,0:T(8,128)(2,1)S(1)}, bf16[256,896]{1,0:T(8,128)(2,1)S(1)}, u32[]{:S(2)}, u32[]{:S(2)}) %collective-permute-start.7) | collective-permute-done | bytes 458784 | tf_op jit(solution)/shard_map/ppermute | solution.py:28
  54.5 0.9 %finish.2.refs_0_ = bf16[512,896]{1,0:T(8,128)(2,1)} custom-call(bf16[512,896]{1,0:T(8,128)(2,1)S(1)} %get-tuple-element.29.near, bf16[512,896]{1,0:T(8,128)(2,1)S(1)} %collective-permute-done.4.other, bf16[256,896]{1,0:T(8,128)(2,1)S(1)} %collective-permute-done.7.across), custom_call_target="tpu_custom_call" | custom-call | flops 1 | bytes 1 | tf_op jit(solution)/shard_map/finish/pallas_call | solution.py:260
  55.5 8.3 %collective-permute-done.5.across = bf16[256,896]{1,0:T(8,128)(2,1)S(1)} collective-permute-done((bf16[256,896]{1,0:T(8,128)(2,1)S(1)}, bf16[256,896]{1,0:T(8,128)(2,1)S(1)}, u32[]{:S(2)}, u32[]{:S(2)}) %collective-permute-start.5) | collective-permute-done | bytes 458784 | tf_op jit(solution)/shard_map/ppermute | solution.py:28
  63.8 0.9 %finish.3 = bf16[512,896]{1,0:T(8,128)(2,1)} custom-call(bf16[512,896]{1,0:T(8,128)(2,1)S(1)} %get-tuple-element.29.near, bf16[512,896]{1,0:T(8,128)(2,1)S(1)} %collective-permute-done.4.other, bf16[256,896]{1,0:T(8,128)(2,1)S(1)} %collective-permute-done.5.across, bf16[512,896]{1,0:T(8,128)(2,1)} %finish.2.refs_0_), custom_call_target="tpu_custom_call", output_to_operand_aliasing={{}: (3, {})} | custom-call | flops 1 | bytes 1 | tf_op jit(solution)/shard_map/finish/pallas_call | solution.py:260
  (14 shorter events, 0.2 us)
Async XLA Ops:
  0.0 0.9 %copy-start.2 = (bf16[512,1,128]{2,0,1:T(8,128)(2,1)S(1)}, bf16[512,1,128]{2,0,1:T(8,128)(2,1)}, u32[]{:S(2)}) copy-start(bf16[512,1,128]{2,0,1:T(8,128)(2,1)} %param.7) | copy-start | bytes 393220
  0.9 0.9 %copy-start.3 = (bf16[512,1,128]{2,0,1:T(8,128)(2,1)S(1)}, bf16[512,1,128]{2,0,1:T(8,128)(2,1)}, u32[]{:S(2)}) copy-start(bf16[512,1,128]{2,0,1:T(8,128)(2,1)} %param.8) | copy-start | bytes 393220
  1.9 10.3 %collective-permute-start.2 = (bf16[512,256]{1,0:T(8,128)(2,1)S(1)}, bf16[512,256]{1,0:T(8,128)(2,1)S(1)}, u32[]{:S(2)}, u32[]{:S(2)}) collective-permute-start(bf16[512,256]{1,0:T(8,128)(2,1)S(1)} %pack.1.first.refs_3_), channel_id=1, source_target_pairs={{0,4},{4,8},{8,12},{1,5},{5,9},{9,13},{2,6},{6,10},{10,14},{3,7},{... | collective-permute-start | bytes 786440 | tf_op jit(solution)/shard_map/ppermute | solution.py:23
  3.2 25.4 %collective-permute-start.1 = (bf16[512,256]{1,0:T(8,128)(2,1)S(1)}, bf16[512,256]{1,0:T(8,128)(2,1)S(1)}, u32[]{:S(2)}, u32[]{:S(2)}) collective-permute-start(bf16[512,256]{1,0:T(8,128)(2,1)S(1)} %pack.1.first.refs_3_), channel_id=1, source_target_pairs={{0,8},{4,12},{1,9},{5,13},{2,10},{6,14},{3,11},{7,15},{16,24},{20,... | collective-permute-start | bytes 786440 | tf_op jit(solution)/shard_map/ppermute | solution.py:23
  4.5 24.1 %collective-permute-start = (bf16[512,256]{1,0:T(8,128)(2,1)S(1)}, bf16[512,256]{1,0:T(8,128)(2,1)S(1)}, u32[]{:S(2)}, u32[]{:S(2)}) collective-permute-start(bf16[512,256]{1,0:T(8,128)(2,1)S(1)} %pack.1.first.refs_3_), channel_id=1, source_target_pairs={{0,12},{1,13},{2,14},{3,15},{16,28},{17,29},{18,30},{19,31}} | collective-permute-start | bytes 786440 | tf_op jit(solution)/shard_map/ppermute | solution.py:23
  5.8 2.8 %copy-start = (bf16[896,3584]{1,0:T(8,128)(2,1)S(1)}, bf16[896,3584]{1,0:T(8,128)(2,1)}, u32[]{:S(2)}) copy-start(bf16[896,3584]{1,0:T(8,128)(2,1)} %weight.1) | copy-start | bytes 19267588
  8.6 1.2 %copy-start.1 = (bf16[512,7,128]{2,0,1:T(8,128)(2,1)S(1)}, bf16[512,7,128]{2,0,1:T(8,128)(2,1)}, u32[]{:S(2)}) copy-start(bf16[512,7,128]{2,0,1:T(8,128)(2,1)} %param.6) | copy-start | bytes 2752516
  9.8 0.8 %copy-start.4 = (s32[1,4]{1,0:T(1,128)S(1)}, s32[1,4]{1,0:T(1,128)}, u32[]{:S(2)}) copy-start(s32[1,4]{1,0:T(1,128)} %param.11) | copy-start | bytes 52
  9.8 0.8 %copy-start.5 = (s32[1,8]{1,0:T(1,128)S(1)}, s32[1,8]{1,0:T(1,128)}, u32[]{:S(2)}) copy-start(s32[1,8]{1,0:T(1,128)} %param.10) | copy-start | bytes 100
  36.5 1.9 %collective-permute-start.3 = (bf16[256,896]{1,0:T(8,128)(2,1)S(1)}, bf16[256,896]{1,0:T(8,128)(2,1)S(1)}, u32[]{:S(2)}, u32[]{:S(2)}) collective-permute-start(bf16[256,896]{1,0:T(8,128)(2,1)S(1)} %get-tuple-element.28), channel_id=1, source_target_pairs={{0,1},{1,0},{2,3},{3,2},{4,5},{5,4},{6,7},{7,6},{8,9},{9,8},{10,11... | collective-permute-start | bytes 1376264 | tf_op jit(solution)/shard_map/ppermute | solution.py:28
  36.5 4.4 %collective-permute-start.6 = (bf16[256,896]{1,0:T(8,128)(2,1)S(1)}, bf16[256,896]{1,0:T(8,128)(2,1)S(1)}, u32[]{:S(2)}, u32[]{:S(2)}) collective-permute-start(bf16[256,896]{1,0:T(8,128)(2,1)S(1)} %get-tuple-element.32), channel_id=1, source_target_pairs={{0,1},{1,0},{2,3},{3,2},{4,5},{5,4},{6,7},{7,6},{8,9},{9,8},{10,11... | collective-permute-start | bytes 1376264 | tf_op jit(solution)/shard_map/ppermute | solution.py:28
  40.7 13.8 %collective-permute-start.4 = (bf16[512,896]{1,0:T(8,128)(2,1)S(1)}, bf16[512,896]{1,0:T(8,128)(2,1)S(1)}, u32[]{:S(2)}, u32[]{:S(2)}) collective-permute-start(bf16[512,896]{1,0:T(8,128)(2,1)S(1)} %get-tuple-element.30), channel_id=1, source_target_pairs={{0,1},{1,0},{2,3},{3,2},{4,5},{5,4},{6,7},{7,6},{8,9},{9,8},{10,11... | collective-permute-start | bytes 2752520 | tf_op jit(solution)/shard_map/ppermute | solution.py:28
  41.1 13.4 %collective-permute-start.7 = (bf16[256,896]{1,0:T(8,128)(2,1)S(1)}, bf16[256,896]{1,0:T(8,128)(2,1)S(1)}, u32[]{:S(2)}, u32[]{:S(2)}) collective-permute-start(bf16[256,896]{1,0:T(8,128)(2,1)S(1)} %add.7), channel_id=1, source_target_pairs={{0,2},{1,3},{2,0},{3,1},{4,6},{5,7},{6,4},{7,5},{8,10},{9,11},{10,... | collective-permute-start | bytes 1376264 | tf_op jit(solution)/shard_map/ppermute | solution.py:28
  42.7 21.1 %collective-permute-start.5 = (bf16[256,896]{1,0:T(8,128)(2,1)S(1)}, bf16[256,896]{1,0:T(8,128)(2,1)S(1)}, u32[]{:S(2)}, u32[]{:S(2)}) collective-permute-start(bf16[256,896]{1,0:T(8,128)(2,1)S(1)} %add.6.after), channel_id=1, source_target_pairs={{0,2},{1,3},{2,0},{3,1},{4,6},{5,7},{6,4},{7,5},{8,10},{9,11},{10,... | collective-permute-start | bytes 1376264 | tf_op jit(solution)/shard_map/ppermute | solution.py:28

commit v3 on v2

--- a/solution.py
+++ b/solution.py
@@ -26,25 +26,6 @@
 def swapped(value, flip):
     count = lax.axis_size("heads")
     return lax.ppermute(value, "heads", [(source, source ^ flip) for source in range(count)])
-
-
-def pack_body(keys, values, whole):
-    head = keys.shape[1]
-    whole[:, :head] = keys[...]
-    whole[:, head:] = values[...]
-
-
-def pack(keys, values):
-    rows, head = keys.shape
-    return pl.pallas_call(
-        pack_body,
-        out_shape=jax.ShapeDtypeStruct((rows, 2 * head), keys.dtype),
-        in_specs=[VMEM, VMEM],
-        out_specs=VMEM,
-        compiler_params=pltpu.CompilerParams(vmem_limit_bytes=VMEM_LIMIT),
-        cost_estimate=COST,
-        name="pack",
-    )(keys, values)
 
 
 def attend_block(cfg, info, q_ref, win, tiles, gathered, local, store):
@@ -124,15 +105,17 @@
         gathered[slot, :, 2 * head :] = jnp.ones((gathered.shape[1], head), jnp.bfloat16)
 
 
-def early_body(cfg, first, n_pieces, info, q_ref, w_send, *refs):
+def early_body(cfg, first, strides, info, q_ref, w_send, *refs):
     head = cfg[-1]
+    n_pieces = len(strides)
     pieces = refs[:n_pieces]
     tiles = refs[n_pieces] if len(refs) > n_pieces + 5 else None
     attended, send, win, gathered, sems = refs[-5:]
     rows = pieces[0].shape[0]
     copies = []
     for index, piece in enumerate(pieces):
-        copies.append(pltpu.make_async_copy(piece, win.at[index * rows : (index + 1) * rows, :], sems.at[index]))
+        at = (BAND - strides[index]) * rows
+        copies.append(pltpu.make_async_copy(piece, win.at[at : at + rows, :], sems.at[index]))
     for copy in copies:
         copy.start()
     fill_ones(gathered, head)
@@ -157,10 +140,10 @@
     return jax.ShapeDtypeStruct((count, like), jnp.bfloat16)
 
 
-def kernel_params(tiles):
+def kernel_params(tiles, rows):
     return dict(
         compiler_params=pltpu.CompilerParams(vmem_limit_bytes=4 * VMEM_LIMIT if tiles else VMEM_LIMIT),
-        cost_estimate=COST,
+        cost_estimate=pl.CostEstimate(flops=8_000_000 * rows, bytes_accessed=6_000_000, transcendentals=6000 * rows),
     )
 
 
@@ -168,17 +151,17 @@
     return pltpu.VMEM((2, (cfg[0] + cfg[1]) * BLOCK, 3 * cfg[-1]), jnp.bfloat16)
 
 
-def attend_early(cfg, first, info, q, w_send, pieces, tiles):
+def attend_early(cfg, first, info, q, w_send, pieces, strides, tiles):
     slash, n_vert, blocks, heads_here, head = cfg
     rows = (blocks - first) * BLOCK
     return pl.pallas_call(
-        functools.partial(early_body, cfg, first, len(pieces)),
+        functools.partial(early_body, cfg, first, strides),
         out_shape=[rows_of(rows, heads_here * head), rows_of(rows, w_send.shape[1]), rows_of((BAND + 1) * blocks * BLOCK, 2 * head)],
         in_specs=[SMEM, VMEM, VMEM] + [HBM] * len(pieces) + [VMEM] * len(tiles),
         out_specs=[VMEM] * 3,
         scratch_shapes=[gather_scratch(cfg), pltpu.SemaphoreType.DMA((len(pieces),))],
         name="attend_early",
-        **kernel_params(tiles),
+        **kernel_params(tiles, rows),
     )(info, q, w_send, *pieces, *tiles)
 
 
@@ -193,7 +176,7 @@
         out_specs=[VMEM] * 4,
         scratch_shapes=[gather_scratch(cfg)],
         name="attend_late",
-        **kernel_params(tiles),
+        **kernel_params(tiles, rows),
     )(info, q, w_send, w_keep, win, early, *tiles)
 
 
@@ -224,50 +207,70 @@
     )(q, weight, first)
 
 
-def project_body(late, early, w_send, w_keep, after, send, keep):
-    rows = late.shape[0]
-    for at, source in ((slice(0, rows), late), (slice(rows, send.shape[0]), early)):
-        matmul(source, w_send, send.at[at, :])
-        matmul(source, w_keep, keep.at[at, :])
-
-
-def project(late, early, w_send, w_keep, after):
-    rows = late.shape[0] + early.shape[0]
-    return pl.pallas_call(
-        project_body,
-        out_shape=[rows_of(rows, w_send.shape[1])] * 2,
-        in_specs=[VMEM] * 4 + [HBM],
-        out_specs=[VMEM] * 2,
+def join_body(keep_late, core_late, keep_early, core_early, mine):
+    rows = keep_late.shape[0]
+    for at, one, two in ((0, keep_late, core_late), (rows, keep_early, core_early)):
+        total = one[...].astype(jnp.float32) + two[...].astype(jnp.float32)
+        mine[at : at + one.shape[0], :] = total.astype(mine.dtype)
+
+
+def join(keep_late, core_late, keep_early, core_early):
+    return pl.pallas_call(
+        join_body,
+        out_shape=rows_of(keep_late.shape[0] + keep_early.shape[0], keep_late.shape[1]),
+        in_specs=[VMEM] * 4,
+        out_specs=VMEM,
         compiler_params=pltpu.CompilerParams(vmem_limit_bytes=VMEM_LIMIT),
         cost_estimate=COST,
+        name="join",
+    )(keep_late, core_late, keep_early, core_early)
+
+
+def project_body(late, early, w_send, w_keep, after, send_late, send_early, keep_late, keep_early):
+    matmul(late, w_send, send_late)
+    matmul(early, w_send, send_early)
+    matmul(late, w_keep, keep_late)
+    matmul(early, w_keep, keep_early)
+
+
+def project(late, early, w_send, w_keep, after):
+    shapes = [rows_of(late.shape[0], w_send.shape[1]), rows_of(early.shape[0], w_send.shape[1])]
+    rows = late.shape[0] + early.shape[0]
+    return pl.pallas_call(
+        project_body,
+        out_shape=shapes + shapes,
+        in_specs=[VMEM] * 4 + [HBM],
+        out_specs=[VMEM] * 4,
+        compiler_params=pltpu.CompilerParams(vmem_limit_bytes=VMEM_LIMIT),
+        cost_estimate=pl.CostEstimate(flops=3_300_000 * rows, bytes_accessed=6_000_000, transcendentals=0),
         name="project",
     )(late, early, w_send, w_keep, after)
 
 
-def finish_body(at, near, other, across, *refs):
-    out, total, sem = refs[-3:]
-    rows = total.shape[0]
-    where = slice(at, at + rows)
-    value = near[where, :].astype(jnp.float32) + other[where, :].astype(jnp.float32) + across[...].astype(jnp.float32)
-    total[...] = value.astype(total.dtype)
-    copy = pltpu.make_async_copy(total, out.at[where, :], sem)
-    copy.start()
-    copy.wait()
-
-
-def finish(near, other, across, at, before=None):
-    held = [] if before is None else [before]
-    return pl.pallas_call(
-        functools.partial(finish_body, at),
-        out_shape=rows_of(*near.shape),
-        in_specs=[VMEM] * 3 + [HBM] * len(held),
+def finish_body(keep_late, keep_early, core_late, core_early, across, out, total, sems):
+    rows = keep_late.shape[0]
+    copies = []
+    for index, (at, one, two) in enumerate(((0, keep_late, core_late), (rows, keep_early, core_early))):
+        where = slice(at, at + one.shape[0])
+        value = one[...].astype(jnp.float32) + two[...].astype(jnp.float32) + across[where, :].astype(jnp.float32)
+        total[where, :] = value.astype(total.dtype)
+        copies.append(pltpu.make_async_copy(total.at[where, :], out.at[where, :], sems.at[index]))
+        copies[-1].start()
+    for copy in copies:
+        copy.wait()
+
+
+def finish(keep_late, keep_early, core_late, core_early, across):
+    return pl.pallas_call(
+        finish_body,
+        out_shape=rows_of(*across.shape),
+        in_specs=[VMEM] * 5,
         out_specs=HBM,
-        scratch_shapes=[pltpu.VMEM(across.shape, across.dtype), pltpu.SemaphoreType.DMA],
-        input_output_aliases={3: 0} if held else {},
+        scratch_shapes=[pltpu.VMEM(across.shape, across.dtype), pltpu.SemaphoreType.DMA((2,))],
         compiler_params=pltpu.CompilerParams(vmem_limit_bytes=VMEM_LIMIT),
         cost_estimate=COST,
         name="finish",
-    )(near, other, across, *held)
+    )(keep_late, keep_early, core_late, core_early, across)
 
 
 def on_device(queries, key_states, value_states, out_weight, slash_offsets, vertical_blocks):
@@ -277,9 +280,13 @@
     ctx_count = lax.axis_size("ctx")
     cfg = (slash_offsets.shape[1], ctx_count, blocks, per_group, head)
 
-    whole = pack(key_states[:, 0, :], value_states[:, 0, :])
-    pieces = [shifted(whole, "ctx", stride) for stride in range(BAND, 0, -1)] + [whole]
+    strides = (1, 3, 2)
+    whole = jnp.concatenate([key_states[:, 0, :], value_states[:, 0, :]], axis=1)
+    one = shifted(whole, "ctx", 1)
+    three = shifted(whole, "ctx", 3)
     q, w_far_send, w_far_keep, w_near_send, w_near_keep = stage(queries.transpose(1, 0, 2), out_weight, whole)
+    one, q = lax.optimization_barrier((one, q))
+    pieces = [whole, one, three, shifted(one, "ctx", 1)]
     tiles = []
     if ctx_count > BAND + 1:
         start = lax.dynamic_index_in_dim(vertical_blocks[0], lax.axis_index("ctx"), 0, keepdims=False) * BLOCK
@@ -287,17 +294,14 @@
         tiles.append(lax.all_gather(tile, "ctx", axis=0, tiled=True))
     info = jnp.concatenate([slash_offsets[0], vertical_blocks[0]])
 
-    early, send, win = attend_early(cfg, late_blocks, info, q, w_far_send, pieces, tiles)
+    early, send, win = attend_early(cfg, late_blocks, info, q, w_far_send, pieces, (0,) + strides, tiles)
     core_early = swapped(send, 1)
     late, send, keep_late, keep_early = attend_late(cfg, late_blocks, info, q, w_far_send, w_far_keep, win, early, tiles)
     core_late = swapped(send, 1)
-    across_early = swapped(keep_early + core_early, 2)
-    mine_late = keep_late + core_late
-    across_late = swapped(mine_late, 2)
-    near_send, near_keep = project(late, early, w_near_send, w_near_keep, mine_late)
-    core_near = swapped(near_send, 1)
-    out = finish(near_keep, core_near, across_early, late_blocks * BLOCK)
-    return finish(near_keep, core_near, across_late, 0, out)
+    mine = join(keep_late, core_late, keep_early, core_early)
+    across = swapped(mine, 2)
+    send_late, send_early, keep_late, keep_early = project(late, early, w_near_send, w_near_keep, mine)
+    return finish(keep_late, keep_early, swapped(send_late, 1), swapped(send_early, 1), across)
 
 
 def solution(mesh):

time: 65 us -> 58.4 us (0.90)
  waiting for transfers between devices: 38.8 us -> 34.1 us
  local copies, waits for them, and re-layouts: 5.81 us -> 4 us
  other arithmetic: 0.32 us -> 1.07 us
    ppermute x3, waiting for transfers between devices: 17.9 us -> 14 us  [shifted(): lax.ppermute(value, axis, [(source, source + steps) for source in range(c...]
    unnamed x12 -> x8, local copies, waits for them, and re-layouts: 5.81 us -> 4 us
    concatenate x0 -> x1, other arithmetic: none -> 1 us  [on_device(): jnp.concatenate([key_states[:, 0, :], value_states[:, 0, :]], axis=1)]
    ppermute x5, waiting for transfers between devices: 20.9 us -> 20 us  [swapped(): lax.ppermute(value, 'heads', [(source, source ^ flip) for source in range...]
    pallas_call x5 -> x4, Pallas kernels: 7.69 us -> 7.09 us  [the longest x1 3.49 us: attend_early(): pl.pallas_call(functools.partial(early_body, cfg, first, strides), out_sh...]
  transfers between devices with their start and end apart: 8 -> 8, of which waited for: 5 -> 8; matrix products, arithmetic and copies ran while one was open for 0% -> 0% of each run, Pallas kernels for 6% -> 5%
where the time goes in v3:
time: 58.4 us; the launch traced here: 58.1 us
  waiting for transfers between devices  34.1 us (58%)
  Pallas kernels  12.3 us (21%)
  starting transfers between devices  6.56 us (11%)
  local copies, waits for them, and re-layouts  4 us (7%)
  other arithmetic  1.07 us (2%)
    ppermute x5, waiting for transfers between devices, swapped(): lax.ppermute(value, 'heads', [(source, source ^ flip) for source in range...  20 us
    ppermute x3, waiting for transfers between devices, shifted(): lax.ppermute(value, axis, [(source, source + steps) for source in range(c...  14 us
    pallas_call x1, Pallas kernels, attend_late(): pl.pallas_call(functools.partial(late_body, cfg), out_shape=[rows_of(rows...  4.43 us
    unnamed x8, local copies, waits for them, and re-layouts  4 us
    ppermute x3, starting transfers between devices, shifted(): lax.ppermute(value, axis, [(source, source + steps) for source in range(c...  3.86 us
    pallas_call x1, Pallas kernels, attend_early(): pl.pallas_call(functools.partial(early_body, cfg, first, strides), out_sh...  3.49 us
    ppermute x5, starting transfers between devices, swapped(): lax.ppermute(value, 'heads', [(source, source ^ flip) for source in range...  2.69 us
    pallas_call x1, Pallas kernels, project(): pl.pallas_call(project_body, out_shape=shapes + shapes, in_specs=[VMEM] *...  2.27 us
  transfers between devices with their start and end apart: 8, of which 8 were waited for; matrix products, arithmetic and copies ran while one was open for 0% of the time, Pallas kernels for 5%

profile of v3, /device:TPU:28, one launch (start us, length us, event | category | flops | bytes accessed | tf_op | source)
XLA Modules:
  0.0 58.1 jit_solution(9965983738760375907)
XLA Ops:
  0.0 1.0 %pad_maximum_fusion.first.refs_0_ = bf16[512,256]{1,0:T(8,128)(2,1)S(1)} fusion(bf16[512,128]{1,0:T(8,128)(2,1)} %bitcast.6, bf16[512,128]{1,0:T(8,128)(2,1)} %bitcast.7), kind=kLoop, calls=%fused_computation | loop fusion | flops 524288 | bytes 524288 | tf_op jit(solution)/shard_map/concatenate | solution.py:284
  1.0 1.3 %collective-permute-start = (bf16[512,256]{1,0:T(8,128)(2,1)S(1)}, bf16[512,256]{1,0:T(8,128)(2,1)S(1)}, u32[]{:S(2)}, u32[]{:S(2)}) collective-permute-start(bf16[512,256]{1,0:T(8,128)(2,1)S(1)} %pad_maximum_fusion.first.refs_0_), channel_id=1, source_target_pairs={{0,4},{4,8},{8,12},{1,5},{5,9},{9,13},{2,6},{6,10},{10,14},{3,7},{... | collective-permute-start | bytes 786440 | tf_op jit(solution)/shard_map/ppermute | solution.py:23
  2.3 1.3 %collective-permute-start.1 = (bf16[512,256]{1,0:T(8,128)(2,1)S(1)}, bf16[512,256]{1,0:T(8,128)(2,1)S(1)}, u32[]{:S(2)}, u32[]{:S(2)}) collective-permute-start(bf16[512,256]{1,0:T(8,128)(2,1)S(1)} %pad_maximum_fusion.first.refs_0_), channel_id=1, source_target_pairs={{0,12},{1,13},{2,14},{3,15},{16,28},{17,29},{18,30},{19,31}} | collective-permute-start | bytes 786440 | tf_op jit(solution)/shard_map/ppermute | solution.py:23
  3.6 2.8 %copy-done = bf16[896,3584]{1,0:T(8,128)(2,1)S(1)} copy-done((bf16[896,3584]{1,0:T(8,128)(2,1)S(1)}, bf16[896,3584]{1,0:T(8,128)(2,1)}, u32[]{:S(2)}) %copy-start) | copy-done | bytes 6422552
  6.4 1.2 %copy-done.1 = bf16[512,7,128]{2,0,1:T(8,128)(2,1)S(1)} copy-done((bf16[512,7,128]{2,0,1:T(8,128)(2,1)S(1)}, bf16[512,7,128]{2,0,1:T(8,128)(2,1)}, u32[]{:S(2)}) %copy-start.1) | copy-done | bytes 917528
  7.6 0.8 %stage.1 = (bf16[7,512,128]{2,1,0:T(8,128)(2,1)S(1)}, bf16[896,896]{1,0:T(8,128)(2,1)S(1)}, bf16[896,896]{1,0:T(8,128)(2,1)S(1)}, bf16[896,896]{1,0:T(8,128)(2,1)S(1)}, bf16[896,896]{1,0:T(8,128)(2,1)S(1)}) custom-call(bf16[7,512,128]{2,1,0:T(8,128)(2,1)S(1)} %bitcast.5, bf16[896,3584]{1,0:T(8,128)(2,1)S(1)} %copy-done, ...), custom_call_target="tpu_custom_call" | custom-call | flops 1 | bytes 1 | tf_op jit(solution)/shard_map/stage/pallas_call | solution.py:198
  8.4 7.2 %collective-permute-done.refs_1_ = bf16[512,256]{1,0:T(8,128)(2,1)S(1)} collective-permute-done((bf16[512,256]{1,0:T(8,128)(2,1)S(1)}, bf16[512,256]{1,0:T(8,128)(2,1)S(1)}, u32[]{:S(2)}, u32[]{:S(2)}) %collective-permute-start) | collective-permute-done | bytes 262176 | tf_op jit(solution)/shard_map/ppermute | solution.py:23
  15.6 1.3 %collective-permute-start.2 = (bf16[512,256]{1,0:T(8,128)(2,1)S(1)}, bf16[512,256]{1,0:T(8,128)(2,1)S(1)}, u32[]{:S(2)}, u32[]{:S(2)}) collective-permute-start(bf16[512,256]{1,0:T(8,128)(2,1)S(1)} %collective-permute-done.refs_1_), channel_id=1, source_target_pairs={{0,4},{4,8},{8,12},{1,5},{5,9},{9,13},{2,6},{6,10},{10,14},{3,7},{... | collective-permute-start | bytes 786440 | tf_op jit(solution)/shard_map/ppermute | solution.py:23
  16.9 0.1 pad_add_fusion.info
  17.0 0.6 collective-permute-done.1.refs_2_
  17.5 6.3 %collective-permute-done.2.refs_3_ = bf16[512,256]{1,0:T(8,128)(2,1)S(1)} collective-permute-done((bf16[512,256]{1,0:T(8,128)(2,1)S(1)}, bf16[512,256]{1,0:T(8,128)(2,1)S(1)}, u32[]{:S(2)}, u32[]{:S(2)}) %collective-permute-start.2) | collective-permute-done | bytes 262176 | tf_op jit(solution)/shard_map/ppermute | solution.py:23
  23.8 3.5 %attend_early.1 = (bf16[256,896]{1,0:T(8,128)(2,1)S(1)}, bf16[256,896]{1,0:T(8,128)(2,1)S(1)}, bf16[2048,256]{1,0:T(8,128)(2,1)S(1)}) custom-call(s32[12]{0:T(128)S(1)} %pad_add_fusion.info, bf16[7,512,128]{2,1,0:T(8,128)(2,1)S(1)} %get-tuple-element.24.q_ref, bf16[896,896]{1,0:T(8,128)(2,1)S(1)} %get-tuple-element.25.w_send, ...), custom_call_target="tpu_custom_call" | custom-call | flops 2048000000 | bytes 6000000 | tf_op jit(solution)/shard_map/attend_early/pallas_call | solution.py:157
  27.3 4.4 %attend_late.1 = (bf16[256,896]{1,0:T(8,128)(2,1)S(1)}, bf16[256,896]{1,0:T(8,128)(2,1)S(1)}, bf16[256,896]{1,0:T(8,128)(2,1)S(1)}, bf16[256,896]{1,0:T(8,128)(2,1)S(1)}) custom-call(s32[12]{0:T(128)S(1)} %pad_add_fusion.info, bf16[7,512,128]{2,1,0:T(8,128)(2,1)S(1)} %get-tuple-element.24.q_ref, bf16[896,896]{1,0:T(8,128)(2,1)S(1)} %get-tuple-element.25.w_send, ...), custom_call_target="tpu_custom_call" | custom-call | flops 2048000000 | bytes 6000000 | tf_op jit(solution)/shard_map/attend_late/pallas_call | solution.py:172
  31.9 0.5 collective-permute-start.4
  32.4 1.3 %collective-permute-done.3.core_late = bf16[256,896]{1,0:T(8,128)(2,1)S(1)} collective-permute-done((bf16[256,896]{1,0:T(8,128)(2,1)S(1)}, bf16[256,896]{1,0:T(8,128)(2,1)S(1)}, u32[]{:S(2)}, u32[]{:S(2)}) %collective-permute-start.3) | collective-permute-done | bytes 458784 | tf_op jit(solution)/shard_map/ppermute | solution.py:28
  33.7 0.7 %collective-permute-done.4.core_early = bf16[256,896]{1,0:T(8,128)(2,1)S(1)} collective-permute-done((bf16[256,896]{1,0:T(8,128)(2,1)S(1)}, bf16[256,896]{1,0:T(8,128)(2,1)S(1)}, u32[]{:S(2)}, u32[]{:S(2)}) %collective-permute-start.4) | collective-permute-done | bytes 458784 | tf_op jit(solution)/shard_map/ppermute | solution.py:28
  34.3 0.2 join.1.after
  34.5 1.6 %collective-permute-start.7 = (bf16[512,896]{1,0:T(8,128)(2,1)S(1)}, bf16[512,896]{1,0:T(8,128)(2,1)S(1)}, u32[]{:S(2)}, u32[]{:S(2)}) collective-permute-start(bf16[512,896]{1,0:T(8,128)(2,1)S(1)} %join.1.after), channel_id=1, source_target_pairs={{0,2},{1,3},{2,0},{3,1},{4,6},{5,7},{6,4},{7,5},{8,10},{9,11},{10,... | collective-permute-start | bytes 2752520 | tf_op jit(solution)/shard_map/ppermute | solution.py:28
  36.1 2.3 %project.1 = (bf16[256,896]{1,0:T(8,128)(2,1)S(1)}, bf16[256,896]{1,0:T(8,128)(2,1)S(1)}, bf16[256,896]{1,0:T(8,128)(2,1)S(1)}, bf16[256,896]{1,0:T(8,128)(2,1)S(1)}) custom-call(bf16[256,896]{1,0:T(8,128)(2,1)S(1)} %get-tuple-element.30.late, bf16[256,896]{1,0:T(8,128)(2,1)S(1)} %get-tuple-element.29.early, bf16[896,896]{1,0:T(8,128)(2,1)S(1)} %get-tuple-element.31.w_send, ...), custom_call_target="tpu_custom_call" | custom-call | flops 1689600000 | bytes 6000000 | tf_op jit(solution)/shard_map/project/pallas_call | solution.py:239
  38.5 0.5 collective-permute-start.6
  38.9 1.3 %collective-permute-done.5.core_late = bf16[256,896]{1,0:T(8,128)(2,1)S(1)} collective-permute-done((bf16[256,896]{1,0:T(8,128)(2,1)S(1)}, bf16[256,896]{1,0:T(8,128)(2,1)S(1)}, u32[]{:S(2)}, u32[]{:S(2)}) %collective-permute-start.5) | collective-permute-done | bytes 458784 | tf_op jit(solution)/shard_map/ppermute | solution.py:28
  40.3 0.7 %collective-permute-done.6.core_early = bf16[256,896]{1,0:T(8,128)(2,1)S(1)} collective-permute-done((bf16[256,896]{1,0:T(8,128)(2,1)S(1)}, bf16[256,896]{1,0:T(8,128)(2,1)S(1)}, u32[]{:S(2)}, u32[]{:S(2)}) %collective-permute-start.6) | collective-permute-done | bytes 458784 | tf_op jit(solution)/shard_map/ppermute | solution.py:28
  40.9 16.1 %collective-permute-done.7.across = bf16[512,896]{1,0:T(8,128)(2,1)S(1)} collective-permute-done((bf16[512,896]{1,0:T(8,128)(2,1)S(1)}, bf16[512,896]{1,0:T(8,128)(2,1)S(1)}, u32[]{:S(2)}, u32[]{:S(2)}) %collective-permute-start.7) | collective-permute-done | bytes 917536 | tf_op jit(solution)/shard_map/ppermute | solution.py:28
  57.0 1.1 %finish.1 = bf16[512,896]{1,0:T(8,128)(2,1)} custom-call(bf16[256,896]{1,0:T(8,128)(2,1)S(1)} %get-tuple-element.37.keep_late, bf16[256,896]{1,0:T(8,128)(2,1)S(1)} %get-tuple-element.38.keep_early, bf16[256,896]{1,0:T(8,128)(2,1)S(1)} %collective-permute-done.5.core_late, bf16[256,896]{1,0:T(8,128)(2,1)S(1)} %collective-permute-done.6.core_early, ...), custom_call_target="tpu_custom_call" | custom-call | flops 1 | bytes 1 | tf_op jit(solution)/shard_map/finish/pallas_call | solution.py:264
  (8 shorter events, 0.2 us)
Async XLA Ops:
  1.0 14.6 %collective-permute-start = (bf16[512,256]{1,0:T(8,128)(2,1)S(1)}, bf16[512,256]{1,0:T(8,128)(2,1)S(1)}, u32[]{:S(2)}, u32[]{:S(2)}) collective-permute-start(bf16[512,256]{1,0:T(8,128)(2,1)S(1)} %pad_maximum_fusion.first.refs_0_), channel_id=1, source_target_pairs={{0,4},{4,8},{8,12},{1,5},{5,9},{9,13},{2,6},{6,10},{10,14},{3,7},{... | collective-permute-start | bytes 786440 | tf_op jit(solution)/shard_map/ppermute | solution.py:23
  2.3 15.2 %collective-permute-start.1 = (bf16[512,256]{1,0:T(8,128)(2,1)S(1)}, bf16[512,256]{1,0:T(8,128)(2,1)S(1)}, u32[]{:S(2)}, u32[]{:S(2)}) collective-permute-start(bf16[512,256]{1,0:T(8,128)(2,1)S(1)} %pad_maximum_fusion.first.refs_0_), channel_id=1, source_target_pairs={{0,12},{1,13},{2,14},{3,15},{16,28},{17,29},{18,30},{19,31}} | collective-permute-start | bytes 786440 | tf_op jit(solution)/shard_map/ppermute | solution.py:23
  3.6 2.8 %copy-start = (bf16[896,3584]{1,0:T(8,128)(2,1)S(1)}, bf16[896,3584]{1,0:T(8,128)(2,1)}, u32[]{:S(2)}) copy-start(bf16[896,3584]{1,0:T(8,128)(2,1)} %weight.1) | copy-start | bytes 19267588
  6.4 1.2 %copy-start.1 = (bf16[512,7,128]{2,0,1:T(8,128)(2,1)S(1)}, bf16[512,7,128]{2,0,1:T(8,128)(2,1)}, u32[]{:S(2)}) copy-start(bf16[512,7,128]{2,0,1:T(8,128)(2,1)} %param.6) | copy-start | bytes 2752516
  7.6 9.3 %copy-start.2 = (s32[1,4]{1,0:T(1,128)S(1)}, s32[1,4]{1,0:T(1,128)}, u32[]{:S(2)}) copy-start(s32[1,4]{1,0:T(1,128)} %param.11) | copy-start | bytes 52
  7.6 9.3 %copy-start.3 = (s32[1,8]{1,0:T(1,128)S(1)}, s32[1,8]{1,0:T(1,128)}, u32[]{:S(2)}) copy-start(s32[1,8]{1,0:T(1,128)} %param.10) | copy-start | bytes 100
  15.6 8.3 %collective-permute-start.2 = (bf16[512,256]{1,0:T(8,128)(2,1)S(1)}, bf16[512,256]{1,0:T(8,128)(2,1)S(1)}, u32[]{:S(2)}, u32[]{:S(2)}) collective-permute-start(bf16[512,256]{1,0:T(8,128)(2,1)S(1)} %collective-permute-done.refs_1_), channel_id=1, source_target_pairs={{0,4},{4,8},{8,12},{1,5},{5,9},{9,13},{2,6},{6,10},{10,14},{3,7},{... | collective-permute-start | bytes 786440 | tf_op jit(solution)/shard_map/ppermute | solution.py:23
  31.8 1.9 %collective-permute-start.3 = (bf16[256,896]{1,0:T(8,128)(2,1)S(1)}, bf16[256,896]{1,0:T(8,128)(2,1)S(1)}, u32[]{:S(2)}, u32[]{:S(2)}) collective-permute-start(bf16[256,896]{1,0:T(8,128)(2,1)S(1)} %get-tuple-element.34), channel_id=1, source_target_pairs={{0,1},{1,0},{2,3},{3,2},{4,5},{5,4},{6,7},{7,6},{8,9},{9,8},{10,11... | collective-permute-start | bytes 1376264 | tf_op jit(solution)/shard_map/ppermute | solution.py:28
  31.9 2.5 %collective-permute-start.4 = (bf16[256,896]{1,0:T(8,128)(2,1)S(1)}, bf16[256,896]{1,0:T(8,128)(2,1)S(1)}, u32[]{:S(2)}, u32[]{:S(2)}) collective-permute-start(bf16[256,896]{1,0:T(8,128)(2,1)S(1)} %get-tuple-element.36), channel_id=1, source_target_pairs={{0,1},{1,0},{2,3},{3,2},{4,5},{5,4},{6,7},{7,6},{8,9},{9,8},{10,11... | collective-permute-start | bytes 1376264 | tf_op jit(solution)/shard_map/ppermute | solution.py:28
  34.5 22.5 %collective-permute-start.7 = (bf16[512,896]{1,0:T(8,128)(2,1)S(1)}, bf16[512,896]{1,0:T(8,128)(2,1)S(1)}, u32[]{:S(2)}, u32[]{:S(2)}) collective-permute-start(bf16[512,896]{1,0:T(8,128)(2,1)S(1)} %join.1.after), channel_id=1, source_target_pairs={{0,2},{1,3},{2,0},{3,1},{4,6},{5,7},{6,4},{7,5},{8,10},{9,11},{10,... | collective-permute-start | bytes 2752520 | tf_op jit(solution)/shard_map/ppermute | solution.py:28
  38.4 1.9 %collective-permute-start.5 = (bf16[256,896]{1,0:T(8,128)(2,1)S(1)}, bf16[256,896]{1,0:T(8,128)(2,1)S(1)}, u32[]{:S(2)}, u32[]{:S(2)}) collective-permute-start(bf16[256,896]{1,0:T(8,128)(2,1)S(1)} %get-tuple-element.39), channel_id=1, source_target_pairs={{0,1},{1,0},{2,3},{3,2},{4,5},{5,4},{6,7},{7,6},{8,9},{9,8},{10,11... | collective-permute-start | bytes 1376264 | tf_op jit(solution)/shard_map/ppermute | solution.py:28
  38.5 2.5 %collective-permute-start.6 = (bf16[256,896]{1,0:T(8,128)(2,1)S(1)}, bf16[256,896]{1,0:T(8,128)(2,1)S(1)}, u32[]{:S(2)}, u32[]{:S(2)}) collective-permute-start(bf16[256,896]{1,0:T(8,128)(2,1)S(1)} %get-tuple-element.40), channel_id=1, source_target_pairs={{0,1},{1,0},{2,3},{3,2},{4,5},{5,4},{6,7},{7,6},{8,9},{9,8},{10,11... | collective-permute-start | bytes 1376264 | tf_op jit(solution)/shard_map/ppermute | solution.py:28

commit v4 on v3

--- a/solution.py
+++ b/solution.py
@@ -105,35 +105,53 @@
         gathered[slot, :, 2 * head :] = jnp.ones((gathered.shape[1], head), jnp.bfloat16)
 
 
-def early_body(cfg, first, strides, info, q_ref, w_send, *refs):
+def fill_body(strides, *refs):
+    win, sems = refs[-2:]
+    rows = refs[0].shape[0]
+    copies = []
+    for index, stride in enumerate(strides):
+        at = (BAND - stride) * rows
+        copies.append(pltpu.make_async_copy(refs[index], win.at[at : at + rows, :], sems.at[index]))
+    for copy in copies:
+        copy.start()
+    for copy in copies:
+        copy.wait()
+
+
+def fill(pieces, strides):
+    rows, width = pieces[0].shape
+    return pl.pallas_call(
+        functools.partial(fill_body, strides),
+        out_shape=rows_of((BAND + 1) * rows, width),
+        in_specs=[HBM] * len(pieces),
+        out_specs=VMEM,
+        scratch_shapes=[pltpu.SemaphoreType.DMA((len(pieces),))],
+        compiler_params=pltpu.CompilerParams(vmem_limit_bytes=VMEM_LIMIT),
+        cost_estimate=COST,
+        name="fill",
+    )(*pieces)
+
+
+def early_body(cfg, first, at, info, q_ref, w_send, held, piece, *refs):
     head = cfg[-1]
-    n_pieces = len(strides)
-    pieces = refs[:n_pieces]
-    tiles = refs[n_pieces] if len(refs) > n_pieces + 5 else None
-    attended, send, win, gathered, sems = refs[-5:]
-    rows = pieces[0].shape[0]
-    copies = []
-    for index, piece in enumerate(pieces):
-        at = (BAND - strides[index]) * rows
-        copies.append(pltpu.make_async_copy(piece, win.at[at : at + rows, :], sems.at[index]))
-    for copy in copies:
-        copy.start()
+    tiles = refs[0] if len(refs) > 5 else None
+    attended, send, win, gathered, sem = refs[-5:]
+    copy = pltpu.make_async_copy(piece, win.at[at : at + piece.shape[0], :], sem)
+    copy.start()
     fill_ones(gathered, head)
-    for copy in copies:
-        copy.wait()
+    copy.wait()
     attend_rows(cfg, info, q_ref, win, tiles, gathered, first, attended)
     matmul(attended, w_send, send)
 
 
-def late_body(cfg, info, q_ref, w_send, w_keep, win, early, *refs):
+def next_body(cfg, first, info, q_ref, w_send, w_keep, win, before, *refs):
     head = cfg[-1]
-    tiles = refs[0] if len(refs) > 5 else None
-    attended, send, keep, keep_early, gathered = refs[-5:]
+    tiles = refs[0] if len(refs) > 4 else None
+    attended, send, keep, gathered = refs[-4:]
     fill_ones(gathered, head)
-    attend_rows(cfg, info, q_ref, win, tiles, gathered, 0, attended)
+    attend_rows(cfg, info, q_ref, win, tiles, gathered, first, attended)
     matmul(attended, w_send, send)
-    matmul(early, w_keep, keep_early)
-    matmul(attended, w_keep, keep)
+    matmul(before, w_keep, keep)
 
 
 def rows_of(count, like):
@@ -151,33 +169,34 @@
     return pltpu.VMEM((2, (cfg[0] + cfg[1]) * BLOCK, 3 * cfg[-1]), jnp.bfloat16)
 
 
-def attend_early(cfg, first, info, q, w_send, pieces, strides, tiles):
+def attend_early(cfg, first, count, info, q, w_send, win, piece, stride, tiles):
     slash, n_vert, blocks, heads_here, head = cfg
-    rows = (blocks - first) * BLOCK
-    return pl.pallas_call(
-        functools.partial(early_body, cfg, first, strides),
-        out_shape=[rows_of(rows, heads_here * head), rows_of(rows, w_send.shape[1]), rows_of((BAND + 1) * blocks * BLOCK, 2 * head)],
-        in_specs=[SMEM, VMEM, VMEM] + [HBM] * len(pieces) + [VMEM] * len(tiles),
+    rows = count * BLOCK
+    return pl.pallas_call(
+        functools.partial(early_body, cfg, first, (BAND - stride) * piece.shape[0]),
+        out_shape=[rows_of(rows, heads_here * head), rows_of(rows, w_send.shape[1]), rows_of(*win.shape)],
+        in_specs=[SMEM] + [VMEM] * 3 + [HBM] + [VMEM] * len(tiles),
         out_specs=[VMEM] * 3,
-        scratch_shapes=[gather_scratch(cfg), pltpu.SemaphoreType.DMA((len(pieces),))],
+        scratch_shapes=[gather_scratch(cfg), pltpu.SemaphoreType.DMA],
+        input_output_aliases={3: 2},
         name="attend_early",
         **kernel_params(tiles, rows),
-    )(info, q, w_send, *pieces, *tiles)
-
-
-def attend_late(cfg, count, info, q, w_send, w_keep, win, early, tiles):
+    )(info, q, w_send, win, piece, *tiles)
+
+
+def attend_next(cfg, first, count, info, q, w_send, w_keep, win, before, tiles):
     slash, n_vert, blocks, heads_here, head = cfg
     rows = count * BLOCK
     width = w_send.shape[1]
     return pl.pallas_call(
-        functools.partial(late_body, cfg),
-        out_shape=[rows_of(rows, heads_here * head), rows_of(rows, width), rows_of(rows, width), rows_of(early.shape[0], width)],
+        functools.partial(next_body, cfg, first),
+        out_shape=[rows_of(rows, heads_here * head), rows_of(rows, width), rows_of(before.shape[0], width)],
         in_specs=[SMEM] + [VMEM] * (5 + len(tiles)),
-        out_specs=[VMEM] * 4,
+        out_specs=[VMEM] * 3,
         scratch_shapes=[gather_scratch(cfg)],
-        name="attend_late",
+        name="attend_next",
         **kernel_params(tiles, rows),
-    )(info, q, w_send, w_keep, win, early, *tiles)
+    )(info, q, w_send, w_keep, win, before, *tiles)
 
 
 def stage_body(queries, weight, first, q, *refs):
@@ -207,86 +226,72 @@
     )(q, weight, first)
 
 
-def join_body(keep_late, core_late, keep_early, core_early, mine):
-    rows = keep_late.shape[0]
-    for at, one, two in ((0, keep_late, core_late), (rows, keep_early, core_early)):
-        total = one[...].astype(jnp.float32) + two[...].astype(jnp.float32)
-        mine[at : at + one.shape[0], :] = total.astype(mine.dtype)
-
-
-def join(keep_late, core_late, keep_early, core_early):
-    return pl.pallas_call(
-        join_body,
-        out_shape=rows_of(keep_late.shape[0] + keep_early.shape[0], keep_late.shape[1]),
-        in_specs=[VMEM] * 4,
-        out_specs=VMEM,
+def project_body(count, *refs):
+    sources, weights, outs = refs[:count], refs[count:-count], refs[-count:]
+    for source, weight, out in zip(sources, weights, outs):
+        matmul(source, weight, out)
+
+
+def project(pairs):
+    count = len(pairs)
+    flops = sum(2 * source.shape[0] * weight.shape[0] * weight.shape[1] for source, weight in pairs)
+    return pl.pallas_call(
+        functools.partial(project_body, count),
+        out_shape=[rows_of(source.shape[0], weight.shape[1]) for source, weight in pairs],
+        in_specs=[VMEM] * (2 * count),
+        out_specs=[VMEM] * count,
         compiler_params=pltpu.CompilerParams(vmem_limit_bytes=VMEM_LIMIT),
-        cost_estimate=COST,
-        name="join",
-    )(keep_late, core_late, keep_early, core_early)
-
-
-def project_body(late, early, w_send, w_keep, after, send_late, send_early, keep_late, keep_early):
-    matmul(late, w_send, send_late)
-    matmul(early, w_send, send_early)
-    matmul(late, w_keep, keep_late)
-    matmul(early, w_keep, keep_early)
-
-
-def project(late, early, w_send, w_keep, after):
-    shapes = [rows_of(late.shape[0], w_send.shape[1]), rows_of(early.shape[0], w_send.shape[1])]
-    rows = late.shape[0] + early.shape[0]
-    return pl.pallas_call(
-        project_body,
-        out_shape=shapes + shapes,
-        in_specs=[VMEM] * 4 + [HBM],
-        out_specs=[VMEM] * 4,
-        compiler_params=pltpu.CompilerParams(vmem_limit_bytes=VMEM_LIMIT),
-        cost_estimate=pl.CostEstimate(flops=3_300_000 * rows, bytes_accessed=6_000_000, transcendentals=0),
+        cost_estimate=pl.CostEstimate(flops=flops, bytes_accessed=6_000_000, transcendentals=0),
         name="project",
-    )(late, early, w_send, w_keep, after)
-
-
-def finish_body(keep_late, keep_early, core_late, core_early, across, out, total, sems):
-    rows = keep_late.shape[0]
+    )(*[source for source, _ in pairs], *[weight for _, weight in pairs])
+
+
+def finish_body(count, *refs):
+    keeps, cores, acrosses = refs[:count], refs[count : 2 * count], refs[2 * count : 3 * count]
+    out, total, sems = refs[-3:]
     copies = []
-    for index, (at, one, two) in enumerate(((0, keep_late, core_late), (rows, keep_early, core_early))):
-        where = slice(at, at + one.shape[0])
-        value = one[...].astype(jnp.float32) + two[...].astype(jnp.float32) + across[where, :].astype(jnp.float32)
-        total[where, :] = value.astype(total.dtype)
+    end = out.shape[0]
+    for index in range(count):
+        where = slice(end - keeps[index].shape[0], end)
+        end = where.start
+        value = keeps[index][...].astype(jnp.float32) + cores[index][...].astype(jnp.float32)
+        total[where, :] = (value + acrosses[index][...].astype(jnp.float32)).astype(total.dtype)
         copies.append(pltpu.make_async_copy(total.at[where, :], out.at[where, :], sems.at[index]))
         copies[-1].start()
     for copy in copies:
         copy.wait()
 
 
-def finish(keep_late, keep_early, core_late, core_early, across):
-    return pl.pallas_call(
-        finish_body,
-        out_shape=rows_of(*across.shape),
-        in_specs=[VMEM] * 5,
+def finish(rows, keeps, cores, acrosses):
+    width = keeps[0].shape[1]
+    count = len(keeps)
+    return pl.pallas_call(
+        functools.partial(finish_body, count),
+        out_shape=rows_of(rows, width),
+        in_specs=[VMEM] * (3 * count),
         out_specs=HBM,
-        scratch_shapes=[pltpu.VMEM(across.shape, across.dtype), pltpu.SemaphoreType.DMA((2,))],
+        scratch_shapes=[pltpu.VMEM((rows, width), jnp.bfloat16), pltpu.SemaphoreType.DMA((count,))],
         compiler_params=pltpu.CompilerParams(vmem_limit_bytes=VMEM_LIMIT),
         cost_estimate=COST,
         name="finish",
-    )(keep_late, keep_early, core_late, core_early, across)
+    )(*keeps, *cores, *acrosses)
 
 
 def on_device(queries, key_states, value_states, out_weight, slash_offsets, vertical_blocks):
     rows_here, per_group, head = queries.shape
     blocks = rows_here // BLOCK
-    late_blocks = blocks // 2
+    shares = (3, 3, 2)
+    counts = [blocks * share // sum(shares) for share in shares]
     ctx_count = lax.axis_size("ctx")
     cfg = (slash_offsets.shape[1], ctx_count, blocks, per_group, head)
 
-    strides = (1, 3, 2)
     whole = jnp.concatenate([key_states[:, 0, :], value_states[:, 0, :]], axis=1)
     one = shifted(whole, "ctx", 1)
     three = shifted(whole, "ctx", 3)
     q, w_far_send, w_far_keep, w_near_send, w_near_keep = stage(queries.transpose(1, 0, 2), out_weight, whole)
     one, q = lax.optimization_barrier((one, q))
-    pieces = [whole, one, three, shifted(one, "ctx", 1)]
+    two = shifted(one, "ctx", 1)
+    win = fill([whole, one, three], (0, 1, BAND))
     tiles = []
     if ctx_count > BAND + 1:
         start = lax.dynamic_index_in_dim(vertical_blocks[0], lax.axis_index("ctx"), 0, keepdims=False) * BLOCK
@@ -294,14 +299,27 @@
         tiles.append(lax.all_gather(tile, "ctx", axis=0, tiled=True))
     info = jnp.concatenate([slash_offsets[0], vertical_blocks[0]])
 
-    early, send, win = attend_early(cfg, late_blocks, info, q, w_far_send, pieces, (0,) + strides, tiles)
-    core_early = swapped(send, 1)
-    late, send, keep_late, keep_early = attend_late(cfg, late_blocks, info, q, w_far_send, w_far_keep, win, early, tiles)
-    core_late = swapped(send, 1)
-    mine = join(keep_late, core_late, keep_early, core_early)
-    across = swapped(mine, 2)
-    send_late, send_early, keep_late, keep_early = project(late, early, w_near_send, w_near_keep, mine)
-    return finish(keep_late, keep_early, swapped(send_late, 1), swapped(send_early, 1), across)
+    first = blocks - counts[0]
+    attended, send, win = attend_early(cfg, first, counts[0], info, q, w_far_send, win, two, 2, tiles)
+    sources, cores, acrosses = [attended], [swapped(send, 1)], []
+    mine = None
+    for count in counts[1:]:
+        first -= count
+        if mine is not None:
+            win, mine = lax.optimization_barrier((win, mine))
+            acrosses.append(swapped(mine, 2))
+        attended, send, keep = attend_next(cfg, first, count, info, q, w_far_send, w_far_keep, win, sources[-1], tiles)
+        mine = keep + cores[-1]
+        sources.append(attended)
+        cores.append(swapped(send, 1))
+    acrosses.append(swapped(mine, 2))
+    (keep,) = project([(sources[-1], w_far_keep)])
+    mine = keep + cores[-1]
+    acrosses.append(swapped(mine, 2))
+    acrosses[0], mine, *sources = lax.optimization_barrier((acrosses[0], mine, *sources))
+    sends = project([(source, w_near_send) for source in sources])
+    keeps = project([(source, w_near_keep) for source in sources])
+    return finish(rows_here, keeps, [swapped(send, 1) for send in sends], acrosses)
 
 
 def solution(mesh):

time: 58.4 us -> 54.4 us (0.932)
  waiting for transfers between devices: 34.1 us -> 26 us
  starting transfers between devices: 6.56 us -> 8.79 us
  Pallas kernels: 12.3 us -> 13.9 us
    ppermute x5 -> x9, waiting for transfers between devices: 20 us -> 12.1 us  [swapped(): lax.ppermute(value, 'heads', [(source, source ^ flip) for source in range...]
    ppermute x5 -> x9, starting transfers between devices: 2.69 us -> 4.92 us  [swapped(): lax.ppermute(value, 'heads', [(source, source ^ flip) for source in range...]
    pallas_call x5 -> x8, Pallas kernels: 11.5 us -> 13.1 us  [the longest x2 6.03 us: attend_next(): pl.pallas_call(functools.partial(next_body, cfg, first), out_shape=[rows_...]
  transfers between devices with their start and end apart: 8 -> 12, of which waited for: 8 -> 7; matrix products, arithmetic and copies ran while one was open for 0% -> 1% of each run, Pallas kernels for 5% -> 18%
where the time goes in v4:
time: 54.4 us; the launch traced here: 54.2 us
  waiting for transfers between devices  26 us (48%)
  Pallas kernels  13.9 us (26%)
  starting transfers between devices  8.79 us (16%)
  local copies, waits for them, and re-layouts  4 us (7%)
  other arithmetic  1.3 us (2%)
    ppermute x3, waiting for transfers between devices, shifted(): lax.ppermute(value, axis, [(source, source + steps) for source in range(c...  14 us
    ppermute x9, waiting for transfers between devices, swapped(): lax.ppermute(value, 'heads', [(source, source ^ flip) for source in range...  12.1 us
    pallas_call x2, Pallas kernels, attend_next(): pl.pallas_call(functools.partial(next_body, cfg, first), out_shape=[rows_...  6.03 us
    ppermute x9, starting transfers between devices, swapped(): lax.ppermute(value, 'heads', [(source, source ^ flip) for source in range...  4.92 us
    unnamed x8, local copies, waits for them, and re-layouts  4 us
    ppermute x3, starting transfers between devices, shifted(): lax.ppermute(value, axis, [(source, source + steps) for source in range(c...  3.86 us
    pallas_call x3, Pallas kernels, project(): pl.pallas_call(functools.partial(project_body, count), out_shape=[rows_of...  3 us
    pallas_call x1, Pallas kernels, attend_early(): pl.pallas_call(functools.partial(early_body, cfg, first, (BAND - stride)...  2.87 us
  transfers between devices with their start and end apart: 12, of which 7 were waited for; matrix products, arithmetic and copies ran while one was open for 1% of the time, Pallas kernels for 18%

profile of v4, /device:TPU:28, one launch (start us, length us, event | category | flops | bytes accessed | tf_op | source)
XLA Modules:
  0.0 54.2 jit_solution(16767087847317122195)
XLA Ops:
  0.0 1.0 %pad_maximum_fusion.first.refs_0_ = bf16[512,256]{1,0:T(8,128)(2,1)S(1)} fusion(bf16[512,128]{1,0:T(8,128)(2,1)} %bitcast.6, bf16[512,128]{1,0:T(8,128)(2,1)} %bitcast.7), kind=kLoop, calls=%fused_computation | loop fusion | flops 524288 | bytes 524288 | tf_op jit(solution)/shard_map/concatenate | solution.py:288
  1.0 1.3 %collective-permute-start = (bf16[512,256]{1,0:T(8,128)(2,1)S(1)}, bf16[512,256]{1,0:T(8,128)(2,1)S(1)}, u32[]{:S(2)}, u32[]{:S(2)}) collective-permute-start(bf16[512,256]{1,0:T(8,128)(2,1)S(1)} %pad_maximum_fusion.first.refs_0_), channel_id=1, source_target_pairs={{0,4},{4,8},{8,12},{1,5},{5,9},{9,13},{2,6},{6,10},{10,14},{3,7},{... | collective-permute-start | bytes 786440 | tf_op jit(solution)/shard_map/ppermute | solution.py:23
  2.3 1.3 %collective-permute-start.1 = (bf16[512,256]{1,0:T(8,128)(2,1)S(1)}, bf16[512,256]{1,0:T(8,128)(2,1)S(1)}, u32[]{:S(2)}, u32[]{:S(2)}) collective-permute-start(bf16[512,256]{1,0:T(8,128)(2,1)S(1)} %pad_maximum_fusion.first.refs_0_), channel_id=1, source_target_pairs={{0,12},{1,13},{2,14},{3,15},{16,28},{17,29},{18,30},{19,31}} | collective-permute-start | bytes 786440 | tf_op jit(solution)/shard_map/ppermute | solution.py:23
  3.6 2.8 %copy-done = bf16[896,3584]{1,0:T(8,128)(2,1)S(1)} copy-done((bf16[896,3584]{1,0:T(8,128)(2,1)S(1)}, bf16[896,3584]{1,0:T(8,128)(2,1)}, u32[]{:S(2)}) %copy-start) | copy-done | bytes 6422552
  6.4 1.2 %copy-done.1 = bf16[512,7,128]{2,0,1:T(8,128)(2,1)S(1)} copy-done((bf16[512,7,128]{2,0,1:T(8,128)(2,1)S(1)}, bf16[512,7,128]{2,0,1:T(8,128)(2,1)}, u32[]{:S(2)}) %copy-start.1) | copy-done | bytes 917528
  7.6 0.8 %stage.1 = (bf16[7,512,128]{2,1,0:T(8,128)(2,1)S(1)}, bf16[896,896]{1,0:T(8,128)(2,1)S(1)}, bf16[896,896]{1,0:T(8,128)(2,1)S(1)}, bf16[896,896]{1,0:T(8,128)(2,1)S(1)}, bf16[896,896]{1,0:T(8,128)(2,1)S(1)}) custom-call(bf16[7,512,128]{2,1,0:T(8,128)(2,1)S(1)} %bitcast.5, bf16[896,3584]{1,0:T(8,128)(2,1)S(1)} %copy-done, ...), custom_call_target="tpu_custom_call" | custom-call | flops 1 | bytes 1 | tf_op jit(solution)/shard_map/stage/pallas_call | solution.py:217
  8.4 7.2 %collective-permute-done.refs_1_ = bf16[512,256]{1,0:T(8,128)(2,1)S(1)} collective-permute-done((bf16[512,256]{1,0:T(8,128)(2,1)S(1)}, bf16[512,256]{1,0:T(8,128)(2,1)S(1)}, u32[]{:S(2)}, u32[]{:S(2)}) %collective-permute-start) | collective-permute-done | bytes 262176 | tf_op jit(solution)/shard_map/ppermute | solution.py:23
  15.6 1.3 %collective-permute-start.2 = (bf16[512,256]{1,0:T(8,128)(2,1)S(1)}, bf16[512,256]{1,0:T(8,128)(2,1)S(1)}, u32[]{:S(2)}, u32[]{:S(2)}) collective-permute-start(bf16[512,256]{1,0:T(8,128)(2,1)S(1)} %collective-permute-done.refs_1_), channel_id=1, source_target_pairs={{0,4},{4,8},{8,12},{1,5},{5,9},{9,13},{2,6},{6,10},{10,14},{3,7},{... | collective-permute-start | bytes 786440 | tf_op jit(solution)/shard_map/ppermute | solution.py:23
  17.0 0.6 %collective-permute-done.1.refs_2_ = bf16[512,256]{1,0:T(8,128)(2,1)S(1)} collective-permute-done((bf16[512,256]{1,0:T(8,128)(2,1)S(1)}, bf16[512,256]{1,0:T(8,128)(2,1)S(1)}, u32[]{:S(2)}, u32[]{:S(2)}) %collective-permute-start.1) | collective-permute-done | bytes 262176 | tf_op jit(solution)/shard_map/ppermute | solution.py:23
  17.6 6.2 %collective-permute-done.2.piece = bf16[512,256]{1,0:T(8,128)(2,1)S(1)} collective-permute-done((bf16[512,256]{1,0:T(8,128)(2,1)S(1)}, bf16[512,256]{1,0:T(8,128)(2,1)S(1)}, u32[]{:S(2)}, u32[]{:S(2)}) %collective-permute-start.2) | collective-permute-done | bytes 262176 | tf_op jit(solution)/shard_map/ppermute | solution.py:23
  23.8 2.9 %attend_early.1 = (bf16[192,896]{1,0:T(8,128)(2,1)S(1)}, bf16[192,896]{1,0:T(8,128)(2,1)S(1)}, bf16[2048,256]{1,0:T(8,128)(2,1)S(1)}) custom-call(s32[12]{0:T(128)S(1)} %pad_add_fusion.info, bf16[7,512,128]{2,1,0:T(8,128)(2,1)S(1)} %get-tuple-element.34.q_ref, bf16[896,896]{1,0:T(8,128)(2,1)S(1)} %get-tuple-element.35.w_send, ...), custom_call_target="tpu_custom_call", output_to_operand_aliasing={{2}: (3, {})} | custom-call | flops 1536000000 | bytes 6000000 | tf_op jit(solution)/shard_map/attend_early/pallas_call | solution.py:175
  26.8 3.2 %attend_next.2 = (bf16[192,896]{1,0:T(8,128)(2,1)S(1)}, bf16[192,896]{1,0:T(8,128)(2,1)S(1)}, bf16[192,896]{1,0:T(8,128)(2,1)S(1)}) custom-call(s32[12]{0:T(128)S(1)} %pad_add_fusion.info, bf16[7,512,128]{2,1,0:T(8,128)(2,1)S(1)} %get-tuple-element.34.q_ref, bf16[896,896]{1,0:T(8,128)(2,1)S(1)} %get-tuple-element.35.w_send, ...), custom_call_target="tpu_custom_call" | custom-call | flops 1536000000 | bytes 6000000 | tf_op jit(solution)/shard_map/attend_next/pallas_call | solution.py:191
  30.1 0.6 %collective-permute-start.9 = (bf16[192,896]{1,0:T(8,128)(2,1)S(1)}, bf16[192,896]{1,0:T(8,128)(2,1)S(1)}, u32[]{:S(2)}, u32[]{:S(2)}) collective-permute-start(bf16[192,896]{1,0:T(8,128)(2,1)S(1)} %get-tuple-element.60), channel_id=1, source_target_pairs={{0,1},{1,0},{2,3},{3,2},{4,5},{5,4},{6,7},{7,6},{8,9},{9,8},{10,11... | collective-permute-start | bytes 1032200 | tf_op jit(solution)/shard_map/ppermute | solution.py:28
  30.7 1.6 %collective-permute-start.4 = (bf16[192,896]{1,0:T(8,128)(2,1)S(1)}, bf16[192,896]{1,0:T(8,128)(2,1)S(1)}, u32[]{:S(2)}, u32[]{:S(2)}) collective-permute-start(bf16[192,896]{1,0:T(8,128)(2,1)S(1)} %add.9), channel_id=1, source_target_pairs={{0,2},{1,3},{2,0},{3,1},{4,6},{5,7},{6,4},{7,5},{8,10},{9,11},{10,... | collective-permute-start | bytes 1032200 | tf_op jit(solution)/shard_map/ppermute | solution.py:28
  32.3 2.8 %attend_next.3 = (bf16[128,896]{1,0:T(8,128)(2,1)S(1)}, bf16[128,896]{1,0:T(8,128)(2,1)S(1)}, bf16[192,896]{1,0:T(8,128)(2,1)S(1)}) custom-call(s32[12]{0:T(128)S(1)} %pad_add_fusion.info, bf16[7,512,128]{2,1,0:T(8,128)(2,1)S(1)} %get-tuple-element.34.q_ref, bf16[896,896]{1,0:T(8,128)(2,1)S(1)} %get-tuple-element.35.w_send, ...), custom_call_target="tpu_custom_call" | custom-call | flops 1024000000 | bytes 6000000 | tf_op jit(solution)/shard_map/attend_next/pallas_call | solution.py:191
  35.2 0.6 %collective-permute-start.10 = (bf16[192,896]{1,0:T(8,128)(2,1)S(1)}, bf16[192,896]{1,0:T(8,128)(2,1)S(1)}, u32[]{:S(2)}, u32[]{:S(2)}) collective-permute-start(bf16[192,896]{1,0:T(8,128)(2,1)S(1)} %add.11), channel_id=1, source_target_pairs={{0,2},{1,3},{2,0},{3,1},{4,6},{5,7},{6,4},{7,5},{8,10},{9,11},{10,... | collective-permute-start | bytes 1032200 | tf_op jit(solution)/shard_map/ppermute | solution.py:28
  36.7 5.0 %collective-permute-done.4.refs_6_ = bf16[192,896]{1,0:T(8,128)(2,1)S(1)} collective-permute-done((bf16[192,896]{1,0:T(8,128)(2,1)S(1)}, bf16[192,896]{1,0:T(8,128)(2,1)S(1)}, u32[]{:S(2)}, u32[]{:S(2)}) %collective-permute-start.4) | collective-permute-done | bytes 344096 | tf_op jit(solution)/shard_map/ppermute | solution.py:28
  41.7 1.3 %project.5 = (bf16[192,896]{1,0:T(8,128)(2,1)S(1)}, bf16[192,896]{1,0:T(8,128)(2,1)S(1)}, bf16[128,896]{1,0:T(8,128)(2,1)S(1)}) custom-call(bf16[192,896]{1,0:T(8,128)(2,1)S(1)} %get-tuple-element.47.before.refs_0_, bf16[192,896]{1,0:T(8,128)(2,1)S(1)} %get-tuple-element.48.before.refs_1_, bf16[128,896]{1,0:T(8,128)(2,1)S(1)} %get-tuple-element.49.refs_0_.refs_2_, ...), custom_call_target="tpu_custom_call" | custom-call | flops 822083584 | bytes 6000000 | tf_op jit(solution)/shard_map/project/pallas_call | solution.py:238
  43.1 0.5 collective-permute-start.7
  43.6 1.5 %collective-permute-start.11 = (bf16[128,896]{1,0:T(8,128)(2,1)S(1)}, bf16[128,896]{1,0:T(8,128)(2,1)S(1)}, u32[]{:S(2)}, u32[]{:S(2)}) collective-permute-start(bf16[128,896]{1,0:T(8,128)(2,1)S(1)} %add.10), channel_id=1, source_target_pairs={{0,2},{1,3},{2,0},{3,1},{4,6},{5,7},{6,4},{7,5},{8,10},{9,11},{10,... | collective-permute-start | bytes 688136 | tf_op jit(solution)/shard_map/ppermute | solution.py:28
  45.0 1.3 %project.4 = (bf16[192,896]{1,0:T(8,128)(2,1)S(1)}, bf16[192,896]{1,0:T(8,128)(2,1)S(1)}, bf16[128,896]{1,0:T(8,128)(2,1)S(1)}) custom-call(bf16[192,896]{1,0:T(8,128)(2,1)S(1)} %get-tuple-element.47.before.refs_0_, bf16[192,896]{1,0:T(8,128)(2,1)S(1)} %get-tuple-element.48.before.refs_1_, bf16[128,896]{1,0:T(8,128)(2,1)S(1)} %get-tuple-element.49.refs_0_.refs_2_, ...), custom_call_target="tpu_custom_call" | custom-call | flops 822083584 | bytes 6000000 | tf_op jit(solution)/shard_map/project/pallas_call | solution.py:238
  46.3 2.7 %collective-permute-done.10.refs_7_ = bf16[192,896]{1,0:T(8,128)(2,1)S(1)} collective-permute-done((bf16[192,896]{1,0:T(8,128)(2,1)S(1)}, bf16[192,896]{1,0:T(8,128)(2,1)S(1)}, u32[]{:S(2)}, u32[]{:S(2)}) %collective-permute-start.10) | collective-permute-done | bytes 344096 | tf_op jit(solution)/shard_map/ppermute | solution.py:28
  49.1 4.0 %collective-permute-done.11.refs_8_ = bf16[128,896]{1,0:T(8,128)(2,1)S(1)} collective-permute-done((bf16[128,896]{1,0:T(8,128)(2,1)S(1)}, bf16[128,896]{1,0:T(8,128)(2,1)S(1)}, u32[]{:S(2)}, u32[]{:S(2)}) %collective-permute-start.11) | collective-permute-done | bytes 229408 | tf_op jit(solution)/shard_map/ppermute | solution.py:28
  53.1 1.1 %finish.1 = bf16[512,896]{1,0:T(8,128)(2,1)} custom-call(bf16[192,896]{1,0:T(8,128)(2,1)S(1)} %get-tuple-element.51.refs_0_, bf16[192,896]{1,0:T(8,128)(2,1)S(1)} %get-tuple-element.52.refs_1_, bf16[128,896]{1,0:T(8,128)(2,1)S(1)} %get-tuple-element.53.refs_2_, bf16[192,896]{1,0:T(8,128)(2,1)S(1)} %collective-permute-done.6.refs_3_, ...), custom_call_target="tpu_custom_call" | custom-call | flops 1 | bytes 1 | tf_op jit(solution)/shard_map/finish/pallas_call | solution.py:268
  (22 shorter events, 1.4 us)
Async XLA Ops:
  1.0 14.6 %collective-permute-start = (bf16[512,256]{1,0:T(8,128)(2,1)S(1)}, bf16[512,256]{1,0:T(8,128)(2,1)S(1)}, u32[]{:S(2)}, u32[]{:S(2)}) collective-permute-start(bf16[512,256]{1,0:T(8,128)(2,1)S(1)} %pad_maximum_fusion.first.refs_0_), channel_id=1, source_target_pairs={{0,4},{4,8},{8,12},{1,5},{5,9},{9,13},{2,6},{6,10},{10,14},{3,7},{... | collective-permute-start | bytes 786440 | tf_op jit(solution)/shard_map/ppermute | solution.py:23
  2.3 15.2 %collective-permute-start.1 = (bf16[512,256]{1,0:T(8,128)(2,1)S(1)}, bf16[512,256]{1,0:T(8,128)(2,1)S(1)}, u32[]{:S(2)}, u32[]{:S(2)}) collective-permute-start(bf16[512,256]{1,0:T(8,128)(2,1)S(1)} %pad_maximum_fusion.first.refs_0_), channel_id=1, source_target_pairs={{0,12},{1,13},{2,14},{3,15},{16,28},{17,29},{18,30},{19,31}} | collective-permute-start | bytes 786440 | tf_op jit(solution)/shard_map/ppermute | solution.py:23
  3.6 2.8 %copy-start = (bf16[896,3584]{1,0:T(8,128)(2,1)S(1)}, bf16[896,3584]{1,0:T(8,128)(2,1)}, u32[]{:S(2)}) copy-start(bf16[896,3584]{1,0:T(8,128)(2,1)} %weight.1) | copy-start | bytes 19267588
  6.4 1.2 %copy-start.1 = (bf16[512,7,128]{2,0,1:T(8,128)(2,1)S(1)}, bf16[512,7,128]{2,0,1:T(8,128)(2,1)}, u32[]{:S(2)}) copy-start(bf16[512,7,128]{2,0,1:T(8,128)(2,1)} %param.6) | copy-start | bytes 2752516
  7.6 9.3 %copy-start.2 = (s32[1,4]{1,0:T(1,128)S(1)}, s32[1,4]{1,0:T(1,128)}, u32[]{:S(2)}) copy-start(s32[1,4]{1,0:T(1,128)} %param.11) | copy-start | bytes 52
  7.6 9.3 %copy-start.3 = (s32[1,8]{1,0:T(1,128)S(1)}, s32[1,8]{1,0:T(1,128)}, u32[]{:S(2)}) copy-start(s32[1,8]{1,0:T(1,128)} %param.10) | copy-start | bytes 100
  15.6 8.3 %collective-permute-start.2 = (bf16[512,256]{1,0:T(8,128)(2,1)S(1)}, bf16[512,256]{1,0:T(8,128)(2,1)S(1)}, u32[]{:S(2)}, u32[]{:S(2)}) collective-permute-start(bf16[512,256]{1,0:T(8,128)(2,1)S(1)} %collective-permute-done.refs_1_), channel_id=1, source_target_pairs={{0,4},{4,8},{8,12},{1,5},{5,9},{9,13},{2,6},{6,10},{10,14},{3,7},{... | collective-permute-start | bytes 786440 | tf_op jit(solution)/shard_map/ppermute | solution.py:23
  26.7 3.9 %collective-permute-start.3 = (bf16[192,896]{1,0:T(8,128)(2,1)S(1)}, bf16[192,896]{1,0:T(8,128)(2,1)S(1)}, u32[]{:S(2)}, u32[]{:S(2)}) collective-permute-start(bf16[192,896]{1,0:T(8,128)(2,1)S(1)} %get-tuple-element.41), channel_id=1, source_target_pairs={{0,1},{1,0},{2,3},{3,2},{4,5},{5,4},{6,7},{7,6},{8,9},{9,8},{10,11... | collective-permute-start | bytes 1032200 | tf_op jit(solution)/shard_map/ppermute | solution.py:28
  30.1 5.1 %collective-permute-start.9 = (bf16[192,896]{1,0:T(8,128)(2,1)S(1)}, bf16[192,896]{1,0:T(8,128)(2,1)S(1)}, u32[]{:S(2)}, u32[]{:S(2)}) collective-permute-start(bf16[192,896]{1,0:T(8,128)(2,1)S(1)} %get-tuple-element.60), channel_id=1, source_target_pairs={{0,1},{1,0},{2,3},{3,2},{4,5},{5,4},{6,7},{7,6},{8,9},{9,8},{10,11... | collective-permute-start | bytes 1032200 | tf_op jit(solution)/shard_map/ppermute | solution.py:28
  30.7 11.0 %collective-permute-start.4 = (bf16[192,896]{1,0:T(8,128)(2,1)S(1)}, bf16[192,896]{1,0:T(8,128)(2,1)S(1)}, u32[]{:S(2)}, u32[]{:S(2)}) collective-permute-start(bf16[192,896]{1,0:T(8,128)(2,1)S(1)} %add.9), channel_id=1, source_target_pairs={{0,2},{1,3},{2,0},{3,1},{4,6},{5,7},{6,4},{7,5},{8,10},{9,11},{10,... | collective-permute-start | bytes 1032200 | tf_op jit(solution)/shard_map/ppermute | solution.py:28
  35.1 1.6 %collective-permute-start.5 = (bf16[128,896]{1,0:T(8,128)(2,1)S(1)}, bf16[128,896]{1,0:T(8,128)(2,1)S(1)}, u32[]{:S(2)}, u32[]{:S(2)}) collective-permute-start(bf16[128,896]{1,0:T(8,128)(2,1)S(1)} %get-tuple-element.46), channel_id=1, source_target_pairs={{0,1},{1,0},{2,3},{3,2},{4,5},{5,4},{6,7},{7,6},{8,9},{9,8},{10,11... | collective-permute-start | bytes 688136 | tf_op jit(solution)/shard_map/ppermute | solution.py:28
  35.2 13.8 %collective-permute-start.10 = (bf16[192,896]{1,0:T(8,128)(2,1)S(1)}, bf16[192,896]{1,0:T(8,128)(2,1)S(1)}, u32[]{:S(2)}, u32[]{:S(2)}) collective-permute-start(bf16[192,896]{1,0:T(8,128)(2,1)S(1)} %add.11), channel_id=1, source_target_pairs={{0,2},{1,3},{2,0},{3,1},{4,6},{5,7},{6,4},{7,5},{8,10},{9,11},{10,... | collective-permute-start | bytes 1032200 | tf_op jit(solution)/shard_map/ppermute | solution.py:28
  43.0 10.1 %collective-permute-start.6 = (bf16[192,896]{1,0:T(8,128)(2,1)S(1)}, bf16[192,896]{1,0:T(8,128)(2,1)S(1)}, u32[]{:S(2)}, u32[]{:S(2)}) collective-permute-start(bf16[192,896]{1,0:T(8,128)(2,1)S(1)} %get-tuple-element.55), channel_id=1, source_target_pairs={{0,1},{1,0},{2,3},{3,2},{4,5},{5,4},{6,7},{7,6},{8,9},{9,8},{10,11... | collective-permute-start | bytes 1032200 | tf_op jit(solution)/shard_map/ppermute | solution.py:28
  43.1 10.0 %collective-permute-start.7 = (bf16[192,896]{1,0:T(8,128)(2,1)S(1)}, bf16[192,896]{1,0:T(8,128)(2,1)S(1)}, u32[]{:S(2)}, u32[]{:S(2)}) collective-permute-start(bf16[192,896]{1,0:T(8,128)(2,1)S(1)} %get-tuple-element.56), channel_id=1, source_target_pairs={{0,1},{1,0},{2,3},{3,2},{4,5},{5,4},{6,7},{7,6},{8,9},{9,8},{10,11... | collective-permute-start | bytes 1032200 | tf_op jit(solution)/shard_map/ppermute | solution.py:28
  43.6 9.5 %collective-permute-start.11 = (bf16[128,896]{1,0:T(8,128)(2,1)S(1)}, bf16[128,896]{1,0:T(8,128)(2,1)S(1)}, u32[]{:S(2)}, u32[]{:S(2)}) collective-permute-start(bf16[128,896]{1,0:T(8,128)(2,1)S(1)} %add.10), channel_id=1, source_target_pairs={{0,2},{1,3},{2,0},{3,1},{4,6},{5,7},{6,4},{7,5},{8,10},{9,11},{10,... | collective-permute-start | bytes 688136 | tf_op jit(solution)/shard_map/ppermute | solution.py:28
  45.0 8.0 %collective-permute-start.8 = (bf16[128,896]{1,0:T(8,128)(2,1)S(1)}, bf16[128,896]{1,0:T(8,128)(2,1)S(1)}, u32[]{:S(2)}, u32[]{:S(2)}) collective-permute-start(bf16[128,896]{1,0:T(8,128)(2,1)S(1)} %get-tuple-element.57), channel_id=1, source_target_pairs={{0,1},{1,0},{2,3},{3,2},{4,5},{5,4},{6,7},{7,6},{8,9},{9,8},{10,11... | collective-permute-start | bytes 688136 | tf_op jit(solution)/shard_map/ppermute | solution.py:28

commit v5 on v4

--- a/solution.py
+++ b/solution.py
@@ -246,35 +246,40 @@
     )(*[source for source, _ in pairs], *[weight for _, weight in pairs])
 
 
-def finish_body(count, *refs):
+def finish_body(end, count, *refs):
     keeps, cores, acrosses = refs[:count], refs[count : 2 * count], refs[2 * count : 3 * count]
     out, total, sems = refs[-3:]
     copies = []
-    end = out.shape[0]
     for index in range(count):
-        where = slice(end - keeps[index].shape[0], end)
+        rows = keeps[index].shape[0]
+        where = slice(end - rows, end)
         end = where.start
+        part = total.at[index, :rows, :]
         value = keeps[index][...].astype(jnp.float32) + cores[index][...].astype(jnp.float32)
-        total[where, :] = (value + acrosses[index][...].astype(jnp.float32)).astype(total.dtype)
-        copies.append(pltpu.make_async_copy(total.at[where, :], out.at[where, :], sems.at[index]))
+        part[...] = (value + acrosses[index][...].astype(jnp.float32)).astype(total.dtype)
+        copies.append(pltpu.make_async_copy(part, out.at[where, :], sems.at[index]))
         copies[-1].start()
     for copy in copies:
         copy.wait()
 
 
-def finish(rows, keeps, cores, acrosses):
+def finish(rows, end, keeps, cores, acrosses, before=()):
     width = keeps[0].shape[1]
     count = len(keeps)
     return pl.pallas_call(
-        functools.partial(finish_body, count),
+        functools.partial(finish_body, end, count),
         out_shape=rows_of(rows, width),
-        in_specs=[VMEM] * (3 * count),
+        in_specs=[VMEM] * (3 * count) + [HBM] * len(before),
         out_specs=HBM,
-        scratch_shapes=[pltpu.VMEM((rows, width), jnp.bfloat16), pltpu.SemaphoreType.DMA((count,))],
+        scratch_shapes=[
+            pltpu.VMEM((count, max(keep.shape[0] for keep in keeps), width), jnp.bfloat16),
+            pltpu.SemaphoreType.DMA((count,)),
+        ],
+        input_output_aliases={3 * count: 0} if before else {},
         compiler_params=pltpu.CompilerParams(vmem_limit_bytes=VMEM_LIMIT),
         cost_estimate=COST,
         name="finish",
-    )(*keeps, *cores, *acrosses)
+    )(*keeps, *cores, *acrosses, *before)
 
 
 def on_device(queries, key_states, value_states, out_weight, slash_offsets, vertical_blocks):
@@ -319,7 +324,9 @@
     acrosses[0], mine, *sources = lax.optimization_barrier((acrosses[0], mine, *sources))
     sends = project([(source, w_near_send) for source in sources])
     keeps = project([(source, w_near_keep) for source in sources])
-    return finish(rows_here, keeps, [swapped(send, 1) for send in sends], acrosses)
+    cores = [swapped(send, 1) for send in sends]
+    out = finish(rows_here, rows_here, keeps[:-1], cores[:-1], acrosses[:-1])
+    return finish(rows_here, keeps[-1].shape[0], keeps[-1:], cores[-1:], acrosses[-1:], (out,))
 
 
 def solution(mesh):

time: 54.4 us -> 54.1 us (level)
  waiting for transfers between devices: 26 us -> 25 us
  Pallas kernels: 13.9 us -> 14.6 us
    ppermute x9, waiting for transfers between devices: 12.1 us -> 11.1 us  [swapped(): lax.ppermute(value, 'heads', [(source, source ^ flip) for source in range...]
    pallas_call x1 -> x2, Pallas kernels: 1.1 us -> 1.78 us  [finish(): pl.pallas_call(functools.partial(finish_body, end, count), out_shape=rows...]
  transfers between devices with their start and end apart: 12 -> 12, of which waited for: 7 -> 7; matrix products, arithmetic and copies ran while one was open for 1% -> 1% of each run, Pallas kernels for 18% -> 20%
where the time goes in v5:
time: 54.1 us; the launch traced here: 53.8 us
  waiting for transfers between devices  25 us (46%)
  Pallas kernels  14.6 us (27%)
  starting transfers between devices  8.78 us (16%)
  local copies, waits for them, and re-layouts  4 us (7%)
  other arithmetic  1.31 us (2%)
    ppermute x3, waiting for transfers between devices, shifted(): lax.ppermute(value, axis, [(source, source + steps) for source in range(c...  14 us
    ppermute x9, waiting for transfers between devices, swapped(): lax.ppermute(value, 'heads', [(source, source ^ flip) for source in range...  11.1 us
    pallas_call x2, Pallas kernels, attend_next(): pl.pallas_call(functools.partial(next_body, cfg, first), out_shape=[rows_...  6.03 us
    ppermute x9, starting transfers between devices, swapped(): lax.ppermute(value, 'heads', [(source, source ^ flip) for source in range...  4.92 us
    unnamed x8, local copies, waits for them, and re-layouts  4 us
    ppermute x3, starting transfers between devices, shifted(): lax.ppermute(value, axis, [(source, source + steps) for source in range(c...  3.86 us
    pallas_call x3, Pallas kernels, project(): pl.pallas_call(functools.partial(project_body, count), out_shape=[rows_of...  3 us
    pallas_call x1, Pallas kernels, attend_early(): pl.pallas_call(functools.partial(early_body, cfg, first, (BAND - stride)...  2.87 us
  transfers between devices with their start and end apart: 12, of which 7 were waited for; matrix products, arithmetic and copies ran while one was open for 1% of the time, Pallas kernels for 20%

profile of v5, /device:TPU:28, one launch (start us, length us, event | category | flops | bytes accessed | tf_op | source)
XLA Modules:
  0.0 53.8 jit_solution(13845683959612177722)
XLA Ops:
  0.0 1.0 %pad_maximum_fusion.first.refs_0_ = bf16[512,256]{1,0:T(8,128)(2,1)S(1)} fusion(bf16[512,128]{1,0:T(8,128)(2,1)} %bitcast.6, bf16[512,128]{1,0:T(8,128)(2,1)} %bitcast.7), kind=kLoop, calls=%fused_computation | loop fusion | flops 524288 | bytes 524288 | tf_op jit(solution)/shard_map/concatenate | solution.py:293
  1.0 1.3 %collective-permute-start = (bf16[512,256]{1,0:T(8,128)(2,1)S(1)}, bf16[512,256]{1,0:T(8,128)(2,1)S(1)}, u32[]{:S(2)}, u32[]{:S(2)}) collective-permute-start(bf16[512,256]{1,0:T(8,128)(2,1)S(1)} %pad_maximum_fusion.first.refs_0_), channel_id=1, source_target_pairs={{0,4},{4,8},{8,12},{1,5},{5,9},{9,13},{2,6},{6,10},{10,14},{3,7},{... | collective-permute-start | bytes 786440 | tf_op jit(solution)/shard_map/ppermute | solution.py:23
  2.3 1.3 %collective-permute-start.1 = (bf16[512,256]{1,0:T(8,128)(2,1)S(1)}, bf16[512,256]{1,0:T(8,128)(2,1)S(1)}, u32[]{:S(2)}, u32[]{:S(2)}) collective-permute-start(bf16[512,256]{1,0:T(8,128)(2,1)S(1)} %pad_maximum_fusion.first.refs_0_), channel_id=1, source_target_pairs={{0,12},{1,13},{2,14},{3,15},{16,28},{17,29},{18,30},{19,31}} | collective-permute-start | bytes 786440 | tf_op jit(solution)/shard_map/ppermute | solution.py:23
  3.6 2.8 %copy-done = bf16[896,3584]{1,0:T(8,128)(2,1)S(1)} copy-done((bf16[896,3584]{1,0:T(8,128)(2,1)S(1)}, bf16[896,3584]{1,0:T(8,128)(2,1)}, u32[]{:S(2)}) %copy-start) | copy-done | bytes 6422552
  6.4 1.2 %copy-done.1 = bf16[512,7,128]{2,0,1:T(8,128)(2,1)S(1)} copy-done((bf16[512,7,128]{2,0,1:T(8,128)(2,1)S(1)}, bf16[512,7,128]{2,0,1:T(8,128)(2,1)}, u32[]{:S(2)}) %copy-start.1) | copy-done | bytes 917528
  7.6 0.8 %stage.1 = (bf16[7,512,128]{2,1,0:T(8,128)(2,1)S(1)}, bf16[896,896]{1,0:T(8,128)(2,1)S(1)}, bf16[896,896]{1,0:T(8,128)(2,1)S(1)}, bf16[896,896]{1,0:T(8,128)(2,1)S(1)}, bf16[896,896]{1,0:T(8,128)(2,1)S(1)}) custom-call(bf16[7,512,128]{2,1,0:T(8,128)(2,1)S(1)} %bitcast.5, bf16[896,3584]{1,0:T(8,128)(2,1)S(1)} %copy-done, ...), custom_call_target="tpu_custom_call" | custom-call | flops 1 | bytes 1 | tf_op jit(solution)/shard_map/stage/pallas_call | solution.py:217
  8.4 7.2 %collective-permute-done.refs_1_ = bf16[512,256]{1,0:T(8,128)(2,1)S(1)} collective-permute-done((bf16[512,256]{1,0:T(8,128)(2,1)S(1)}, bf16[512,256]{1,0:T(8,128)(2,1)S(1)}, u32[]{:S(2)}, u32[]{:S(2)}) %collective-permute-start) | collective-permute-done | bytes 262176 | tf_op jit(solution)/shard_map/ppermute | solution.py:23
  15.6 1.3 %collective-permute-start.2 = (bf16[512,256]{1,0:T(8,128)(2,1)S(1)}, bf16[512,256]{1,0:T(8,128)(2,1)S(1)}, u32[]{:S(2)}, u32[]{:S(2)}) collective-permute-start(bf16[512,256]{1,0:T(8,128)(2,1)S(1)} %collective-permute-done.refs_1_), channel_id=1, source_target_pairs={{0,4},{4,8},{8,12},{1,5},{5,9},{9,13},{2,6},{6,10},{10,14},{3,7},{... | collective-permute-start | bytes 786440 | tf_op jit(solution)/shard_map/ppermute | solution.py:23
  17.0 0.6 %collective-permute-done.1.refs_2_ = bf16[512,256]{1,0:T(8,128)(2,1)S(1)} collective-permute-done((bf16[512,256]{1,0:T(8,128)(2,1)S(1)}, bf16[512,256]{1,0:T(8,128)(2,1)S(1)}, u32[]{:S(2)}, u32[]{:S(2)}) %collective-permute-start.1) | collective-permute-done | bytes 262176 | tf_op jit(solution)/shard_map/ppermute | solution.py:23
  17.6 6.2 %collective-permute-done.2.piece = bf16[512,256]{1,0:T(8,128)(2,1)S(1)} collective-permute-done((bf16[512,256]{1,0:T(8,128)(2,1)S(1)}, bf16[512,256]{1,0:T(8,128)(2,1)S(1)}, u32[]{:S(2)}, u32[]{:S(2)}) %collective-permute-start.2) | collective-permute-done | bytes 262176 | tf_op jit(solution)/shard_map/ppermute | solution.py:23
  23.8 2.9 %attend_early.1 = (bf16[192,896]{1,0:T(8,128)(2,1)S(1)}, bf16[192,896]{1,0:T(8,128)(2,1)S(1)}, bf16[2048,256]{1,0:T(8,128)(2,1)S(1)}) custom-call(s32[12]{0:T(128)S(1)} %pad_add_fusion.info, bf16[7,512,128]{2,1,0:T(8,128)(2,1)S(1)} %get-tuple-element.34.q_ref, bf16[896,896]{1,0:T(8,128)(2,1)S(1)} %get-tuple-element.35.w_send, ...), custom_call_target="tpu_custom_call", output_to_operand_aliasing={{2}: (3, {})} | custom-call | flops 1536000000 | bytes 6000000 | tf_op jit(solution)/shard_map/attend_early/pallas_call | solution.py:175
  26.8 3.2 %attend_next.2 = (bf16[192,896]{1,0:T(8,128)(2,1)S(1)}, bf16[192,896]{1,0:T(8,128)(2,1)S(1)}, bf16[192,896]{1,0:T(8,128)(2,1)S(1)}) custom-call(s32[12]{0:T(128)S(1)} %pad_add_fusion.info, bf16[7,512,128]{2,1,0:T(8,128)(2,1)S(1)} %get-tuple-element.34.q_ref, bf16[896,896]{1,0:T(8,128)(2,1)S(1)} %get-tuple-element.35.w_send, ...), custom_call_target="tpu_custom_call" | custom-call | flops 1536000000 | bytes 6000000 | tf_op jit(solution)/shard_map/attend_next/pallas_call | solution.py:191
  30.1 0.6 %collective-permute-start.10 = (bf16[192,896]{1,0:T(8,128)(2,1)S(1)}, bf16[192,896]{1,0:T(8,128)(2,1)S(1)}, u32[]{:S(2)}, u32[]{:S(2)}) collective-permute-start(bf16[192,896]{1,0:T(8,128)(2,1)S(1)} %get-tuple-element.60), channel_id=1, source_target_pairs={{0,1},{1,0},{2,3},{3,2},{4,5},{5,4},{6,7},{7,6},{8,9},{9,8},{10,11... | collective-permute-start | bytes 1032200 | tf_op jit(solution)/shard_map/ppermute | solution.py:28
  30.7 1.6 %collective-permute-start.4 = (bf16[192,896]{1,0:T(8,128)(2,1)S(1)}, bf16[192,896]{1,0:T(8,128)(2,1)S(1)}, u32[]{:S(2)}, u32[]{:S(2)}) collective-permute-start(bf16[192,896]{1,0:T(8,128)(2,1)S(1)} %add.9), channel_id=1, source_target_pairs={{0,2},{1,3},{2,0},{3,1},{4,6},{5,7},{6,4},{7,5},{8,10},{9,11},{10,... | collective-permute-start | bytes 1032200 | tf_op jit(solution)/shard_map/ppermute | solution.py:28
  32.3 2.8 %attend_next.3 = (bf16[128,896]{1,0:T(8,128)(2,1)S(1)}, bf16[128,896]{1,0:T(8,128)(2,1)S(1)}, bf16[192,896]{1,0:T(8,128)(2,1)S(1)}) custom-call(s32[12]{0:T(128)S(1)} %pad_add_fusion.info, bf16[7,512,128]{2,1,0:T(8,128)(2,1)S(1)} %get-tuple-element.34.q_ref, bf16[896,896]{1,0:T(8,128)(2,1)S(1)} %get-tuple-element.35.w_send, ...), custom_call_target="tpu_custom_call" | custom-call | flops 1024000000 | bytes 6000000 | tf_op jit(solution)/shard_map/attend_next/pallas_call | solution.py:191
  35.3 0.6 %collective-permute-start.11 = (bf16[192,896]{1,0:T(8,128)(2,1)S(1)}, bf16[192,896]{1,0:T(8,128)(2,1)S(1)}, u32[]{:S(2)}, u32[]{:S(2)}) collective-permute-start(bf16[192,896]{1,0:T(8,128)(2,1)S(1)} %add.11), channel_id=1, source_target_pairs={{0,2},{1,3},{2,0},{3,1},{4,6},{5,7},{6,4},{7,5},{8,10},{9,11},{10,... | collective-permute-start | bytes 1032200 | tf_op jit(solution)/shard_map/ppermute | solution.py:28
  36.7 5.0 %collective-permute-done.4.refs_4_ = bf16[192,896]{1,0:T(8,128)(2,1)S(1)} collective-permute-done((bf16[192,896]{1,0:T(8,128)(2,1)S(1)}, bf16[192,896]{1,0:T(8,128)(2,1)S(1)}, u32[]{:S(2)}, u32[]{:S(2)}) %collective-permute-start.4) | collective-permute-done | bytes 344096 | tf_op jit(solution)/shard_map/ppermute | solution.py:28
  41.7 1.3 %project.5 = (bf16[192,896]{1,0:T(8,128)(2,1)S(1)}, bf16[192,896]{1,0:T(8,128)(2,1)S(1)}, bf16[128,896]{1,0:T(8,128)(2,1)S(1)}) custom-call(bf16[192,896]{1,0:T(8,128)(2,1)S(1)} %get-tuple-element.47.before.refs_0_, bf16[192,896]{1,0:T(8,128)(2,1)S(1)} %get-tuple-element.48.before.refs_1_, bf16[128,896]{1,0:T(8,128)(2,1)S(1)} %get-tuple-element.49.refs_0_.refs_2_, ...), custom_call_target="tpu_custom_call" | custom-call | flops 822083584 | bytes 6000000 | tf_op jit(solution)/shard_map/project/pallas_call | solution.py:238
  43.6 1.5 %collective-permute-start.7 = (bf16[128,896]{1,0:T(8,128)(2,1)S(1)}, bf16[128,896]{1,0:T(8,128)(2,1)S(1)}, u32[]{:S(2)}, u32[]{:S(2)}) collective-permute-start(bf16[128,896]{1,0:T(8,128)(2,1)S(1)} %add.10), channel_id=1, source_target_pairs={{0,2},{1,3},{2,0},{3,1},{4,6},{5,7},{6,4},{7,5},{8,10},{9,11},{10,... | collective-permute-start | bytes 688136 | tf_op jit(solution)/shard_map/ppermute | solution.py:28
  45.1 1.3 %project.4 = (bf16[192,896]{1,0:T(8,128)(2,1)S(1)}, bf16[192,896]{1,0:T(8,128)(2,1)S(1)}, bf16[128,896]{1,0:T(8,128)(2,1)S(1)}) custom-call(bf16[192,896]{1,0:T(8,128)(2,1)S(1)} %get-tuple-element.47.before.refs_0_, bf16[192,896]{1,0:T(8,128)(2,1)S(1)} %get-tuple-element.48.before.refs_1_, bf16[128,896]{1,0:T(8,128)(2,1)S(1)} %get-tuple-element.49.refs_0_.refs_2_, ...), custom_call_target="tpu_custom_call" | custom-call | flops 822083584 | bytes 6000000 | tf_op jit(solution)/shard_map/project/pallas_call | solution.py:238
  46.3 2.7 %collective-permute-done.11.refs_5_ = bf16[192,896]{1,0:T(8,128)(2,1)S(1)} collective-permute-done((bf16[192,896]{1,0:T(8,128)(2,1)S(1)}, bf16[192,896]{1,0:T(8,128)(2,1)S(1)}, u32[]{:S(2)}, u32[]{:S(2)}) %collective-permute-start.11) | collective-permute-done | bytes 344096 | tf_op jit(solution)/shard_map/ppermute | solution.py:28
  49.1 1.0 %finish.2.refs_3_ = bf16[512,896]{1,0:T(8,128)(2,1)} custom-call(bf16[192,896]{1,0:T(8,128)(2,1)S(1)} %get-tuple-element.54.refs_0_, bf16[192,896]{1,0:T(8,128)(2,1)S(1)} %get-tuple-element.55.refs_1_, bf16[192,896]{1,0:T(8,128)(2,1)S(1)} %collective-permute-done.8.refs_2_, bf16[192,896]{1,0:T(8,128)(2,1)S(1)} %collective-permute-done.9.refs_3_, ...), custom_call_target="tpu_custom_call" | custom-call | flops 1 | bytes 1 | tf_op jit(solution)/shard_map/finish/pallas_call | solution.py:269
  50.1 3.0 %collective-permute-done.7.refs_2_ = bf16[128,896]{1,0:T(8,128)(2,1)S(1)} collective-permute-done((bf16[128,896]{1,0:T(8,128)(2,1)S(1)}, bf16[128,896]{1,0:T(8,128)(2,1)S(1)}, u32[]{:S(2)}, u32[]{:S(2)}) %collective-permute-start.7) | collective-permute-done | bytes 229408 | tf_op jit(solution)/shard_map/ppermute | solution.py:28
  53.1 0.8 %finish.3 = bf16[512,896]{1,0:T(8,128)(2,1)} custom-call(bf16[128,896]{1,0:T(8,128)(2,1)S(1)} %get-tuple-element.51.refs_0_, bf16[128,896]{1,0:T(8,128)(2,1)S(1)} %collective-permute-done.6.refs_1_, bf16[128,896]{1,0:T(8,128)(2,1)S(1)} %collective-permute-done.7.refs_2_, bf16[512,896]{1,0:T(8,128)(2,1)} %finish.2.refs_3_), custom_call_target="tpu_custom_call", output_to_operand_aliasing={{}: (3, {})} | custom-call | flops 1 | bytes 1 | tf_op jit(solution)/shard_map/finish/pallas_call | solution.py:269
  (23 shorter events, 1.9 us)
Async XLA Ops:
  1.0 14.6 %collective-permute-start = (bf16[512,256]{1,0:T(8,128)(2,1)S(1)}, bf16[512,256]{1,0:T(8,128)(2,1)S(1)}, u32[]{:S(2)}, u32[]{:S(2)}) collective-permute-start(bf16[512,256]{1,0:T(8,128)(2,1)S(1)} %pad_maximum_fusion.first.refs_0_), channel_id=1, source_target_pairs={{0,4},{4,8},{8,12},{1,5},{5,9},{9,13},{2,6},{6,10},{10,14},{3,7},{... | collective-permute-start | bytes 786440 | tf_op jit(solution)/shard_map/ppermute | solution.py:23
  2.3 15.2 %collective-permute-start.1 = (bf16[512,256]{1,0:T(8,128)(2,1)S(1)}, bf16[512,256]{1,0:T(8,128)(2,1)S(1)}, u32[]{:S(2)}, u32[]{:S(2)}) collective-permute-start(bf16[512,256]{1,0:T(8,128)(2,1)S(1)} %pad_maximum_fusion.first.refs_0_), channel_id=1, source_target_pairs={{0,12},{1,13},{2,14},{3,15},{16,28},{17,29},{18,30},{19,31}} | collective-permute-start | bytes 786440 | tf_op jit(solution)/shard_map/ppermute | solution.py:23
  3.6 2.8 %copy-start = (bf16[896,3584]{1,0:T(8,128)(2,1)S(1)}, bf16[896,3584]{1,0:T(8,128)(2,1)}, u32[]{:S(2)}) copy-start(bf16[896,3584]{1,0:T(8,128)(2,1)} %weight.1) | copy-start | bytes 19267588
  6.4 1.2 %copy-start.1 = (bf16[512,7,128]{2,0,1:T(8,128)(2,1)S(1)}, bf16[512,7,128]{2,0,1:T(8,128)(2,1)}, u32[]{:S(2)}) copy-start(bf16[512,7,128]{2,0,1:T(8,128)(2,1)} %param.6) | copy-start | bytes 2752516
  7.6 9.3 %copy-start.2 = (s32[1,4]{1,0:T(1,128)S(1)}, s32[1,4]{1,0:T(1,128)}, u32[]{:S(2)}) copy-start(s32[1,4]{1,0:T(1,128)} %param.11) | copy-start | bytes 52
  7.6 9.3 %copy-start.3 = (s32[1,8]{1,0:T(1,128)S(1)}, s32[1,8]{1,0:T(1,128)}, u32[]{:S(2)}) copy-start(s32[1,8]{1,0:T(1,128)} %param.10) | copy-start | bytes 100
  15.6 8.3 %collective-permute-start.2 = (bf16[512,256]{1,0:T(8,128)(2,1)S(1)}, bf16[512,256]{1,0:T(8,128)(2,1)S(1)}, u32[]{:S(2)}, u32[]{:S(2)}) collective-permute-start(bf16[512,256]{1,0:T(8,128)(2,1)S(1)} %collective-permute-done.refs_1_), channel_id=1, source_target_pairs={{0,4},{4,8},{8,12},{1,5},{5,9},{9,13},{2,6},{6,10},{10,14},{3,7},{... | collective-permute-start | bytes 786440 | tf_op jit(solution)/shard_map/ppermute | solution.py:23
  26.7 3.9 %collective-permute-start.3 = (bf16[192,896]{1,0:T(8,128)(2,1)S(1)}, bf16[192,896]{1,0:T(8,128)(2,1)S(1)}, u32[]{:S(2)}, u32[]{:S(2)}) collective-permute-start(bf16[192,896]{1,0:T(8,128)(2,1)S(1)} %get-tuple-element.41), channel_id=1, source_target_pairs={{0,1},{1,0},{2,3},{3,2},{4,5},{5,4},{6,7},{7,6},{8,9},{9,8},{10,11... | collective-permute-start | bytes 1032200 | tf_op jit(solution)/shard_map/ppermute | solution.py:28
  30.1 5.1 %collective-permute-start.10 = (bf16[192,896]{1,0:T(8,128)(2,1)S(1)}, bf16[192,896]{1,0:T(8,128)(2,1)S(1)}, u32[]{:S(2)}, u32[]{:S(2)}) collective-permute-start(bf16[192,896]{1,0:T(8,128)(2,1)S(1)} %get-tuple-element.60), channel_id=1, source_target_pairs={{0,1},{1,0},{2,3},{3,2},{4,5},{5,4},{6,7},{7,6},{8,9},{9,8},{10,11... | collective-permute-start | bytes 1032200 | tf_op jit(solution)/shard_map/ppermute | solution.py:28
  30.7 11.0 %collective-permute-start.4 = (bf16[192,896]{1,0:T(8,128)(2,1)S(1)}, bf16[192,896]{1,0:T(8,128)(2,1)S(1)}, u32[]{:S(2)}, u32[]{:S(2)}) collective-permute-start(bf16[192,896]{1,0:T(8,128)(2,1)S(1)} %add.9), channel_id=1, source_target_pairs={{0,2},{1,3},{2,0},{3,1},{4,6},{5,7},{6,4},{7,5},{8,10},{9,11},{10,... | collective-permute-start | bytes 1032200 | tf_op jit(solution)/shard_map/ppermute | solution.py:28
  35.1 1.6 %collective-permute-start.5 = (bf16[128,896]{1,0:T(8,128)(2,1)S(1)}, bf16[128,896]{1,0:T(8,128)(2,1)S(1)}, u32[]{:S(2)}, u32[]{:S(2)}) collective-permute-start(bf16[128,896]{1,0:T(8,128)(2,1)S(1)} %get-tuple-element.46), channel_id=1, source_target_pairs={{0,1},{1,0},{2,3},{3,2},{4,5},{5,4},{6,7},{7,6},{8,9},{9,8},{10,11... | collective-permute-start | bytes 688136 | tf_op jit(solution)/shard_map/ppermute | solution.py:28
  35.3 13.8 %collective-permute-start.11 = (bf16[192,896]{1,0:T(8,128)(2,1)S(1)}, bf16[192,896]{1,0:T(8,128)(2,1)S(1)}, u32[]{:S(2)}, u32[]{:S(2)}) collective-permute-start(bf16[192,896]{1,0:T(8,128)(2,1)S(1)} %add.11), channel_id=1, source_target_pairs={{0,2},{1,3},{2,0},{3,1},{4,6},{5,7},{6,4},{7,5},{8,10},{9,11},{10,... | collective-permute-start | bytes 1032200 | tf_op jit(solution)/shard_map/ppermute | solution.py:28
  43.0 6.1 %collective-permute-start.8 = (bf16[192,896]{1,0:T(8,128)(2,1)S(1)}, bf16[192,896]{1,0:T(8,128)(2,1)S(1)}, u32[]{:S(2)}, u32[]{:S(2)}) collective-permute-start(bf16[192,896]{1,0:T(8,128)(2,1)S(1)} %get-tuple-element.56), channel_id=1, source_target_pairs={{0,1},{1,0},{2,3},{3,2},{4,5},{5,4},{6,7},{7,6},{8,9},{9,8},{10,11... | collective-permute-start | bytes 1032200 | tf_op jit(solution)/shard_map/ppermute | solution.py:28
  43.1 6.0 %collective-permute-start.9 = (bf16[192,896]{1,0:T(8,128)(2,1)S(1)}, bf16[192,896]{1,0:T(8,128)(2,1)S(1)}, u32[]{:S(2)}, u32[]{:S(2)}) collective-permute-start(bf16[192,896]{1,0:T(8,128)(2,1)S(1)} %get-tuple-element.57), channel_id=1, source_target_pairs={{0,1},{1,0},{2,3},{3,2},{4,5},{5,4},{6,7},{7,6},{8,9},{9,8},{10,11... | collective-permute-start | bytes 1032200 | tf_op jit(solution)/shard_map/ppermute | solution.py:28
  43.6 9.5 %collective-permute-start.7 = (bf16[128,896]{1,0:T(8,128)(2,1)S(1)}, bf16[128,896]{1,0:T(8,128)(2,1)S(1)}, u32[]{:S(2)}, u32[]{:S(2)}) collective-permute-start(bf16[128,896]{1,0:T(8,128)(2,1)S(1)} %add.10), channel_id=1, source_target_pairs={{0,2},{1,3},{2,0},{3,1},{4,6},{5,7},{6,4},{7,5},{8,10},{9,11},{10,... | collective-permute-start | bytes 688136 | tf_op jit(solution)/shard_map/ppermute | solution.py:28
  45.0 8.0 %collective-permute-start.6 = (bf16[128,896]{1,0:T(8,128)(2,1)S(1)}, bf16[128,896]{1,0:T(8,128)(2,1)S(1)}, u32[]{:S(2)}, u32[]{:S(2)}) collective-permute-start(bf16[128,896]{1,0:T(8,128)(2,1)S(1)} %get-tuple-element.53), channel_id=1, source_target_pairs={{0,1},{1,0},{2,3},{3,2},{4,5},{5,4},{6,7},{7,6},{8,9},{9,8},{10,11... | collective-permute-start | bytes 688136 | tf_op jit(solution)/shard_map/ppermute | solution.py:28

commit v6 on v5

--- a/solution.py
+++ b/solution.py
@@ -28,7 +28,7 @@
     return lax.ppermute(value, "heads", [(source, source ^ flip) for source in range(count)])
 
 
-def attend_block(cfg, info, q_ref, win, tiles, gathered, local, store):
+def block_scores(cfg, info, q_ref, win, tiles, gathered, local):
     slash, n_vert, blocks, heads_here, head = cfg
     shard = lax.axis_index("ctx")
     own = shard * blocks + local
@@ -71,7 +71,11 @@
     near = jnp.concatenate([near] * heads_here, axis=0)
     q = q_ref[:, local * BLOCK : (local + 1) * BLOCK, :].reshape(rows, head)
     scores = lax.dot_general(q, gathered[:, :head], (((1,), (1,)), ((), ())), preferred_element_type=jnp.float32)
-    scores = jnp.concatenate([scores[:, : 2 * BLOCK] + near, scores[:, 2 * BLOCK :] + bias[:, 2 * BLOCK :]], axis=1)
+    return jnp.concatenate([scores[:, : 2 * BLOCK] + near, scores[:, 2 * BLOCK :] + bias[:, 2 * BLOCK :]], axis=1)
+
+
+def block_mix(cfg, scores, gathered, store):
+    slash, n_vert, blocks, heads_here, head = cfg
     factor = math.log2(math.e) * head ** (-0.5)
     row_max = jnp.max(scores, axis=1, keepdims=True)
     weights = jnp.exp2((scores - row_max) * factor).astype(jnp.bfloat16)
@@ -91,13 +95,20 @@
 
 def attend_rows(cfg, info, q_ref, win, tiles, gathered, first, attended):
     slash, n_vert, blocks, heads_here, head = cfg
-    for index in range(attended.shape[0] // BLOCK):
+    count = attended.shape[0] // BLOCK
+
+    def scores_of(index):
+        return block_scores(cfg, info, q_ref, win, tiles, gathered.at[index % gathered.shape[0]], first + index)
+
+    scores = scores_of(0)
+    for index in range(count):
+        ahead = scores_of(index + 1) if index + 1 < count else None
 
         def store(h, value):
             attended[index * BLOCK : (index + 1) * BLOCK, h * head : (h + 1) * head] = value
 
-        part = gathered.at[index % gathered.shape[0]]
-        attend_block(cfg, info, q_ref, win, tiles, part, first + index, store)
+        block_mix(cfg, scores, gathered.at[index % gathered.shape[0]], store)
+        scores = ahead
 
 
 def fill_ones(gathered, head):
@@ -149,9 +160,9 @@
     tiles = refs[0] if len(refs) > 4 else None
     attended, send, keep, gathered = refs[-4:]
     fill_ones(gathered, head)
+    matmul(before, w_keep, keep)
     attend_rows(cfg, info, q_ref, win, tiles, gathered, first, attended)
     matmul(attended, w_send, send)
-    matmul(before, w_keep, keep)
 
 
 def rows_of(count, like):

time: 54.1 us -> 53.7 us (level)
  Pallas kernels: 14.6 us -> 13.9 us
where the time goes in v6:
time: 53.7 us; the launch traced here: 53.5 us
  waiting for transfers between devices  25.3 us (47%)
  Pallas kernels  13.9 us (26%)
  starting transfers between devices  8.77 us (16%)
  local copies, waits for them, and re-layouts  4 us (7%)
  other arithmetic  1.31 us (2%)
    ppermute x3, waiting for transfers between devices, shifted(): lax.ppermute(value, axis, [(source, source + steps) for source in range(c...  14 us
    ppermute x9, waiting for transfers between devices, swapped(): lax.ppermute(value, 'heads', [(source, source ^ flip) for source in range...  11.3 us
    pallas_call x2, Pallas kernels, attend_next(): pl.pallas_call(functools.partial(next_body, cfg, first), out_shape=[rows_...  5.59 us
    ppermute x9, starting transfers between devices, swapped(): lax.ppermute(value, 'heads', [(source, source ^ flip) for source in range...  4.91 us
    unnamed x8, local copies, waits for them, and re-layouts  4 us
    ppermute x3, starting transfers between devices, shifted(): lax.ppermute(value, axis, [(source, source + steps) for source in range(c...  3.86 us
    pallas_call x3, Pallas kernels, project(): pl.pallas_call(functools.partial(project_body, count), out_shape=[rows_of...  3 us
    pallas_call x1, Pallas kernels, attend_early(): pl.pallas_call(functools.partial(early_body, cfg, first, (BAND - stride)...  2.69 us
  transfers between devices with their start and end apart: 12, of which 7 were waited for; matrix products, arithmetic and copies ran while one was open for 1% of the time, Pallas kernels for 20%

profile of v6, /device:TPU:28, one launch (start us, length us, event | category | flops | bytes accessed | tf_op | source)
XLA Modules:
  0.0 53.5 jit_solution(15717100278941993621)
XLA Ops:
  0.0 1.0 %pad_maximum_fusion.first.refs_0_ = bf16[512,256]{1,0:T(8,128)(2,1)S(1)} fusion(bf16[512,128]{1,0:T(8,128)(2,1)} %bitcast.6, bf16[512,128]{1,0:T(8,128)(2,1)} %bitcast.7), kind=kLoop, calls=%fused_computation | loop fusion | flops 524288 | bytes 524288 | tf_op jit(solution)/shard_map/concatenate | solution.py:304
  1.0 1.3 %collective-permute-start = (bf16[512,256]{1,0:T(8,128)(2,1)S(1)}, bf16[512,256]{1,0:T(8,128)(2,1)S(1)}, u32[]{:S(2)}, u32[]{:S(2)}) collective-permute-start(bf16[512,256]{1,0:T(8,128)(2,1)S(1)} %pad_maximum_fusion.first.refs_0_), channel_id=1, source_target_pairs={{0,4},{4,8},{8,12},{1,5},{5,9},{9,13},{2,6},{6,10},{10,14},{3,7},{... | collective-permute-start | bytes 786440 | tf_op jit(solution)/shard_map/ppermute | solution.py:23
  2.3 1.3 %collective-permute-start.1 = (bf16[512,256]{1,0:T(8,128)(2,1)S(1)}, bf16[512,256]{1,0:T(8,128)(2,1)S(1)}, u32[]{:S(2)}, u32[]{:S(2)}) collective-permute-start(bf16[512,256]{1,0:T(8,128)(2,1)S(1)} %pad_maximum_fusion.first.refs_0_), channel_id=1, source_target_pairs={{0,12},{1,13},{2,14},{3,15},{16,28},{17,29},{18,30},{19,31}} | collective-permute-start | bytes 786440 | tf_op jit(solution)/shard_map/ppermute | solution.py:23
  3.6 2.8 %copy-done = bf16[896,3584]{1,0:T(8,128)(2,1)S(1)} copy-done((bf16[896,3584]{1,0:T(8,128)(2,1)S(1)}, bf16[896,3584]{1,0:T(8,128)(2,1)}, u32[]{:S(2)}) %copy-start) | copy-done | bytes 6422552
  6.4 1.2 %copy-done.1 = bf16[512,7,128]{2,0,1:T(8,128)(2,1)S(1)} copy-done((bf16[512,7,128]{2,0,1:T(8,128)(2,1)S(1)}, bf16[512,7,128]{2,0,1:T(8,128)(2,1)}, u32[]{:S(2)}) %copy-start.1) | copy-done | bytes 917528
  7.6 0.8 %stage.1 = (bf16[7,512,128]{2,1,0:T(8,128)(2,1)S(1)}, bf16[896,896]{1,0:T(8,128)(2,1)S(1)}, bf16[896,896]{1,0:T(8,128)(2,1)S(1)}, bf16[896,896]{1,0:T(8,128)(2,1)S(1)}, bf16[896,896]{1,0:T(8,128)(2,1)S(1)}) custom-call(bf16[7,512,128]{2,1,0:T(8,128)(2,1)S(1)} %bitcast.5, bf16[896,3584]{1,0:T(8,128)(2,1)S(1)} %copy-done, ...), custom_call_target="tpu_custom_call" | custom-call | flops 1 | bytes 1 | tf_op jit(solution)/shard_map/stage/pallas_call | solution.py:228
  8.4 7.2 %collective-permute-done.refs_1_ = bf16[512,256]{1,0:T(8,128)(2,1)S(1)} collective-permute-done((bf16[512,256]{1,0:T(8,128)(2,1)S(1)}, bf16[512,256]{1,0:T(8,128)(2,1)S(1)}, u32[]{:S(2)}, u32[]{:S(2)}) %collective-permute-start) | collective-permute-done | bytes 262176 | tf_op jit(solution)/shard_map/ppermute | solution.py:23
  15.6 1.3 %collective-permute-start.2 = (bf16[512,256]{1,0:T(8,128)(2,1)S(1)}, bf16[512,256]{1,0:T(8,128)(2,1)S(1)}, u32[]{:S(2)}, u32[]{:S(2)}) collective-permute-start(bf16[512,256]{1,0:T(8,128)(2,1)S(1)} %collective-permute-done.refs_1_), channel_id=1, source_target_pairs={{0,4},{4,8},{8,12},{1,5},{5,9},{9,13},{2,6},{6,10},{10,14},{3,7},{... | collective-permute-start | bytes 786440 | tf_op jit(solution)/shard_map/ppermute | solution.py:23
  17.0 0.6 %collective-permute-done.1.refs_2_ = bf16[512,256]{1,0:T(8,128)(2,1)S(1)} collective-permute-done((bf16[512,256]{1,0:T(8,128)(2,1)S(1)}, bf16[512,256]{1,0:T(8,128)(2,1)S(1)}, u32[]{:S(2)}, u32[]{:S(2)}) %collective-permute-start.1) | collective-permute-done | bytes 262176 | tf_op jit(solution)/shard_map/ppermute | solution.py:23
  17.6 6.2 %collective-permute-done.2.piece = bf16[512,256]{1,0:T(8,128)(2,1)S(1)} collective-permute-done((bf16[512,256]{1,0:T(8,128)(2,1)S(1)}, bf16[512,256]{1,0:T(8,128)(2,1)S(1)}, u32[]{:S(2)}, u32[]{:S(2)}) %collective-permute-start.2) | collective-permute-done | bytes 262176 | tf_op jit(solution)/shard_map/ppermute | solution.py:23
  23.8 2.7 %attend_early.1 = (bf16[192,896]{1,0:T(8,128)(2,1)S(1)}, bf16[192,896]{1,0:T(8,128)(2,1)S(1)}, bf16[2048,256]{1,0:T(8,128)(2,1)S(1)}) custom-call(s32[12]{0:T(128)S(1)} %pad_add_fusion.info, bf16[7,512,128]{2,1,0:T(8,128)(2,1)S(1)} %get-tuple-element.34.q_ref, bf16[896,896]{1,0:T(8,128)(2,1)S(1)} %get-tuple-element.35.w_send, ...), custom_call_target="tpu_custom_call", output_to_operand_aliasing={{2}: (3, {})} | custom-call | flops 1536000000 | bytes 6000000 | tf_op jit(solution)/shard_map/attend_early/pallas_call | solution.py:186
  26.6 3.1 %attend_next.2 = (bf16[192,896]{1,0:T(8,128)(2,1)S(1)}, bf16[192,896]{1,0:T(8,128)(2,1)S(1)}, bf16[192,896]{1,0:T(8,128)(2,1)S(1)}) custom-call(s32[12]{0:T(128)S(1)} %pad_add_fusion.info, bf16[7,512,128]{2,1,0:T(8,128)(2,1)S(1)} %get-tuple-element.34.q_ref, bf16[896,896]{1,0:T(8,128)(2,1)S(1)} %get-tuple-element.35.w_send, ...), custom_call_target="tpu_custom_call" | custom-call | flops 1536000000 | bytes 6000000 | tf_op jit(solution)/shard_map/attend_next/pallas_call | solution.py:202
  29.7 0.6 %collective-permute-start.10 = (bf16[192,896]{1,0:T(8,128)(2,1)S(1)}, bf16[192,896]{1,0:T(8,128)(2,1)S(1)}, u32[]{:S(2)}, u32[]{:S(2)}) collective-permute-start(bf16[192,896]{1,0:T(8,128)(2,1)S(1)} %get-tuple-element.60), channel_id=1, source_target_pairs={{0,1},{1,0},{2,3},{3,2},{4,5},{5,4},{6,7},{7,6},{8,9},{9,8},{10,11... | collective-permute-start | bytes 1032200 | tf_op jit(solution)/shard_map/ppermute | solution.py:28
  30.3 1.6 %collective-permute-start.4 = (bf16[192,896]{1,0:T(8,128)(2,1)S(1)}, bf16[192,896]{1,0:T(8,128)(2,1)S(1)}, u32[]{:S(2)}, u32[]{:S(2)}) collective-permute-start(bf16[192,896]{1,0:T(8,128)(2,1)S(1)} %add.9), channel_id=1, source_target_pairs={{0,2},{1,3},{2,0},{3,1},{4,6},{5,7},{6,4},{7,5},{8,10},{9,11},{10,... | collective-permute-start | bytes 1032200 | tf_op jit(solution)/shard_map/ppermute | solution.py:28
  31.9 2.5 %attend_next.3 = (bf16[128,896]{1,0:T(8,128)(2,1)S(1)}, bf16[128,896]{1,0:T(8,128)(2,1)S(1)}, bf16[192,896]{1,0:T(8,128)(2,1)S(1)}) custom-call(s32[12]{0:T(128)S(1)} %pad_add_fusion.info, bf16[7,512,128]{2,1,0:T(8,128)(2,1)S(1)} %get-tuple-element.34.q_ref, bf16[896,896]{1,0:T(8,128)(2,1)S(1)} %get-tuple-element.35.w_send, ...), custom_call_target="tpu_custom_call" | custom-call | flops 1024000000 | bytes 6000000 | tf_op jit(solution)/shard_map/attend_next/pallas_call | solution.py:202
  34.6 0.6 %collective-permute-start.11 = (bf16[192,896]{1,0:T(8,128)(2,1)S(1)}, bf16[192,896]{1,0:T(8,128)(2,1)S(1)}, u32[]{:S(2)}, u32[]{:S(2)}) collective-permute-start(bf16[192,896]{1,0:T(8,128)(2,1)S(1)} %add.11), channel_id=1, source_target_pairs={{0,2},{1,3},{2,0},{3,1},{4,6},{5,7},{6,4},{7,5},{8,10},{9,11},{10,... | collective-permute-start | bytes 1032200 | tf_op jit(solution)/shard_map/ppermute | solution.py:28
  36.0 5.3 %collective-permute-done.4.refs_4_ = bf16[192,896]{1,0:T(8,128)(2,1)S(1)} collective-permute-done((bf16[192,896]{1,0:T(8,128)(2,1)S(1)}, bf16[192,896]{1,0:T(8,128)(2,1)S(1)}, u32[]{:S(2)}, u32[]{:S(2)}) %collective-permute-start.4) | collective-permute-done | bytes 344096 | tf_op jit(solution)/shard_map/ppermute | solution.py:28
  41.3 1.3 %project.5 = (bf16[192,896]{1,0:T(8,128)(2,1)S(1)}, bf16[192,896]{1,0:T(8,128)(2,1)S(1)}, bf16[128,896]{1,0:T(8,128)(2,1)S(1)}) custom-call(bf16[192,896]{1,0:T(8,128)(2,1)S(1)} %get-tuple-element.47.before.refs_0_, bf16[192,896]{1,0:T(8,128)(2,1)S(1)} %get-tuple-element.48.before.refs_1_, bf16[128,896]{1,0:T(8,128)(2,1)S(1)} %get-tuple-element.49.refs_0_.refs_2_, ...), custom_call_target="tpu_custom_call" | custom-call | flops 822083584 | bytes 6000000 | tf_op jit(solution)/shard_map/project/pallas_call | solution.py:249
  43.2 1.5 %collective-permute-start.7 = (bf16[128,896]{1,0:T(8,128)(2,1)S(1)}, bf16[128,896]{1,0:T(8,128)(2,1)S(1)}, u32[]{:S(2)}, u32[]{:S(2)}) collective-permute-start(bf16[128,896]{1,0:T(8,128)(2,1)S(1)} %add.10), channel_id=1, source_target_pairs={{0,2},{1,3},{2,0},{3,1},{4,6},{5,7},{6,4},{7,5},{8,10},{9,11},{10,... | collective-permute-start | bytes 688136 | tf_op jit(solution)/shard_map/ppermute | solution.py:28
  44.7 1.3 %project.4 = (bf16[192,896]{1,0:T(8,128)(2,1)S(1)}, bf16[192,896]{1,0:T(8,128)(2,1)S(1)}, bf16[128,896]{1,0:T(8,128)(2,1)S(1)}) custom-call(bf16[192,896]{1,0:T(8,128)(2,1)S(1)} %get-tuple-element.47.before.refs_0_, bf16[192,896]{1,0:T(8,128)(2,1)S(1)} %get-tuple-element.48.before.refs_1_, bf16[128,896]{1,0:T(8,128)(2,1)S(1)} %get-tuple-element.49.refs_0_.refs_2_, ...), custom_call_target="tpu_custom_call" | custom-call | flops 822083584 | bytes 6000000 | tf_op jit(solution)/shard_map/project/pallas_call | solution.py:249
  46.0 2.7 %collective-permute-done.11.refs_5_ = bf16[192,896]{1,0:T(8,128)(2,1)S(1)} collective-permute-done((bf16[192,896]{1,0:T(8,128)(2,1)S(1)}, bf16[192,896]{1,0:T(8,128)(2,1)S(1)}, u32[]{:S(2)}, u32[]{:S(2)}) %collective-permute-start.11) | collective-permute-done | bytes 344096 | tf_op jit(solution)/shard_map/ppermute | solution.py:28
  48.7 1.0 %finish.2.refs_3_ = bf16[512,896]{1,0:T(8,128)(2,1)} custom-call(bf16[192,896]{1,0:T(8,128)(2,1)S(1)} %get-tuple-element.54.refs_0_, bf16[192,896]{1,0:T(8,128)(2,1)S(1)} %get-tuple-element.55.refs_1_, bf16[192,896]{1,0:T(8,128)(2,1)S(1)} %collective-permute-done.8.refs_2_, bf16[192,896]{1,0:T(8,128)(2,1)S(1)} %collective-permute-done.9.refs_3_, ...), custom_call_target="tpu_custom_call" | custom-call | flops 1 | bytes 1 | tf_op jit(solution)/shard_map/finish/pallas_call | solution.py:280
  49.7 3.0 %collective-permute-done.7.refs_2_ = bf16[128,896]{1,0:T(8,128)(2,1)S(1)} collective-permute-done((bf16[128,896]{1,0:T(8,128)(2,1)S(1)}, bf16[128,896]{1,0:T(8,128)(2,1)S(1)}, u32[]{:S(2)}, u32[]{:S(2)}) %collective-permute-start.7) | collective-permute-done | bytes 229408 | tf_op jit(solution)/shard_map/ppermute | solution.py:28
  52.7 0.8 %finish.3 = bf16[512,896]{1,0:T(8,128)(2,1)} custom-call(bf16[128,896]{1,0:T(8,128)(2,1)S(1)} %get-tuple-element.51.refs_0_, bf16[128,896]{1,0:T(8,128)(2,1)S(1)} %collective-permute-done.6.refs_1_, bf16[128,896]{1,0:T(8,128)(2,1)S(1)} %collective-permute-done.7.refs_2_, bf16[512,896]{1,0:T(8,128)(2,1)} %finish.2.refs_3_), custom_call_target="tpu_custom_call", output_to_operand_aliasing={{}: (3, {})} | custom-call | flops 1 | bytes 1 | tf_op jit(solution)/shard_map/finish/pallas_call | solution.py:280
  (23 shorter events, 1.9 us)
Async XLA Ops:
  1.0 14.6 %collective-permute-start = (bf16[512,256]{1,0:T(8,128)(2,1)S(1)}, bf16[512,256]{1,0:T(8,128)(2,1)S(1)}, u32[]{:S(2)}, u32[]{:S(2)}) collective-permute-start(bf16[512,256]{1,0:T(8,128)(2,1)S(1)} %pad_maximum_fusion.first.refs_0_), channel_id=1, source_target_pairs={{0,4},{4,8},{8,12},{1,5},{5,9},{9,13},{2,6},{6,10},{10,14},{3,7},{... | collective-permute-start | bytes 786440 | tf_op jit(solution)/shard_map/ppermute | solution.py:23
  2.3 15.2 %collective-permute-start.1 = (bf16[512,256]{1,0:T(8,128)(2,1)S(1)}, bf16[512,256]{1,0:T(8,128)(2,1)S(1)}, u32[]{:S(2)}, u32[]{:S(2)}) collective-permute-start(bf16[512,256]{1,0:T(8,128)(2,1)S(1)} %pad_maximum_fusion.first.refs_0_), channel_id=1, source_target_pairs={{0,12},{1,13},{2,14},{3,15},{16,28},{17,29},{18,30},{19,31}} | collective-permute-start | bytes 786440 | tf_op jit(solution)/shard_map/ppermute | solution.py:23
  3.6 2.8 %copy-start = (bf16[896,3584]{1,0:T(8,128)(2,1)S(1)}, bf16[896,3584]{1,0:T(8,128)(2,1)}, u32[]{:S(2)}) copy-start(bf16[896,3584]{1,0:T(8,128)(2,1)} %weight.1) | copy-start | bytes 19267588
  6.4 1.2 %copy-start.1 = (bf16[512,7,128]{2,0,1:T(8,128)(2,1)S(1)}, bf16[512,7,128]{2,0,1:T(8,128)(2,1)}, u32[]{:S(2)}) copy-start(bf16[512,7,128]{2,0,1:T(8,128)(2,1)} %param.6) | copy-start | bytes 2752516
  7.6 9.3 %copy-start.2 = (s32[1,4]{1,0:T(1,128)S(1)}, s32[1,4]{1,0:T(1,128)}, u32[]{:S(2)}) copy-start(s32[1,4]{1,0:T(1,128)} %param.11) | copy-start | bytes 52
  7.6 9.3 %copy-start.3 = (s32[1,8]{1,0:T(1,128)S(1)}, s32[1,8]{1,0:T(1,128)}, u32[]{:S(2)}) copy-start(s32[1,8]{1,0:T(1,128)} %param.10) | copy-start | bytes 100
  15.6 8.3 %collective-permute-start.2 = (bf16[512,256]{1,0:T(8,128)(2,1)S(1)}, bf16[512,256]{1,0:T(8,128)(2,1)S(1)}, u32[]{:S(2)}, u32[]{:S(2)}) collective-permute-start(bf16[512,256]{1,0:T(8,128)(2,1)S(1)} %collective-permute-done.refs_1_), channel_id=1, source_target_pairs={{0,4},{4,8},{8,12},{1,5},{5,9},{9,13},{2,6},{6,10},{10,14},{3,7},{... | collective-permute-start | bytes 786440 | tf_op jit(solution)/shard_map/ppermute | solution.py:23
  26.5 3.7 %collective-permute-start.3 = (bf16[192,896]{1,0:T(8,128)(2,1)S(1)}, bf16[192,896]{1,0:T(8,128)(2,1)S(1)}, u32[]{:S(2)}, u32[]{:S(2)}) collective-permute-start(bf16[192,896]{1,0:T(8,128)(2,1)S(1)} %get-tuple-element.41), channel_id=1, source_target_pairs={{0,1},{1,0},{2,3},{3,2},{4,5},{5,4},{6,7},{7,6},{8,9},{9,8},{10,11... | collective-permute-start | bytes 1032200 | tf_op jit(solution)/shard_map/ppermute | solution.py:28
  29.7 4.8 %collective-permute-start.10 = (bf16[192,896]{1,0:T(8,128)(2,1)S(1)}, bf16[192,896]{1,0:T(8,128)(2,1)S(1)}, u32[]{:S(2)}, u32[]{:S(2)}) collective-permute-start(bf16[192,896]{1,0:T(8,128)(2,1)S(1)} %get-tuple-element.60), channel_id=1, source_target_pairs={{0,1},{1,0},{2,3},{3,2},{4,5},{5,4},{6,7},{7,6},{8,9},{9,8},{10,11... | collective-permute-start | bytes 1032200 | tf_op jit(solution)/shard_map/ppermute | solution.py:28
  30.3 11.0 %collective-permute-start.4 = (bf16[192,896]{1,0:T(8,128)(2,1)S(1)}, bf16[192,896]{1,0:T(8,128)(2,1)S(1)}, u32[]{:S(2)}, u32[]{:S(2)}) collective-permute-start(bf16[192,896]{1,0:T(8,128)(2,1)S(1)} %add.9), channel_id=1, source_target_pairs={{0,2},{1,3},{2,0},{3,1},{4,6},{5,7},{6,4},{7,5},{8,10},{9,11},{10,... | collective-permute-start | bytes 1032200 | tf_op jit(solution)/shard_map/ppermute | solution.py:28
  34.4 1.6 %collective-permute-start.5 = (bf16[128,896]{1,0:T(8,128)(2,1)S(1)}, bf16[128,896]{1,0:T(8,128)(2,1)S(1)}, u32[]{:S(2)}, u32[]{:S(2)}) collective-permute-start(bf16[128,896]{1,0:T(8,128)(2,1)S(1)} %get-tuple-element.46), channel_id=1, source_target_pairs={{0,1},{1,0},{2,3},{3,2},{4,5},{5,4},{6,7},{7,6},{8,9},{9,8},{10,11... | collective-permute-start | bytes 688136 | tf_op jit(solution)/shard_map/ppermute | solution.py:28
  34.6 14.1 %collective-permute-start.11 = (bf16[192,896]{1,0:T(8,128)(2,1)S(1)}, bf16[192,896]{1,0:T(8,128)(2,1)S(1)}, u32[]{:S(2)}, u32[]{:S(2)}) collective-permute-start(bf16[192,896]{1,0:T(8,128)(2,1)S(1)} %add.11), channel_id=1, source_target_pairs={{0,2},{1,3},{2,0},{3,1},{4,6},{5,7},{6,4},{7,5},{8,10},{9,11},{10,... | collective-permute-start | bytes 1032200 | tf_op jit(solution)/shard_map/ppermute | solution.py:28
  42.6 6.1 %collective-permute-start.8 = (bf16[192,896]{1,0:T(8,128)(2,1)S(1)}, bf16[192,896]{1,0:T(8,128)(2,1)S(1)}, u32[]{:S(2)}, u32[]{:S(2)}) collective-permute-start(bf16[192,896]{1,0:T(8,128)(2,1)S(1)} %get-tuple-element.56), channel_id=1, source_target_pairs={{0,1},{1,0},{2,3},{3,2},{4,5},{5,4},{6,7},{7,6},{8,9},{9,8},{10,11... | collective-permute-start | bytes 1032200 | tf_op jit(solution)/shard_map/ppermute | solution.py:28
  42.7 6.0 %collective-permute-start.9 = (bf16[192,896]{1,0:T(8,128)(2,1)S(1)}, bf16[192,896]{1,0:T(8,128)(2,1)S(1)}, u32[]{:S(2)}, u32[]{:S(2)}) collective-permute-start(bf16[192,896]{1,0:T(8,128)(2,1)S(1)} %get-tuple-element.57), channel_id=1, source_target_pairs={{0,1},{1,0},{2,3},{3,2},{4,5},{5,4},{6,7},{7,6},{8,9},{9,8},{10,11... | collective-permute-start | bytes 1032200 | tf_op jit(solution)/shard_map/ppermute | solution.py:28
  43.2 9.5 %collective-permute-start.7 = (bf16[128,896]{1,0:T(8,128)(2,1)S(1)}, bf16[128,896]{1,0:T(8,128)(2,1)S(1)}, u32[]{:S(2)}, u32[]{:S(2)}) collective-permute-start(bf16[128,896]{1,0:T(8,128)(2,1)S(1)} %add.10), channel_id=1, source_target_pairs={{0,2},{1,3},{2,0},{3,1},{4,6},{5,7},{6,4},{7,5},{8,10},{9,11},{10,... | collective-permute-start | bytes 688136 | tf_op jit(solution)/shard_map/ppermute | solution.py:28
  44.7 8.0 %collective-permute-start.6 = (bf16[128,896]{1,0:T(8,128)(2,1)S(1)}, bf16[128,896]{1,0:T(8,128)(2,1)S(1)}, u32[]{:S(2)}, u32[]{:S(2)}) collective-permute-start(bf16[128,896]{1,0:T(8,128)(2,1)S(1)} %get-tuple-element.53), channel_id=1, source_target_pairs={{0,1},{1,0},{2,3},{3,2},{4,5},{5,4},{6,7},{7,6},{8,9},{9,8},{10,11... | collective-permute-start | bytes 688136 | tf_op jit(solution)/shard_map/ppermute | solution.py:28

commit v7 on v6

--- a/solution.py
+++ b/solution.py
@@ -258,7 +258,7 @@
 
 
 def finish_body(end, count, *refs):
-    keeps, cores, acrosses = refs[:count], refs[count : 2 * count], refs[2 * count : 3 * count]
+    keeps, acrosses, cores = refs[:count], refs[count : 2 * count], refs[2 * count : 3 * count]
     out, total, sems = refs[-3:]
     copies = []
     for index in range(count):
@@ -290,7 +290,7 @@
         compiler_params=pltpu.CompilerParams(vmem_limit_bytes=VMEM_LIMIT),
         cost_estimate=COST,
         name="finish",
-    )(*keeps, *cores, *acrosses, *before)
+    )(*keeps, *acrosses, *cores, *before)
 
 
 def on_device(queries, key_states, value_states, out_weight, slash_offsets, vertical_blocks):
@@ -326,6 +326,7 @@
             acrosses.append(swapped(mine, 2))
         attended, send, keep = attend_next(cfg, first, count, info, q, w_far_send, w_far_keep, win, sources[-1], tiles)
         mine = keep + cores[-1]
+        mine, send = lax.optimization_barrier((mine, send))
         sources.append(attended)
         cores.append(swapped(send, 1))
     acrosses.append(swapped(mine, 2))

time: 53.7 us -> 53.7 us (level)
  transfers between devices with their start and end apart: 12 -> 12, of which waited for: 7 -> 7; matrix products, arithmetic and copies ran while one was open for 1% -> 0% of each run, Pallas kernels for 20% -> 20%
where the time goes in v7:
time: 53.7 us; the launch traced here: 53.5 us
  waiting for transfers between devices  25.2 us (47%)
  Pallas kernels  13.9 us (26%)
  starting transfers between devices  8.77 us (16%)
  local copies, waits for them, and re-layouts  4 us (7%)
  other arithmetic  1.3 us (2%)
    ppermute x3, waiting for transfers between devices, shifted(): lax.ppermute(value, axis, [(source, source + steps) for source in range(c...  14 us
    ppermute x9, waiting for transfers between devices, swapped(): lax.ppermute(value, 'heads', [(source, source ^ flip) for source in range...  11.3 us
    pallas_call x2, Pallas kernels, attend_next(): pl.pallas_call(functools.partial(next_body, cfg, first), out_shape=[rows_...  5.59 us
    ppermute x9, starting transfers between devices, swapped(): lax.ppermute(value, 'heads', [(source, source ^ flip) for source in range...  4.91 us
    unnamed x8, local copies, waits for them, and re-layouts  4 us
    ppermute x3, starting transfers between devices, shifted(): lax.ppermute(value, axis, [(source, source + steps) for source in range(c...  3.86 us
    pallas_call x3, Pallas kernels, project(): pl.pallas_call(functools.partial(project_body, count), out_shape=[rows_of...  3.01 us
    pallas_call x1, Pallas kernels, attend_early(): pl.pallas_call(functools.partial(early_body, cfg, first, (BAND - stride)...  2.69 us
  transfers between devices with their start and end apart: 12, of which 7 were waited for; matrix products, arithmetic and copies ran while one was open for 0% of the time, Pallas kernels for 20%

profile of v7, /device:TPU:28, one launch (start us, length us, event | category | flops | bytes accessed | tf_op | source)
XLA Modules:
  0.0 53.5 jit_solution(14150043063665596030)
XLA Ops:
  0.0 1.0 %pad_maximum_fusion.first.refs_0_ = bf16[512,256]{1,0:T(8,128)(2,1)S(1)} fusion(bf16[512,128]{1,0:T(8,128)(2,1)} %bitcast.6, bf16[512,128]{1,0:T(8,128)(2,1)} %bitcast.7), kind=kLoop, calls=%fused_computation | loop fusion | flops 524288 | bytes 524288 | tf_op jit(solution)/shard_map/concatenate | solution.py:304
  1.0 1.3 %collective-permute-start = (bf16[512,256]{1,0:T(8,128)(2,1)S(1)}, bf16[512,256]{1,0:T(8,128)(2,1)S(1)}, u32[]{:S(2)}, u32[]{:S(2)}) collective-permute-start(bf16[512,256]{1,0:T(8,128)(2,1)S(1)} %pad_maximum_fusion.first.refs_0_), channel_id=1, source_target_pairs={{0,4},{4,8},{8,12},{1,5},{5,9},{9,13},{2,6},{6,10},{10,14},{3,7},{... | collective-permute-start | bytes 786440 | tf_op jit(solution)/shard_map/ppermute | solution.py:23
  2.3 1.3 %collective-permute-start.1 = (bf16[512,256]{1,0:T(8,128)(2,1)S(1)}, bf16[512,256]{1,0:T(8,128)(2,1)S(1)}, u32[]{:S(2)}, u32[]{:S(2)}) collective-permute-start(bf16[512,256]{1,0:T(8,128)(2,1)S(1)} %pad_maximum_fusion.first.refs_0_), channel_id=1, source_target_pairs={{0,12},{1,13},{2,14},{3,15},{16,28},{17,29},{18,30},{19,31}} | collective-permute-start | bytes 786440 | tf_op jit(solution)/shard_map/ppermute | solution.py:23
  3.6 2.8 %copy-done = bf16[896,3584]{1,0:T(8,128)(2,1)S(1)} copy-done((bf16[896,3584]{1,0:T(8,128)(2,1)S(1)}, bf16[896,3584]{1,0:T(8,128)(2,1)}, u32[]{:S(2)}) %copy-start) | copy-done | bytes 6422552
  6.4 1.2 %copy-done.1 = bf16[512,7,128]{2,0,1:T(8,128)(2,1)S(1)} copy-done((bf16[512,7,128]{2,0,1:T(8,128)(2,1)S(1)}, bf16[512,7,128]{2,0,1:T(8,128)(2,1)}, u32[]{:S(2)}) %copy-start.1) | copy-done | bytes 917528
  7.6 0.8 %stage.1 = (bf16[7,512,128]{2,1,0:T(8,128)(2,1)S(1)}, bf16[896,896]{1,0:T(8,128)(2,1)S(1)}, bf16[896,896]{1,0:T(8,128)(2,1)S(1)}, bf16[896,896]{1,0:T(8,128)(2,1)S(1)}, bf16[896,896]{1,0:T(8,128)(2,1)S(1)}) custom-call(bf16[7,512,128]{2,1,0:T(8,128)(2,1)S(1)} %bitcast.5, bf16[896,3584]{1,0:T(8,128)(2,1)S(1)} %copy-done, ...), custom_call_target="tpu_custom_call" | custom-call | flops 1 | bytes 1 | tf_op jit(solution)/shard_map/stage/pallas_call | solution.py:228
  8.4 7.2 %collective-permute-done.refs_1_ = bf16[512,256]{1,0:T(8,128)(2,1)S(1)} collective-permute-done((bf16[512,256]{1,0:T(8,128)(2,1)S(1)}, bf16[512,256]{1,0:T(8,128)(2,1)S(1)}, u32[]{:S(2)}, u32[]{:S(2)}) %collective-permute-start) | collective-permute-done | bytes 262176 | tf_op jit(solution)/shard_map/ppermute | solution.py:23
  15.6 1.3 %collective-permute-start.2 = (bf16[512,256]{1,0:T(8,128)(2,1)S(1)}, bf16[512,256]{1,0:T(8,128)(2,1)S(1)}, u32[]{:S(2)}, u32[]{:S(2)}) collective-permute-start(bf16[512,256]{1,0:T(8,128)(2,1)S(1)} %collective-permute-done.refs_1_), channel_id=1, source_target_pairs={{0,4},{4,8},{8,12},{1,5},{5,9},{9,13},{2,6},{6,10},{10,14},{3,7},{... | collective-permute-start | bytes 786440 | tf_op jit(solution)/shard_map/ppermute | solution.py:23
  17.0 0.6 %collective-permute-done.1.refs_2_ = bf16[512,256]{1,0:T(8,128)(2,1)S(1)} collective-permute-done((bf16[512,256]{1,0:T(8,128)(2,1)S(1)}, bf16[512,256]{1,0:T(8,128)(2,1)S(1)}, u32[]{:S(2)}, u32[]{:S(2)}) %collective-permute-start.1) | collective-permute-done | bytes 262176 | tf_op jit(solution)/shard_map/ppermute | solution.py:23
  17.6 6.2 %collective-permute-done.2.piece = bf16[512,256]{1,0:T(8,128)(2,1)S(1)} collective-permute-done((bf16[512,256]{1,0:T(8,128)(2,1)S(1)}, bf16[512,256]{1,0:T(8,128)(2,1)S(1)}, u32[]{:S(2)}, u32[]{:S(2)}) %collective-permute-start.2) | collective-permute-done | bytes 262176 | tf_op jit(solution)/shard_map/ppermute | solution.py:23
  23.8 2.7 %attend_early.1 = (bf16[192,896]{1,0:T(8,128)(2,1)S(1)}, bf16[192,896]{1,0:T(8,128)(2,1)S(1)}, bf16[2048,256]{1,0:T(8,128)(2,1)S(1)}) custom-call(s32[12]{0:T(128)S(1)} %pad_add_fusion.info, bf16[7,512,128]{2,1,0:T(8,128)(2,1)S(1)} %get-tuple-element.38.q_ref, bf16[896,896]{1,0:T(8,128)(2,1)S(1)} %get-tuple-element.39.w_send, ...), custom_call_target="tpu_custom_call", output_to_operand_aliasing={{2}: (3, {})} | custom-call | flops 1536000000 | bytes 6000000 | tf_op jit(solution)/shard_map/attend_early/pallas_call | solution.py:186
  26.6 3.1 %attend_next.2 = (bf16[192,896]{1,0:T(8,128)(2,1)S(1)}, bf16[192,896]{1,0:T(8,128)(2,1)S(1)}, bf16[192,896]{1,0:T(8,128)(2,1)S(1)}) custom-call(s32[12]{0:T(128)S(1)} %pad_add_fusion.info, bf16[7,512,128]{2,1,0:T(8,128)(2,1)S(1)} %get-tuple-element.38.q_ref, bf16[896,896]{1,0:T(8,128)(2,1)S(1)} %get-tuple-element.39.w_send, ...), custom_call_target="tpu_custom_call" | custom-call | flops 1536000000 | bytes 6000000 | tf_op jit(solution)/shard_map/attend_next/pallas_call | solution.py:202
  29.8 0.6 %collective-permute-start.5 = (bf16[192,896]{1,0:T(8,128)(2,1)S(1)}, bf16[192,896]{1,0:T(8,128)(2,1)S(1)}, u32[]{:S(2)}, u32[]{:S(2)}) collective-permute-start(bf16[192,896]{1,0:T(8,128)(2,1)S(1)} %get-tuple-element.53), channel_id=1, source_target_pairs={{0,1},{1,0},{2,3},{3,2},{4,5},{5,4},{6,7},{7,6},{8,9},{9,8},{10,11... | collective-permute-start | bytes 1032200 | tf_op jit(solution)/shard_map/ppermute | solution.py:28
  30.3 1.5 %collective-permute-start.4 = (bf16[192,896]{1,0:T(8,128)(2,1)S(1)}, bf16[192,896]{1,0:T(8,128)(2,1)S(1)}, u32[]{:S(2)}, u32[]{:S(2)}) collective-permute-start(bf16[192,896]{1,0:T(8,128)(2,1)S(1)} %add.9), channel_id=1, source_target_pairs={{0,2},{1,3},{2,0},{3,1},{4,6},{5,7},{6,4},{7,5},{8,10},{9,11},{10,... | collective-permute-start | bytes 1032200 | tf_op jit(solution)/shard_map/ppermute | solution.py:28
  31.8 2.5 %attend_next.3 = (bf16[128,896]{1,0:T(8,128)(2,1)S(1)}, bf16[128,896]{1,0:T(8,128)(2,1)S(1)}, bf16[192,896]{1,0:T(8,128)(2,1)S(1)}) custom-call(s32[12]{0:T(128)S(1)} %pad_add_fusion.info, bf16[7,512,128]{2,1,0:T(8,128)(2,1)S(1)} %get-tuple-element.38.q_ref, bf16[896,896]{1,0:T(8,128)(2,1)S(1)} %get-tuple-element.39.w_send, ...), custom_call_target="tpu_custom_call" | custom-call | flops 1024000000 | bytes 6000000 | tf_op jit(solution)/shard_map/attend_next/pallas_call | solution.py:202
  35.0 0.6 %collective-permute-start.9 = (bf16[192,896]{1,0:T(8,128)(2,1)S(1)}, bf16[192,896]{1,0:T(8,128)(2,1)S(1)}, u32[]{:S(2)}, u32[]{:S(2)}) collective-permute-start(bf16[192,896]{1,0:T(8,128)(2,1)S(1)} %add.10), channel_id=1, source_target_pairs={{0,2},{1,3},{2,0},{3,1},{4,6},{5,7},{6,4},{7,5},{8,10},{9,11},{10,... | collective-permute-start | bytes 1032200 | tf_op jit(solution)/shard_map/ppermute | solution.py:28
  36.1 5.2 %collective-permute-done.4.refs_2_ = bf16[192,896]{1,0:T(8,128)(2,1)S(1)} collective-permute-done((bf16[192,896]{1,0:T(8,128)(2,1)S(1)}, bf16[192,896]{1,0:T(8,128)(2,1)S(1)}, u32[]{:S(2)}, u32[]{:S(2)}) %collective-permute-start.4) | collective-permute-done | bytes 344096 | tf_op jit(solution)/shard_map/ppermute | solution.py:28
  41.3 1.3 %project.5 = (bf16[192,896]{1,0:T(8,128)(2,1)S(1)}, bf16[192,896]{1,0:T(8,128)(2,1)S(1)}, bf16[128,896]{1,0:T(8,128)(2,1)S(1)}) custom-call(bf16[192,896]{1,0:T(8,128)(2,1)S(1)} %get-tuple-element.56.before.refs_0_, bf16[192,896]{1,0:T(8,128)(2,1)S(1)} %get-tuple-element.57.before.refs_1_, bf16[128,896]{1,0:T(8,128)(2,1)S(1)} %get-tuple-element.58.refs_0_.refs_2_, ...), custom_call_target="tpu_custom_call" | custom-call | flops 822083584 | bytes 6000000 | tf_op jit(solution)/shard_map/project/pallas_call | solution.py:249
  43.2 1.5 %collective-permute-start.7 = (bf16[128,896]{1,0:T(8,128)(2,1)S(1)}, bf16[128,896]{1,0:T(8,128)(2,1)S(1)}, u32[]{:S(2)}, u32[]{:S(2)}) collective-permute-start(bf16[128,896]{1,0:T(8,128)(2,1)S(1)} %add.11), channel_id=1, source_target_pairs={{0,2},{1,3},{2,0},{3,1},{4,6},{5,7},{6,4},{7,5},{8,10},{9,11},{10,... | collective-permute-start | bytes 688136 | tf_op jit(solution)/shard_map/ppermute | solution.py:28
  44.7 1.3 %project.4 = (bf16[192,896]{1,0:T(8,128)(2,1)S(1)}, bf16[192,896]{1,0:T(8,128)(2,1)S(1)}, bf16[128,896]{1,0:T(8,128)(2,1)S(1)}) custom-call(bf16[192,896]{1,0:T(8,128)(2,1)S(1)} %get-tuple-element.56.before.refs_0_, bf16[192,896]{1,0:T(8,128)(2,1)S(1)} %get-tuple-element.57.before.refs_1_, bf16[128,896]{1,0:T(8,128)(2,1)S(1)} %get-tuple-element.58.refs_0_.refs_2_, ...), custom_call_target="tpu_custom_call" | custom-call | flops 822083584 | bytes 6000000 | tf_op jit(solution)/shard_map/project/pallas_call | solution.py:249
  46.0 2.7 %collective-permute-done.9.refs_3_ = bf16[192,896]{1,0:T(8,128)(2,1)S(1)} collective-permute-done((bf16[192,896]{1,0:T(8,128)(2,1)S(1)}, bf16[192,896]{1,0:T(8,128)(2,1)S(1)}, u32[]{:S(2)}, u32[]{:S(2)}) %collective-permute-start.9) | collective-permute-done | bytes 344096 | tf_op jit(solution)/shard_map/ppermute | solution.py:28
  48.6 1.0 %finish.2.refs_3_ = bf16[512,896]{1,0:T(8,128)(2,1)} custom-call(bf16[192,896]{1,0:T(8,128)(2,1)S(1)} %get-tuple-element.63.refs_0_, bf16[192,896]{1,0:T(8,128)(2,1)S(1)} %get-tuple-element.64.refs_1_, bf16[192,896]{1,0:T(8,128)(2,1)S(1)} %collective-permute-done.4.refs_2_, bf16[192,896]{1,0:T(8,128)(2,1)S(1)} %collective-permute-done.9.refs_3_, ...), custom_call_target="tpu_custom_call" | custom-call | flops 1 | bytes 1 | tf_op jit(solution)/shard_map/finish/pallas_call | solution.py:280
  49.7 3.0 %collective-permute-done.7.refs_1_ = bf16[128,896]{1,0:T(8,128)(2,1)S(1)} collective-permute-done((bf16[128,896]{1,0:T(8,128)(2,1)S(1)}, bf16[128,896]{1,0:T(8,128)(2,1)S(1)}, u32[]{:S(2)}, u32[]{:S(2)}) %collective-permute-start.7) | collective-permute-done | bytes 229408 | tf_op jit(solution)/shard_map/ppermute | solution.py:28
  52.7 0.8 %finish.3 = bf16[512,896]{1,0:T(8,128)(2,1)} custom-call(bf16[128,896]{1,0:T(8,128)(2,1)S(1)} %get-tuple-element.60.refs_0_, bf16[128,896]{1,0:T(8,128)(2,1)S(1)} %collective-permute-done.7.refs_1_, bf16[128,896]{1,0:T(8,128)(2,1)S(1)} %collective-permute-done.8.refs_2_, bf16[512,896]{1,0:T(8,128)(2,1)} %finish.2.refs_3_), custom_call_target="tpu_custom_call", output_to_operand_aliasing={{}: (3, {})} | custom-call | flops 1 | bytes 1 | tf_op jit(solution)/shard_map/finish/pallas_call | solution.py:280
  (23 shorter events, 2.1 us)
Async XLA Ops:
  1.0 14.6 %collective-permute-start = (bf16[512,256]{1,0:T(8,128)(2,1)S(1)}, bf16[512,256]{1,0:T(8,128)(2,1)S(1)}, u32[]{:S(2)}, u32[]{:S(2)}) collective-permute-start(bf16[512,256]{1,0:T(8,128)(2,1)S(1)} %pad_maximum_fusion.first.refs_0_), channel_id=1, source_target_pairs={{0,4},{4,8},{8,12},{1,5},{5,9},{9,13},{2,6},{6,10},{10,14},{3,7},{... | collective-permute-start | bytes 786440 | tf_op jit(solution)/shard_map/ppermute | solution.py:23
  2.3 15.2 %collective-permute-start.1 = (bf16[512,256]{1,0:T(8,128)(2,1)S(1)}, bf16[512,256]{1,0:T(8,128)(2,1)S(1)}, u32[]{:S(2)}, u32[]{:S(2)}) collective-permute-start(bf16[512,256]{1,0:T(8,128)(2,1)S(1)} %pad_maximum_fusion.first.refs_0_), channel_id=1, source_target_pairs={{0,12},{1,13},{2,14},{3,15},{16,28},{17,29},{18,30},{19,31}} | collective-permute-start | bytes 786440 | tf_op jit(solution)/shard_map/ppermute | solution.py:23
  3.6 2.8 %copy-start = (bf16[896,3584]{1,0:T(8,128)(2,1)S(1)}, bf16[896,3584]{1,0:T(8,128)(2,1)}, u32[]{:S(2)}) copy-start(bf16[896,3584]{1,0:T(8,128)(2,1)} %weight.1) | copy-start | bytes 19267588
  6.4 1.2 %copy-start.1 = (bf16[512,7,128]{2,0,1:T(8,128)(2,1)S(1)}, bf16[512,7,128]{2,0,1:T(8,128)(2,1)}, u32[]{:S(2)}) copy-start(bf16[512,7,128]{2,0,1:T(8,128)(2,1)} %param.6) | copy-start | bytes 2752516
  7.6 9.3 %copy-start.2 = (s32[1,4]{1,0:T(1,128)S(1)}, s32[1,4]{1,0:T(1,128)}, u32[]{:S(2)}) copy-start(s32[1,4]{1,0:T(1,128)} %param.11) | copy-start | bytes 52
  7.6 9.3 %copy-start.3 = (s32[1,8]{1,0:T(1,128)S(1)}, s32[1,8]{1,0:T(1,128)}, u32[]{:S(2)}) copy-start(s32[1,8]{1,0:T(1,128)} %param.10) | copy-start | bytes 100
  15.6 8.3 %collective-permute-start.2 = (bf16[512,256]{1,0:T(8,128)(2,1)S(1)}, bf16[512,256]{1,0:T(8,128)(2,1)S(1)}, u32[]{:S(2)}, u32[]{:S(2)}) collective-permute-start(bf16[512,256]{1,0:T(8,128)(2,1)S(1)} %collective-permute-done.refs_1_), channel_id=1, source_target_pairs={{0,4},{4,8},{8,12},{1,5},{5,9},{9,13},{2,6},{6,10},{10,14},{3,7},{... | collective-permute-start | bytes 786440 | tf_op jit(solution)/shard_map/ppermute | solution.py:23
  26.5 3.1 %collective-permute-start.3 = (bf16[192,896]{1,0:T(8,128)(2,1)S(1)}, bf16[192,896]{1,0:T(8,128)(2,1)S(1)}, u32[]{:S(2)}, u32[]{:S(2)}) collective-permute-start(bf16[192,896]{1,0:T(8,128)(2,1)S(1)} %get-tuple-element.45), channel_id=1, source_target_pairs={{0,1},{1,0},{2,3},{3,2},{4,5},{5,4},{6,7},{7,6},{8,9},{9,8},{10,11... | collective-permute-start | bytes 1032200 | tf_op jit(solution)/shard_map/ppermute | solution.py:28
  29.8 4.6 %collective-permute-start.5 = (bf16[192,896]{1,0:T(8,128)(2,1)S(1)}, bf16[192,896]{1,0:T(8,128)(2,1)S(1)}, u32[]{:S(2)}, u32[]{:S(2)}) collective-permute-start(bf16[192,896]{1,0:T(8,128)(2,1)S(1)} %get-tuple-element.53), channel_id=1, source_target_pairs={{0,1},{1,0},{2,3},{3,2},{4,5},{5,4},{6,7},{7,6},{8,9},{9,8},{10,11... | collective-permute-start | bytes 1032200 | tf_op jit(solution)/shard_map/ppermute | solution.py:28
  30.3 10.9 %collective-permute-start.4 = (bf16[192,896]{1,0:T(8,128)(2,1)S(1)}, bf16[192,896]{1,0:T(8,128)(2,1)S(1)}, u32[]{:S(2)}, u32[]{:S(2)}) collective-permute-start(bf16[192,896]{1,0:T(8,128)(2,1)S(1)} %add.9), channel_id=1, source_target_pairs={{0,2},{1,3},{2,0},{3,1},{4,6},{5,7},{6,4},{7,5},{8,10},{9,11},{10,... | collective-permute-start | bytes 1032200 | tf_op jit(solution)/shard_map/ppermute | solution.py:28
  34.5 1.6 %collective-permute-start.6 = (bf16[128,896]{1,0:T(8,128)(2,1)S(1)}, bf16[128,896]{1,0:T(8,128)(2,1)S(1)}, u32[]{:S(2)}, u32[]{:S(2)}) collective-permute-start(bf16[128,896]{1,0:T(8,128)(2,1)S(1)} %get-tuple-element.55), channel_id=1, source_target_pairs={{0,1},{1,0},{2,3},{3,2},{4,5},{5,4},{6,7},{7,6},{8,9},{9,8},{10,11... | collective-permute-start | bytes 688136 | tf_op jit(solution)/shard_map/ppermute | solution.py:28
  35.0 13.6 %collective-permute-start.9 = (bf16[192,896]{1,0:T(8,128)(2,1)S(1)}, bf16[192,896]{1,0:T(8,128)(2,1)S(1)}, u32[]{:S(2)}, u32[]{:S(2)}) collective-permute-start(bf16[192,896]{1,0:T(8,128)(2,1)S(1)} %add.10), channel_id=1, source_target_pairs={{0,2},{1,3},{2,0},{3,1},{4,6},{5,7},{6,4},{7,5},{8,10},{9,11},{10,... | collective-permute-start | bytes 1032200 | tf_op jit(solution)/shard_map/ppermute | solution.py:28
  42.5 6.1 %collective-permute-start.10 = (bf16[192,896]{1,0:T(8,128)(2,1)S(1)}, bf16[192,896]{1,0:T(8,128)(2,1)S(1)}, u32[]{:S(2)}, u32[]{:S(2)}) collective-permute-start(bf16[192,896]{1,0:T(8,128)(2,1)S(1)} %get-tuple-element.67), channel_id=1, source_target_pairs={{0,1},{1,0},{2,3},{3,2},{4,5},{5,4},{6,7},{7,6},{8,9},{9,8},{10,11... | collective-permute-start | bytes 1032200 | tf_op jit(solution)/shard_map/ppermute | solution.py:28
  42.6 6.0 %collective-permute-start.11 = (bf16[192,896]{1,0:T(8,128)(2,1)S(1)}, bf16[192,896]{1,0:T(8,128)(2,1)S(1)}, u32[]{:S(2)}, u32[]{:S(2)}) collective-permute-start(bf16[192,896]{1,0:T(8,128)(2,1)S(1)} %get-tuple-element.68), channel_id=1, source_target_pairs={{0,1},{1,0},{2,3},{3,2},{4,5},{5,4},{6,7},{7,6},{8,9},{9,8},{10,11... | collective-permute-start | bytes 1032200 | tf_op jit(solution)/shard_map/ppermute | solution.py:28
  43.1 6.5 %collective-permute-start.8 = (bf16[128,896]{1,0:T(8,128)(2,1)S(1)}, bf16[128,896]{1,0:T(8,128)(2,1)S(1)}, u32[]{:S(2)}, u32[]{:S(2)}) collective-permute-start(bf16[128,896]{1,0:T(8,128)(2,1)S(1)} %get-tuple-element.62), channel_id=1, source_target_pairs={{0,1},{1,0},{2,3},{3,2},{4,5},{5,4},{6,7},{7,6},{8,9},{9,8},{10,11... | collective-permute-start | bytes 688136 | tf_op jit(solution)/shard_map/ppermute | solution.py:28
  43.2 9.5 %collective-permute-start.7 = (bf16[128,896]{1,0:T(8,128)(2,1)S(1)}, bf16[128,896]{1,0:T(8,128)(2,1)S(1)}, u32[]{:S(2)}, u32[]{:S(2)}) collective-permute-start(bf16[128,896]{1,0:T(8,128)(2,1)S(1)} %add.11), channel_id=1, source_target_pairs={{0,2},{1,3},{2,0},{3,1},{4,6},{5,7},{6,4},{7,5},{8,10},{9,11},{10,... | collective-permute-start | bytes 688136 | tf_op jit(solution)/shard_map/ppermute | solution.py:28
